TPU v7x, 128 devices: a whole 4x4x4 slice. The times are simulated.
128 devices in a mesh: front: 4 (over x), row: 8 (over y, core), col: 4 (over z).
Axes of the slice: x: 4, y: 4, z: 4, core: 2. Of those that a mesh axis runs over, the one named last changes fastest.
Arguments:
- front: float32 [4, 9, 8, 128, 18, 4, 128], P('front', None, 'row', None, None, 'col')
- child_updates: float32 [4, 1024, 128, 128], P('front', ('row', 'col')), may hold values from -3 to 3
- child_owner: int32 [4, 1024, 1], P('front', ('row', 'col')), may hold values from 0 to 31; in each aligned block of 32 rows (0 to 31, 32 to 63, ..., all dimensions but the last counted through in order) at most 2 rows name the same one
- child_rows: int32 [4, 1024, 128], P('front', ('row', 'col')), may hold values from 0 to 128, as said below
- child_cols: int32 [4, 1024, 128], P('front', ('row', 'col')), may hold values from 0 to 128, as said below
- child_slot: int32 [4, 1024], P('front', ('row', 'col')), may hold values from 0 to 161, as said below
Outputs:
- factored: float32 [4, 9, 8, 128, 18, 4, 128], P('front', None, 'row', None, None, 'col')
Inputs may be any that keep to these rules, and one draw needn't show every extreme that they name: `child_owner`: among the child blocks of one device (aligned blocks of 32), no owner is named more than 2 times. `child_rows`: in each block the entries below 128 come first and rise strictly; the rest equal 128. `child_cols`: in each block the entries below 128 come first and rise strictly; the rest equal 128. `child_slot`: A slot never names local tile column 0 together with one of the first 1 local tile rows.
All inputs are finite; a program needn't handle non-finite values.
Results may differ from a plain program's by a relative error of at most 0.0003.
Values sent between devices are 32-bit elements; how exact they have to be, the bound alone decides.
No kernel may reach another device: no remote copies, remote signals or barrier semaphores. Data moves between devices by JAX's collectives and lax.ppermute only.
A program may use at most 192 MiB of HBM per device.

v0:
```python
import jax
import jax.numpy as jnp
from jax import lax
from jax.sharding import PartitionSpec as P


def local(front, child_updates, child_owner, child_rows, child_cols, child_slot):
    row_count = lax.axis_size("row")
    col_count = lax.axis_size("col")
    owner_count = row_count * col_count
    my_row = lax.axis_index("row")
    my_col = lax.axis_index("col")
    tile_rows = front.shape[1]
    tile_size = front.shape[3]
    tile_cols = front.shape[4]
    slot_total = tile_rows * tile_cols
    rows_local = tile_rows * tile_size
    cols_local = tile_cols * tile_size
    panel_width = tile_size * col_count
    matrix = front.reshape(rows_local, cols_local)
    blocks = child_updates[0]
    block_count = blocks.shape[0]
    capacity = max(2, 2 * block_count // owner_count)
    owners_of = child_owner[0, :, 0]
    places = jnp.stack([child_rows[0], child_cols[0]], axis=1)
    one_hot = (owners_of[:, None] == jnp.arange(owner_count, dtype=jnp.int32)[None, :]).astype(
        jnp.int32
    )
    earlier = jnp.cumsum(one_hot, axis=0) - one_hot
    position = owners_of * capacity + jnp.sum(earlier * one_hot, axis=1)
    send_blocks = (
        jnp.zeros((owner_count * capacity, tile_size, tile_size), jnp.float32)
        .at[position]
        .set(blocks)
    )
    send_places = (
        jnp.full((owner_count * capacity, 2, tile_size), tile_size, jnp.int32)
        .at[position]
        .set(places)
    )
    send_slots = (
        jnp.full((owner_count * capacity,), slot_total, jnp.int32).at[position].set(child_slot[0])
    )
    got_blocks, got_places, got_slots = (
        lax.all_to_all(send_blocks, ("row", "col"), split_axis=0, concat_axis=0, tiled=True),
        lax.all_to_all(send_places, ("row", "col"), split_axis=0, concat_axis=0, tiled=True),
        lax.all_to_all(send_slots, ("row", "col"), split_axis=0, concat_axis=0, tiled=True),
    )
    inner = jnp.arange(tile_size, dtype=jnp.int32)
    rows_hot = (got_places[:, 0, :, None] == inner[None, None, :]).astype(jnp.float32)
    cols_hot = (got_places[:, 1, :, None] == inner[None, None, :]).astype(jnp.float32)
    row_placed = jnp.einsum("npi,npq->niq", rows_hot, got_blocks, precision=lax.Precision.HIGHEST)
    placed = jnp.einsum("niq,nqj->nij", row_placed, cols_hot, precision=lax.Precision.HIGHEST)
    slot_hot = (got_slots[None, :] == jnp.arange(slot_total, dtype=jnp.int32)[:, None]).astype(
        jnp.float32
    )
    slot_tiles = jnp.dot(
        slot_hot,
        placed.reshape(placed.shape[0], tile_size * tile_size),
        precision=lax.Precision.HIGHEST,
    )
    added = (
        slot_tiles.reshape(tile_rows, tile_cols, tile_size, tile_size)
        .transpose(0, 2, 1, 3)
        .reshape(rows_local, cols_local)
    )
    assembled = matrix + added
    panel_rows = lax.all_gather(assembled[:, :tile_size], "col", axis=1, tiled=True)
    leading_tiles = max(1, panel_width // (tile_size * row_count))
    leading_part = panel_rows[: leading_tiles * tile_size].reshape(
        leading_tiles, 1, tile_size, panel_width
    )
    leading_all = lax.all_gather(leading_part, "row", axis=1, tiled=True)
    leading = leading_all.reshape(leading_tiles * row_count * tile_size, panel_width)[:panel_width]
    factor = jnp.linalg.cholesky(0.5 * (leading + leading.T))
    panel_factor = jax.scipy.linalg.solve_triangular(factor, panel_rows.T, lower=True).T
    share_rows = tile_size // col_count
    solved_tiles = panel_factor.reshape(tile_rows, tile_size, panel_width)
    share = lax.dynamic_slice_in_dim(solved_tiles, my_col * share_rows, share_rows, axis=1)
    everyone = lax.all_gather(
        share.reshape(tile_rows, 1, share_rows, panel_width), ("row", "col"), axis=1, tiled=True
    )
    all_tiles = everyone.reshape(tile_cols, col_count, tile_size, panel_width)
    column_factor = lax.dynamic_index_in_dim(all_tiles, my_col, axis=1, keepdims=False)
    column_factor = column_factor.reshape(cols_local, panel_width)
    update = lax.dot_general(
        panel_factor, column_factor, (((1,), (1,)), ((), ())), precision=lax.Precision.HIGHEST
    )
    global_row = (
        jnp.arange(tile_rows, dtype=jnp.int32)[:, None] * row_count + my_row
    ) * tile_size + jnp.arange(tile_size, dtype=jnp.int32)[None, :]
    upper_rows = global_row.reshape(rows_local) < panel_width
    trailing = jnp.where(upper_rows[:, None], assembled, assembled - update)
    own_panel = lax.dynamic_slice_in_dim(panel_factor, my_col * tile_size, tile_size, axis=1)
    result = jnp.concatenate([own_panel, trailing[:, tile_size:]], axis=1)
    return result.reshape(front.shape)


def solution(mesh):
    in_specs = (
        P("front", None, "row", None, None, "col", None),
        P("front", ("row", "col"), None, None),
        P("front", ("row", "col"), None),
        P("front", ("row", "col"), None),
        P("front", ("row", "col"), None),
        P("front", ("row", "col")),
    )
    out_specs = P("front", None, "row", None, None, "col", None)
    return jax.shard_map(local, mesh=mesh, in_specs=in_specs, out_specs=out_specs, check_vma=False)
```

profile of v0, /device:TPU:0, one launch (start us, length us, event | category | flops | bytes accessed | tf_op | source)
XLA Modules:
  0.0 584.1 jit_solution(1307602778336260700)
XLA Ops:
  10.5 8.4 %all-to-all-start = ((s32[32,2,1]{1,2,0:T(1,128)}), s32[32,2,1]{1,2,0:T(1,128)S(1)}, u32[]{:S(2)}, u32[]{:S(2)}) async-start(s32[32,2,1]{1,2,0:T(1,128)} %bitcast.5), calls=%async_computation | async-start | bytes 32768 | tf_op jit(solution)/shard_map/all_to_all | solution.py:47
  47.0 66.9 %reduce.24 = f32[9,128,18,128]{3,2,1,0:T(8,128)} reduce(f32[1,9,1,128,18,1,128]{6,5,4,3,2,1,0:T(1,128)} %param.6, f32[]{:T(128)} %constant.208), dimensions={0,2,5}, to_apply=%param.6.reduce_sub_computation | reduce | bytes 21233668 | tf_op args[0]
  113.9 11.7 %copy.65 = f32[144,8,18,128]{3,1,2,0:T(8,128)} copy(f32[144,8,18,128]{3,2,1,0:T(8,128)} %bitcast.134) | data formatting | bytes 21233664
  125.6 12.6 %copy.34 = f32[1152,2304]{0,1:T(8,128)} copy(f32[1152,2304]{1,0:T(8,128)} %bitcast.135) | data formatting | bytes 21233664 | tf_op jit(solution)/shard_map/reshape | solution.py:20
  148.5 12.3 %fusion = f32[9,18,128,128]{3,1,2,0:T(8,128)} fusion(s32[9,18]{1,0:T(8,128)S(1)} %multiply_add_fusion, s32[64]{0:T(128)S(1)} %eq.75, f32[8,8,128,128]{3,2,1,0:T(8,128)S(1)} %bitcast.138), kind=kOutput, calls=%fused_computation.11 | convolution fusion | flops 2038442112 | bytes 14812040 | tf_op jit(solution)/shard_map/dot_general | solution.py:57
  160.7 11.7 %copy.64 = f32[144,8,18,128]{3,1,2,0:T(8,128)} copy(f32[144,8,18,128]{3,2,1,0:T(8,128)} %bitcast.133) | data formatting | bytes 21233664
  172.4 12.6 %copy.35 = f32[1152,2304]{0,1:T(8,128)} copy(f32[1152,2304]{1,0:T(8,128)} %bitcast.136) | data formatting | bytes 21233664 | tf_op jit(solution)/shard_map/reshape | solution.py:65
  185.1 7.7 %add.115 = f32[1152,2304]{0,1:T(8,128)S(1)} add(f32[1152,2304]{0,1:T(8,128)} %copy.34, f32[1152,2304]{0,1:T(8,128)} %copy.35) | non-fusion elementwise | flops 2654208 | bytes 31850496 | tf_op jit(solution)/shard_map/add | solution.py:67
  197.7 34.7 %all-gather.6.cloned.1.call-done = f32[1152,512]{0,1:T(8,128)} async-done(((f32[1152,128]{0,1:T(8,128)}), f32[1152,512]{0,1:T(8,128)}) %all-gather.6.cloned.1.call-update) | async-done | bytes 2359312 | tf_op jit(solution)/shard_map/all_gather | solution.py:68
  234.5 26.8 %all-gather.8.cloned.1.call-done = f32[1024,512]{0,1:T(8,128)} async-done(((f32[128,512]{0,1:T(8,128)}), f32[1024,512]{0,1:T(8,128)}) %all-gather.8.cloned.1.call-update) | async-done | bytes 2097168 | tf_op jit(solution)/shard_map/all_gather | solution.py:73
  264.8 11.7 %cholesky.104 = f32[128,128]{1,0:T(8,128)S(1)} custom-call(f32[128,128]{1,0:T(8,128)S(1)} %cholesky.266), custom_call_target="Cholesky" | custom-call | tf_op jit(solution)/shard_map/jit(cholesky)/cholesky | solution.py:75
  276.7 9.8 %custom-call.31 = f32[1,128,128]{1,2,0:T(8,128)S(1)} custom-call(f32[1,128,128]{2,1,0:T(8,128)S(1)} %get-tuple-element.34), custom_call_target="InvertDiagBlocksLowerTriangular" | custom-call | tf_op jit(solution)/shard_map/jit(cholesky)/cholesky | solution.py:75
  287.1 11.9 %cholesky.217 = f32[128,128]{1,0:T(8,128)S(1)} custom-call(f32[128,128]{1,0:T(8,128)S(1)} %cholesky.270), custom_call_target="Cholesky" | custom-call | tf_op jit(solution)/shard_map/jit(cholesky)/cholesky | solution.py:75
  299.0 9.8 %custom-call.32 = f32[1,128,128]{1,2,0:T(8,128)S(1)} custom-call(f32[1,128,128]{2,1,0:T(8,128)S(1)} %get-tuple-element.31), custom_call_target="InvertDiagBlocksLowerTriangular" | custom-call | tf_op jit(solution)/shard_map/jit(cholesky)/cholesky | solution.py:75
  309.5 11.7 %cholesky.238 = f32[128,128]{1,0:T(8,128)S(1)} custom-call(f32[128,128]{1,0:T(8,128)S(1)} %cholesky.275), custom_call_target="Cholesky" | custom-call | tf_op jit(solution)/shard_map/jit(cholesky)/cholesky | solution.py:75
  321.9 9.8 %custom-call.33 = f32[1,128,128]{1,2,0:T(8,128)S(1)} custom-call(f32[1,128,128]{2,1,0:T(8,128)S(1)} %get-tuple-element.28), custom_call_target="InvertDiagBlocksLowerTriangular" | custom-call | tf_op jit(solution)/shard_map/jit(cholesky)/cholesky | solution.py:75
  332.3 11.9 %cholesky.255 = f32[128,128]{1,0:T(8,128)S(1)} custom-call(f32[128,128]{1,0:T(8,128)S(1)} %convolution_subtract_fusion.5), custom_call_target="Cholesky" | custom-call | tf_op jit(solution)/shard_map/jit(cholesky)/cholesky | solution.py:75
  356.0 39.3 %custom-call.34 = f32[4,128,128]{1,2,0:T(8,128)S(1)} custom-call(f32[4,128,128]{2,1,0:T(8,128)S(1)} %get-tuple-element.12), custom_call_target="InvertDiagBlocksLowerTriangular" | custom-call | tf_op jit(solution)/shard_map/jit(_solve_triangular)/triangular_solve | solution.py:76
  413.8 77.4 %all-gather.10.cloned.1.call-done = f32[9,1024,512]{2,1,0:T(8,128)} async-done(((f32[9,32,512]{2,1,0:T(8,128)}), f32[9,1024,512]{2,1,0:T(8,128)}) %all-gather.10.cloned.1.call-update) | async-done | bytes 18874384 | tf_op jit(solution)/shard_map/all_gather | solution.py:80
  494.2 22.0 %fusion.46 = f32[1152,2304]{0,1:T(8,128)} fusion(f32[2304,512]{1,0:T(8,128)S(1)} %bitcast.137, f32[128,1152]{1,0:T(8,128)S(1)} %fusion.28, f32[128,1152]{1,0:T(8,128)S(1)} %fusion.29, f32[128,1152]{1,0:T(8,128)S(1)} %fusion.31, f32[128,1152]{1,0:T(8,128)S(1)} %fusion.16), kind=kOutput, calls=%fused_computation.106 | convolution fusion | flops 16309223424 | bytes 17694720 | tf_op jit(solution)/shard_map/dot_general | solution.py:86
  516.2 11.5 %subtract_select_fusion = f32[1152,2176]{0,1:T(8,128)} fusion(f32[1152,2304]{0,1:T(8,128)} %fusion.46, f32[1152,2304]{0,1:T(8,128)} %copy-done, pred[1152]{0:T(1024)(128)(4,1)S(1)} %fusion.40), kind=kLoop, calls=%fused_computation.5 | loop fusion | flops 5013504 | bytes 30082176 | tf_op jit(solution)/shard_map/jit(_where)/select_n | solution.py:93
  527.8 8.7 %pad_maximum_fusion = f32[1152,2304]{0,1:T(8,128)} fusion(f32[1152,2176]{0,1:T(8,128)} %subtract_select_fusion, f32[1152,128]{0,1:T(8,128)S(1)} %dynamic-slice_bitcast_fusion), kind=kLoop, calls=%fused_computation.8 | loop fusion | flops 2654208 | bytes 21233664 | tf_op jit(solution)/shard_map/concatenate | solution.py:95
  536.4 14.2 %reshape.206 = f32[1,9,1,128,18,1,128]{3,1,6,4,5,2,0:T(8,128)} reshape(f32[1152,2304]{0,1:T(8,128)} %pad_maximum_fusion) | data formatting | bytes 21233664 | tf_op jit(solution)/shard_map/reshape | solution.py:96
  550.7 26.5 %copy.41 = f32[1,9,1,128,18,1,128]{6,5,4,3,2,1,0:T(1,128)} copy(f32[1,9,1,128,18,1,128]{3,1,6,4,5,2,0:T(8,128)} %reshape.206) | data formatting | bytes 21233664 | tf_op jit(solution)/shard_map/reshape | solution.py:96
  (91 shorter events, 93.5 us)
Async XLA Ops:
  6.5 27.3 %copy-start.1 = (f32[1,32,128,128]{3,2,1,0:T(8,128)S(1)}, f32[1,32,128,128]{3,2,1,0:T(8,128)}, u32[]{:S(2)}) copy-start(f32[1,32,128,128]{3,2,1,0:T(8,128)} %param.7) | copy-start | bytes 6291460
  10.5 15.6 %all-to-all-start = ((s32[32,2,1]{1,2,0:T(1,128)}), s32[32,2,1]{1,2,0:T(1,128)S(1)}, u32[]{:S(2)}, u32[]{:S(2)}) async-start(s32[32,2,1]{1,2,0:T(1,128)} %bitcast.5), calls=%async_computation | async-start | bytes 32768 | tf_op jit(solution)/shard_map/all_to_all | solution.py:47
  26.1 13.1 %all-to-all-start.1 = ((s32[64,2,128]{2,1,0:T(2,128)}), s32[64,2,128]{2,1,0:T(2,128)S(1)}, u32[]{:S(2)}, u32[]{:S(2)}) async-start(s32[64,2,128]{2,1,0:T(2,128)} %scatter_fusion), calls=%async_computation.1 | async-start | bytes 131072 | tf_op jit(solution)/shard_map/all_to_all | solution.py:46
  39.2 100.4 %all-to-all-start.2 = ((f32[64,128,128]{2,1,0:T(8,128)}), f32[64,128,128]{2,1,0:T(8,128)}, u32[]{:S(2)}, u32[]{:S(2)}) async-start(f32[64,128,128]{2,1,0:T(8,128)} %scatter_fusion.1), calls=%async_computation.2 | async-start | bytes 8388608 | tf_op jit(solution)/shard_map/all_to_all | solution.py:45
  46.8 185.5 %all-gather.6.cloned.1.call-start = ((), (), s32[]{:S(2)}) async-start(), calls=%async_computation.3 | async-start | bytes 2949120 | tf_op jit(solution)/shard_map/all_gather | solution.py:68
  192.8 3.9 copy-start
  197.6 63.7 %all-gather.8.cloned.1.call-start = ((), (), s32[]{:S(2)}) async-start(), calls=%async_computation.4 | async-start | bytes 2359296 | tf_op jit(solution)/shard_map/all_gather | solution.py:73
  234.0 257.2 %all-gather.10.cloned.1.call-start = ((), (), s32[]{:S(2)}) async-start(), calls=%async_computation.5 | async-start | bytes 19464192 | tf_op jit(solution)/shard_map/all_gather | solution.py:80
Sparse Core Ops, SparseCore 0:
  197.7 34.5 all-gather.5
  234.1 27.1 all-gather.7
  412.7 78.4 all-gather.9
where the time goes:
time: 591 us; the launch traced here: 584 us
  other arithmetic  220 us (37%)
  waiting for transfers between devices  141 us (24%)
  local copies, waits for them, and re-layouts  130 us (22%)
  matrix products  54.6 us (9%)
  starting transfers between devices  22.1 us (4%)
  between operations  16.5 us (3%)
    another operation x14, other arithmetic, local(): factor = jnp.linalg.cholesky(0.5 * (leading + leading.T))  78.8 us
    all_gather x1, waiting for transfers between devices, local(): lax.all_gather(share.reshape(tile_rows, 1, share_rows, panel_width), ('ro...  77.4 us
    unnamed x2, other arithmetic  66.9 us
    another operation x4, other arithmetic, local(): jax.scipy.linalg.solve_triangular(factor, panel_rows.T, lower=True)  41.9 us
    reshape x2, local copies, waits for them, and re-layouts, local(): return result.reshape(front.shape)  40.7 us
    all_gather x1, waiting for transfers between devices, local(): lax.all_gather(assembled[:, :tile_size], 'col', axis=1, tiled=True)  34.7 us
    unnamed x8, local copies, waits for them, and re-layouts  29.5 us
    all_gather x1, waiting for transfers between devices, local(): leading_all = lax.all_gather(leading_part, 'row', axis=1, tiled=True)  26.8 us
  transfers between devices with their start and end apart: 6, of which 4 were waited for; matrix products, arithmetic and copies ran while one was open for 18% of the time, Pallas kernels for 0%

commit v1 on v0

v1 whole, which is shorter than its diff:
```python
import functools

import jax
import jax.numpy as jnp
from jax import lax
from jax.experimental import pallas as pl
from jax.experimental.pallas import tpu as pltpu
from jax.sharding import PartitionSpec as P

T = 128
F32 = jnp.float32
BF16 = jnp.bfloat16
HIGHEST = lax.Precision.HIGHEST
NT = (((1,), (1,)), ((), ()))
NN = (((1,), (0,)), ((), ()))
VM = functools.partial(pl.BlockSpec, memory_space=pltpu.VMEM)
ANY = functools.partial(pl.BlockSpec, memory_space=pl.ANY)
LIMIT = 60 * 1024 * 1024


def params():
    return pltpu.CompilerParams(vmem_limit_bytes=LIMIT)


def split(x):
    high = x.astype(BF16)
    low = (x - high.astype(F32)).astype(BF16)
    return high, low


def dot3(x, y, dims):
    xh, xl = split(x)
    yh, yl = split(y)
    dot = functools.partial(lax.dot_general, dimension_numbers=dims, preferred_element_type=F32)
    return dot(xh, yh) + (dot(xh, yl) + dot(xl, yh))


def route_kernel(blocks, slot_total, owner_ref, slot_ref, blocks_ref, rows_ref, cols_ref, send_ref, meta, count, sem):
    owners = meta.shape[0]
    meta[...] = jnp.full(meta.shape, float(slot_total), F32)

    def clear(o, _):
        count[o] = 0
        return 0

    lax.fori_loop(0, owners, clear, 0)

    def place(g, _):
        o = owner_ref[g]
        k = count[o]
        count[o] = k + 1
        pltpu.make_async_copy(blocks_ref.at[g], send_ref.at[o, pl.ds(pl.multiple_of(k * T, T), T), :], sem.at[g]).start()
        meta[o, pl.ds(2 * k, 1), :] = rows_ref[pl.ds(g, 1), :].astype(F32)
        meta[o, pl.ds(2 * k + 1, 1), :] = cols_ref[pl.ds(g, 1), :].astype(F32)
        meta[o, pl.ds(4 + k, 1), :] = jnp.full((1, T), slot_ref[g], jnp.int32).astype(F32)
        return 0

    lax.fori_loop(0, blocks, place, 0)
    tail = pltpu.make_async_copy(meta, send_ref.at[:, pl.ds(2 * T, 8), :], sem.at[blocks])
    tail.start()

    def finish(g, _):
        pltpu.make_async_copy(blocks_ref.at[g], send_ref.at[0, pl.ds(0, T), :], sem.at[g]).wait()
        return 0

    lax.fori_loop(0, blocks, finish, 0)
    tail.wait()


def route(owner, slot, blocks, rows, cols, owners, slot_total):
    count = blocks.shape[0]
    return pl.pallas_call(
        functools.partial(route_kernel, count, slot_total),
        out_shape=jax.ShapeDtypeStruct((owners, 2 * T + 8, T), F32),
        grid_spec=pltpu.PrefetchScalarGridSpec(
            num_scalar_prefetch=2,
            grid=(),
            in_specs=[ANY(), VM(), VM()],
            out_specs=ANY(),
            scratch_shapes=[
                pltpu.VMEM((owners, 8, T), F32),
                pltpu.SMEM((owners,), jnp.int32),
                pltpu.SemaphoreType.DMA((count + 1,)),
            ],
        ),
        compiler_params=params(),
        name="route",
    )(owner, slot, blocks, rows, cols)


def inverse_factor(s, out_ref):
    groups = T // 8
    lane = lax.broadcasted_iota(jnp.int32, (8, T), 1)
    sub = lax.broadcasted_iota(jnp.int32, (8, T), 0)
    m = [s[8 * g : 8 * g + 8, :] for g in range(groups)]
    e = [jnp.where(lane == sub + 8 * g, 1.0, 0.0).astype(F32) for g in range(groups)]
    for k in range(T):
        g0, s0 = divmod(k, 8)
        row = jnp.broadcast_to(m[g0][s0 : s0 + 1, :], (8, T))
        erow = jnp.broadcast_to(e[g0][s0 : s0 + 1, :], (8, T))
        pivot = jnp.broadcast_to(row[:, k : k + 1], (8, T))
        out_ref[k : k + 1, :] = (erow * lax.rsqrt(pivot))[0:1, :]
        if k == T - 1:
            break
        inv = 1.0 / pivot
        row = row * inv
        erow = erow * inv
        for g in range(g0, groups):
            col = jnp.broadcast_to(m[g][:, k : k + 1], (8, T))
            if g == g0:
                if s0 == 7:
                    continue
                col = jnp.where(sub > s0, col, 0.0)
            m[g] = m[g] - col * row
            e[g] = e[g] - col * erow


def leading_kernel(lead_ref, wt_ref, s_ref, e_ref, w_ref):
    n = 4
    dot = functools.partial(lax.dot_general, precision=HIGHEST, preferred_element_type=F32)
    for i in range(n):
        for j in range(i + 1):
            s_ref[i, j] = 0.5 * (lead_ref[j, i] + lead_ref[i, j].T)
    e_ref[...] = jnp.zeros_like(e_ref)

    def step(k, _):
        inverse_factor(s_ref[k, k], w_ref)
        wk = w_ref[...]
        own = dot(wk, e_ref[k], NN)
        column = lax.broadcasted_iota(jnp.int32, (T, n * T), 1)
        spread = jnp.concatenate([wk] * n, axis=1)
        own = jnp.where(column // T == k, spread, own)
        for j in range(n):
            wt_ref[j, :, pl.ds(pl.multiple_of(k * T, T), T)] = own[:, j * T : (j + 1) * T].T

        for i in range(1, n):
            @pl.when(i > k)
            def _():
                lik = dot(s_ref[i, k], wk, NT)
                s_ref[i, k] = lik
                e_ref[i] = e_ref[i] - dot(lik, own, NN)
                for j in range(1, i + 1):
                    @pl.when(j > k)
                    def _():
                        s_ref[i, j] = s_ref[i, j] - dot(lik, s_ref[j, k], NT)
        return 0

    lax.fori_loop(0, n, step, 0)


def leading_inverse(lead):
    return pl.pallas_call(
        leading_kernel,
        out_shape=jax.ShapeDtypeStruct((4, T, 4 * T), F32),
        in_specs=[VM()],
        out_specs=VM(),
        scratch_shapes=[
            pltpu.VMEM((4, 4, T, T), F32),
            pltpu.VMEM((4, T, 4 * T), F32),
            pltpu.VMEM((T, T), F32),
        ],
        compiler_params=params(),
        cost_estimate=pl.CostEstimate(flops=60_000_000_000, bytes_accessed=2_000_000, transcendentals=0),
        name="leading_inverse",
    )(lead)


def placed_block(block, rows, cols):
    inner = lax.broadcasted_iota(jnp.int32, (T, T), 0).astype(F32)
    row_hot = jnp.where(inner == rows, 1.0, 0.0).astype(BF16)
    col_hot = jnp.where(inner == cols, 1.0, 0.0).astype(BF16)
    high, low = split(block)
    x = lax.dot_general(
        jnp.concatenate([row_hot, row_hot], axis=1), jnp.concatenate([high, low], axis=0), NN, preferred_element_type=F32
    )
    high, low = split(x)
    return lax.dot_general(
        jnp.concatenate([high, low], axis=1), jnp.concatenate([col_hot, col_hot], axis=1), NT, preferred_element_type=F32
    )


def got_block(got_ref, n):
    g, k = n // 2, n % 2
    block = got_ref[g, pl.ds(pl.multiple_of(k * T, T), T), :]
    rows = got_ref[g, pl.ds(2 * T + 2 * k, 1), :]
    cols = got_ref[g, pl.ds(2 * T + 2 * k + 1, 1), :]
    return placed_block(block, rows, cols)


def panel_kernel(tile_cols, slot_total, slot_ref, got_ref, base_ref, out_ref):
    out_ref[...] = base_ref[...]

    def step(n, _):
        slot = slot_ref[n]

        @pl.when((slot < slot_total) & (slot % tile_cols == 0))
        def _():
            a = pl.ds(pl.multiple_of(slot // tile_cols * T, T), T)
            out_ref[a, :] = out_ref[a, :] + got_block(got_ref, n)

        return 0

    lax.fori_loop(0, slot_ref.shape[0], step, 0)


def panel(slots, got, base, tile_cols, slot_total):
    return pl.pallas_call(
        functools.partial(panel_kernel, tile_cols, slot_total),
        out_shape=jax.ShapeDtypeStruct(base.shape, F32),
        grid_spec=pltpu.PrefetchScalarGridSpec(
            num_scalar_prefetch=1, grid=(), in_specs=[VM(), VM()], out_specs=VM()
        ),
        compiler_params=params(),
        name="panel",
    )(slots, got, base)


def rest_kernel(tile_cols, slot_total, slot_ref, got_ref, base_ref, out_ref):
    a = pl.program_id(0)
    out_ref[...] = base_ref[...]

    def step(n, _):
        slot = slot_ref[n]
        b = slot % tile_cols

        @pl.when((slot < slot_total) & (slot // tile_cols == a) & (b > 0))
        def _():
            at = pl.ds(b, T, stride=tile_cols)
            out_ref[at, :] = out_ref[at, :] + got_block(got_ref, n)

        return 0

    lax.fori_loop(0, slot_ref.shape[0], step, 0)


def rest(slots, got, base, tile_rows, tile_cols):
    size = T * tile_cols
    block = pl.BlockSpec((size, T), lambda a, s: (a, 0))
    return pl.pallas_call(
        functools.partial(rest_kernel, tile_cols, tile_rows * tile_cols),
        out_shape=jax.ShapeDtypeStruct(base.shape, F32),
        grid_spec=pltpu.PrefetchScalarGridSpec(
            num_scalar_prefetch=1,
            grid=(tile_rows,),
            in_specs=[pl.BlockSpec(got.shape, lambda a, s: (0, 0, 0)), block],
            out_specs=block,
        ),
        compiler_params=params(),
        cost_estimate=pl.CostEstimate(flops=10_000_000_000, bytes_accessed=26_000_000, transcendentals=0),
        name="rest",
    )(slots, got, base)


def share_kernel(order_ref, x0, x1, x2, x3, wt_ref, out_ref):
    total = None
    for m, x in enumerate((x0, x1, x2, x3)):
        term = dot3(x[...], wt_ref[order_ref[m]], NN)
        total = term if total is None else total + term
    out_ref[...] = total


def share_solve(order, parts, wt):
    return pl.pallas_call(
        share_kernel,
        out_shape=jax.ShapeDtypeStruct((parts[0].shape[0], 4 * T), F32),
        grid_spec=pltpu.PrefetchScalarGridSpec(
            num_scalar_prefetch=1, grid=(), in_specs=[VM()] * 5, out_specs=VM()
        ),
        compiler_params=params(),
        name="share_solve",
    )(order, *parts, wt)


def rows_kernel(info_ref, x0, x1, x2, x3, wt_ref, lhs_ref, own_ref):
    my_col, zero_first = info_ref[4], info_ref[5]
    total = None
    for m, x in enumerate((x0, x1, x2, x3)):
        term = dot3(x[...], wt_ref[info_ref[m]], NN)
        total = term if total is None else total + term
    for j in range(4):
        @pl.when(my_col == j)
        def _():
            own_ref[...] = total[:, j * T : (j + 1) * T]

    row = lax.broadcasted_iota(jnp.int32, total.shape, 0)
    total = jnp.where((row < T) & (zero_first == 1), 0.0, total)
    high, low = split(total)
    lhs_ref[:, 0:512] = high
    lhs_ref[:, 512:1024] = high
    lhs_ref[:, 1024:1536] = low


def rows_solve(info, parts, wt):
    rows = parts[0].shape[0]
    return pl.pallas_call(
        rows_kernel,
        out_shape=(jax.ShapeDtypeStruct((rows, 12 * T), BF16), jax.ShapeDtypeStruct((rows, T), F32)),
        grid_spec=pltpu.PrefetchScalarGridSpec(
            num_scalar_prefetch=1, grid=(), in_specs=[VM()] * 5, out_specs=(VM(), VM())
        ),
        compiler_params=params(),
        cost_estimate=pl.CostEstimate(flops=4_000_000_000, bytes_accessed=8_000_000, transcendentals=0),
        name="rows_solve",
    )(info, *parts, wt)


def update_kernel(tile_cols, group, g_ref, lhs_ref, own_ref, base_ref, out_ref, rhs_ref):
    pairs = tile_cols // 2

    @pl.when(pl.program_id(0) == 0)
    def _():
        for q in range(pairs):
            x = g_ref[:, 32 * q : 32 * q + 32, :].reshape(2 * T, 4 * T)
            high, low = split(x)
            rhs_ref[q, :, 0:512] = high
            rhs_ref[q, :, 512:1024] = low
            rhs_ref[q, :, 1024:1536] = high

    for q in range(pairs):
        u = lax.dot_general(lhs_ref[...], rhs_ref[q], NT, preferred_element_type=F32)
        for a in range(group):
            for b in (2 * q, 2 * q + 1):
                at = pl.ds(a * T * tile_cols + b, T, stride=tile_cols)
                if b == 0:
                    out_ref[at, :] = own_ref[a * T : (a + 1) * T, :]
                else:
                    h = b - 2 * q
                    out_ref[at, :] = base_ref[at, :] - u[a * T : (a + 1) * T, h * T : (h + 1) * T]


def update(gathered, lhs, own, base, tile_rows, tile_cols):
    group = 3
    size = group * T * tile_cols
    return pl.pallas_call(
        functools.partial(update_kernel, tile_cols, group),
        out_shape=jax.ShapeDtypeStruct(base.shape, F32),
        grid=(tile_rows // group,),
        in_specs=[
            pl.BlockSpec(gathered.shape, lambda a: (0, 0, 0)),
            pl.BlockSpec((group * T, 12 * T), lambda a: (a, 0)),
            pl.BlockSpec((group * T, T), lambda a: (a, 0)),
            pl.BlockSpec((size, T), lambda a: (a, 0)),
        ],
        out_specs=pl.BlockSpec((size, T), lambda a: (a, 0)),
        scratch_shapes=[pltpu.VMEM((tile_cols // 2, 2 * T, 12 * T), BF16)],
        compiler_params=params(),
        name="update",
    )(gathered, lhs, own, base)


def local(front, child_updates, child_owner, child_rows, child_cols, child_slot):
    my_row = lax.axis_index("row")
    my_col = lax.axis_index("col")
    tile_rows, tile_cols = front.shape[1], front.shape[4]
    slot_total = tile_rows * tile_cols
    flat = front.reshape(tile_rows * T * tile_cols, T)
    base_panel = front[0, :, 0, :, 0, 0, :].reshape(tile_rows * T, T)

    send = route(child_owner[0, :, 0], child_slot[0], child_updates[0], child_rows[0], child_cols[0], 32, slot_total)
    got = lax.all_to_all(send, ("row", "col"), split_axis=0, concat_axis=0, tiled=True)

    lead = lax.all_gather(base_panel[:T], "row", axis=0)
    lead = lax.all_gather(lead[:4], "col", axis=0)
    wt = leading_inverse(lead)

    slots = got[:, 2 * T + 4 : 2 * T + 6, 0].astype(jnp.int32).reshape(64)
    columns = panel(slots, got, base_panel, tile_cols, slot_total)

    pieces = columns.reshape(tile_rows, 4, T // 4, T)
    parts = []
    for m in range(4):
        piece = lax.dynamic_index_in_dim(pieces, (my_col + m) % 4, axis=1, keepdims=False)
        piece = piece.reshape(tile_rows * T // 4, T)
        moves = [
            ((4 * h + c) * 4 + j, (4 * h + (j + m) % 4) * 4 + c) for h in range(2) for c in range(4) for j in range(4)
        ]
        parts.append(lax.ppermute(piece, ("row", "col"), moves))
    order = (my_row - jnp.arange(4, dtype=jnp.int32)) % 4
    share = share_solve(order, parts, wt)
    gathered = lax.all_gather(share, "row", axis=0)

    right = [(i, (i + 1) % 4) for i in range(4)]
    left = [(i, (i - 1) % 4) for i in range(4)]
    half = tile_rows * T // 2
    from_left = lax.ppermute(columns, "col", right)
    from_right = lax.ppermute(columns, "col", left)
    far_top = lax.ppermute(from_left[:half], "col", right)
    far_bottom = lax.ppermute(from_right[half:], "col", left)
    far = jnp.concatenate([far_top, far_bottom], axis=0)
    info = jnp.concatenate(
        [
            (my_col + jnp.array([0, -1, 1, 2], jnp.int32)) % 4,
            jnp.stack([my_col, (my_row < 4).astype(jnp.int32)]).astype(jnp.int32),
        ]
    )
    lhs, own = rows_solve(info, (columns, from_left, from_right, far), wt)
    base = rest(slots, got, flat, tile_rows, tile_cols)
    result = update(gathered, lhs, own, base, tile_rows, tile_cols)
    return result.reshape(front.shape)


def solution(mesh):
    in_specs = (
        P("front", None, "row", None, None, "col", None),
        P("front", ("row", "col"), None, None),
        P("front", ("row", "col"), None),
        P("front", ("row", "col"), None),
        P("front", ("row", "col"), None),
        P("front", ("row", "col")),
    )
    out_specs = P("front", None, "row", None, None, "col", None)
    return jax.shard_map(local, mesh=mesh, in_specs=in_specs, out_specs=out_specs, check_vma=False)
```

time: 591 us -> 345 us (0.58)
  the two profiles are of different devices: /device:TPU:0 before, /device:TPU:27 now
where the time goes in v1:
time: 345 us; the launch traced here: 343 us
  Pallas kernels  219 us (63%)
  blocking collectives  56.2 us (16%)
  starting transfers between devices  25.4 us (7%)
  waiting for transfers between devices  19.2 us (6%)
  between operations  13.6 us (4%)
  local copies, waits for them, and re-layouts  6.75 us (2%)
  other arithmetic  3.57 us (1%)
    pallas_call x1, Pallas kernels, leading_inverse(): pl.pallas_call(leading_kernel, out_shape=jax.ShapeDtypeStruct((4, T, 4 *...  79.1 us
    pallas_call x1, Pallas kernels, route(): pl.pallas_call(functools.partial(route_kernel, count, slot_total), out_sh...  66.5 us
    all_gather x1, blocking collectives, local(): lead = lax.all_gather(base_panel[:T], 'row', axis=0)  56.2 us
    pallas_call x1, Pallas kernels, rest(): pl.pallas_call(functools.partial(rest_kernel, tile_cols, tile_rows * tile...  37.8 us
    pallas_call x1, Pallas kernels, update(): pl.pallas_call(functools.partial(update_kernel, tile_cols, group), out_sh...  16.3 us
    ppermute x4, starting transfers between devices, local(): parts.append(lax.ppermute(piece, ('row', 'col'), moves))  12.2 us
    ppermute x1, waiting for transfers between devices, local(): from_right = lax.ppermute(columns, 'col', left)  11.4 us
    all_to_all x1, starting transfers between devices, local(): lax.all_to_all(send, ('row', 'col'), split_axis=0, concat_axis=0, tiled=T...  8.75 us
  transfers between devices with their start and end apart: 11, of which 2 were waited for; matrix products, arithmetic and copies ran while one was open for 3% of the time, Pallas kernels for 38%

profile of v1, /device:TPU:27, one launch (start us, length us, event | category | flops | bytes accessed | tf_op | source)
XLA Modules:
  0.0 343.2 jit_solution(4457073290877087081)
XLA Ops:
  6.5 66.5 %route.1 = f32[32,264,128]{2,1,0:T(8,128)} custom-call(s32[32]{0:T(128)} %bitcast.38, s32[32]{0:T(128)} %bitcast.39, f32[32,128,128]{2,1,0:T(8,128)} %bitcast.29, s32[32,128]{1,0:T(8,128)} %bitcast.36, s32[32,128]{1,0:T(8,128)} %bitcast.37), custom_call_target="tpu_custom_call" | custom-call | tf_op jit(solution)/shard_map/route/pallas_call | solution.py:72
  73.1 8.7 %all-to-all-start = ((f32[32,264,128]{2,1,0:T(8,128)}), f32[32,264,128]{2,1,0:T(8,128)}, u32[]{:S(2)}, u32[]{:S(2)}) async-start(f32[32,264,128]{2,1,0:T(8,128)} %route.1), calls=%async_computation | async-start | bytes 8650752 | tf_op jit(solution)/shard_map/all_to_all | solution.py:360
  81.9 0.8 slice.22
  82.7 56.2 %all-gather = f32[8,1,1,128,1,1,128]{6,3,5,4,2,1,0:T(8,128)S(1)} all-gather(f32[1,1,1,128,1,1,128]{6,3,5,4,2,1,0:T(8,128)S(1)} %bitcast.30), channel_id=2, replica_groups=mesh['front'=4,'row'=8,'col'=4] {'row'}, dimensions={0}, use_global_device_ids=true | all-gather | bytes 589824 | tf_op jit(solution)/shard_map/all_gather | solution.py:362
  138.9 0.7 slice.28
  139.8 1.9 slice.21
  142.2 1.5 fusion
  144.4 6.3 %panel.1.x0 = f32[1152,128]{1,0:T(8,128)} custom-call(s32[64]{0:T(128)} %convert_element_type.9.slot_ref, f32[32,264,128]{2,1,0:T(8,128)} %all-to-all-done.got_ref, f32[1152,128]{1,0:T(8,128)} %bitcast.28), custom_call_target="tpu_custom_call" | custom-call | tf_op jit(solution)/shard_map/panel/pallas_call | solution.py:207
  150.7 1.2 constant_dynamic-slice_fusion
  151.8 5.9 %collective-permute-start.2 = (f32[288,128]{1,0:T(8,128)S(1)}, f32[288,128]{1,0:T(8,128)S(1)}, u32[]{:S(2)}, u32[]{:S(2)}) collective-permute-start(f32[288,128]{1,0:T(8,128)S(1)} %bitcast.34), channel_id=1, source_target_pairs={{0,8},{1,12},{2,0},{3,4},{4,9},{5,13},{6,1},{7,5},{8,10},{9,14},{1... | collective-permute-start | bytes 442376 | tf_op jit(solution)/shard_map/ppermute | solution.py:377
  157.7 1.2 collective-permute-start.1
  159.0 5.1 %collective-permute-start = (f32[288,128]{1,0:T(8,128)S(1)}, f32[288,128]{1,0:T(8,128)S(1)}, u32[]{:S(2)}, u32[]{:S(2)}) collective-permute-start(f32[288,128]{1,0:T(8,128)S(1)} %bitcast.31), channel_id=1, source_target_pairs={{0,0},{1,4},{2,8},{3,12},{4,1},{5,5},{6,9},{7,13},{8,2},{9,6},{10,... | collective-permute-start | bytes 442376 | tf_op jit(solution)/shard_map/ppermute | solution.py:377
  164.1 7.7 %all-gather.9.cloned.1.call-done = f32[16,1,1,128,1,1,128]{6,3,5,4,2,1,0:T(8,128)} async-done(((f32[4,1,1,128,1,1,128]{6,3,5,4,2,1,0:T(8,128)}), f32[16,1,1,128,1,1,128]{6,3,5,4,2,1,0:T(8,128)}) %all-gather.9.cloned.1.call-update) | async-done | bytes 1048592 | tf_op jit(solution)/shard_map/all_gather | solution.py:363
  171.8 79.1 %leading_inverse.1.wt_ref = f32[4,128,512]{2,1,0:T(8,128)} custom-call(f32[4,4,128,128]{3,2,1,0:T(8,128)} %bitcast.40), custom_call_target="tpu_custom_call" | custom-call | flops 60000002048 | bytes 2000000 | tf_op jit(solution)/shard_map/leading_inverse/pallas_call | solution.py:152
  251.6 0.6 copy-done.4
  252.3 4.1 %share_solve.1 = f32[288,512]{1,0:T(8,128)} custom-call(s32[4]{0:T(128)} %and_select_fusion.1.order_ref, f32[288,128]{1,0:T(8,128)} %copy-done.4, f32[288,128]{1,0:T(8,128)} %copy-done.3, f32[288,128]{1,0:T(8,128)} %copy-done.1, f32[288,128]{1,0:T(8,128)} %copy-done.2, f32[4,128,512]{2,1,0:T(8,128)} %leading_inverse.1.wt_ref), custom_call_target="tpu_custom_call" | custom-call | tf_op jit(solution)/shard_map/share_solve/pallas_call | solution.py:263
  256.4 1.1 collective-permute-start.5
  257.9 0.7 pad_add_fusion.info_ref
  258.6 11.4 %collective-permute-done.5.x2 = f32[1152,128]{1,0:T(8,128)S(1)} collective-permute-done((f32[1152,128]{1,0:T(8,128)S(1)}, f32[1152,128]{1,0:T(8,128)S(1)}, u32[]{:S(2)}, u32[]{:S(2)}) %collective-permute-start.5) | collective-permute-done | bytes 589856 | tf_op jit(solution)/shard_map/ppermute | solution.py:386
  270.0 2.5 collective-permute-start.7
  272.8 37.8 %rest.1.base_ref = f32[20736,128]{1,0:T(8,128)} custom-call(s32[64]{0:T(128)} %convert_element_type.9.slot_ref, f32[32,264,128]{2,1,0:T(8,128)} %all-to-all-done.got_ref, f32[20736,128]{1,0:T(8,128)} %bitcast.35), custom_call_target="tpu_custom_call" | custom-call | flops 10000000000 | bytes 26000000 | tf_op jit(solution)/shard_map/rest/pallas_call | solution.py:239
  310.6 0.9 pad_maximum_fusion.x3
  311.5 8.6 %rows_solve.1 = (bf16[1152,1536]{1,0:T(8,128)(2,1)}, f32[1152,128]{1,0:T(8,128)}) custom-call(s32[6]{0:T(128)} %pad_add_fusion.info_ref, f32[1152,128]{1,0:T(8,128)} %panel.1.x0, f32[1152,128]{1,0:T(8,128)} %copy-done.6, f32[1152,128]{1,0:T(8,128)} %copy-done.5, f32[1152,128]{1,0:T(8,128)} %pad_maximum_fusion.x3, f32[4,128,512]{2,1,0:T(8,128)} %leading_inverse.1.wt_ref), custom_call_target="tpu_custom_call" | custom-call | flops 4000000000 | bytes 8000000 | tf_op jit(solution)/shard_map/rows_solve/pallas_call | solution.py:295
  320.1 16.3 %update.1 = f32[20736,128]{1,0:T(8,128)} custom-call(f32[8,288,512]{2,1,0:T(8,128)} %bitcast.26, bf16[1152,1536]{1,0:T(8,128)(2,1)} %get-tuple-element.7.lhs_ref, f32[1152,128]{1,0:T(8,128)} %get-tuple-element.8.own_ref, f32[20736,128]{1,0:T(8,128)} %rest.1.base_ref), custom_call_target="tpu_custom_call" | custom-call | tf_op jit(solution)/shard_map/update/pallas_call | solution.py:334
  (36 shorter events, 2.8 us)
Async XLA Ops:
  73.1 69.2 %all-to-all-start = ((f32[32,264,128]{2,1,0:T(8,128)}), f32[32,264,128]{2,1,0:T(8,128)}, u32[]{:S(2)}, u32[]{:S(2)}) async-start(f32[32,264,128]{2,1,0:T(8,128)} %route.1), calls=%async_computation | async-start | bytes 8650752 | tf_op jit(solution)/shard_map/all_to_all | solution.py:360
  81.8 90.0 %all-gather.9.cloned.1.call-start = ((), (), s32[]{:S(2)}) async-start(), calls=%async_computation.2 | async-start | bytes 1310720 | tf_op jit(solution)/shard_map/all_gather | solution.py:363
  139.7 180.4 %all-gather.7.cloned.1.call-start = ((), (), s32[]{:S(2)}) async-start(), calls=%async_computation.1 | async-start | bytes 5308416 | tf_op jit(solution)/shard_map/all_gather | solution.py:380
  151.8 99.0 %collective-permute-start.2 = (f32[288,128]{1,0:T(8,128)S(1)}, f32[288,128]{1,0:T(8,128)S(1)}, u32[]{:S(2)}, u32[]{:S(2)}) collective-permute-start(f32[288,128]{1,0:T(8,128)S(1)} %bitcast.34), channel_id=1, source_target_pairs={{0,8},{1,12},{2,0},{3,4},{4,9},{5,13},{6,1},{7,5},{8,10},{9,14},{1... | collective-permute-start | bytes 442376 | tf_op jit(solution)/shard_map/ppermute | solution.py:377
  157.7 93.1 %collective-permute-start.3 = (f32[288,128]{1,0:T(8,128)S(1)}, f32[288,128]{1,0:T(8,128)S(1)}, u32[]{:S(2)}, u32[]{:S(2)}) collective-permute-start(f32[288,128]{1,0:T(8,128)S(1)} %bitcast.33), channel_id=1, source_target_pairs={{0,12},{1,0},{2,4},{3,8},{4,13},{5,1},{6,5},{7,9},{8,14},{9,2},{10... | collective-permute-start | bytes 442376 | tf_op jit(solution)/shard_map/ppermute | solution.py:377
  157.7 93.1 %collective-permute-start.1 = (f32[288,128]{1,0:T(8,128)S(1)}, f32[288,128]{1,0:T(8,128)S(1)}, u32[]{:S(2)}, u32[]{:S(2)}) collective-permute-start(f32[288,128]{1,0:T(8,128)S(1)} %bitcast.32), channel_id=1, source_target_pairs={{0,4},{1,8},{2,12},{3,0},{4,5},{5,9},{6,13},{7,1},{8,6},{9,10},{10... | collective-permute-start | bytes 442376 | tf_op jit(solution)/shard_map/ppermute | solution.py:377
  159.0 91.9 %collective-permute-start = (f32[288,128]{1,0:T(8,128)S(1)}, f32[288,128]{1,0:T(8,128)S(1)}, u32[]{:S(2)}, u32[]{:S(2)}) collective-permute-start(f32[288,128]{1,0:T(8,128)S(1)} %bitcast.31), channel_id=1, source_target_pairs={{0,0},{1,4},{2,8},{3,12},{4,1},{5,5},{6,9},{7,13},{8,2},{9,6},{10,... | collective-permute-start | bytes 442376 | tf_op jit(solution)/shard_map/ppermute | solution.py:377
  171.8 84.6 %copy-start = (f32[1152,128]{1,0:T(8,128)S(1)}, f32[1152,128]{1,0:T(8,128)}, u32[]{:S(2)}) copy-start(f32[1152,128]{1,0:T(8,128)} %panel.1.x0) | copy-start | bytes 1769476
  171.8 86.1 %copy-start.7 = (s32[4]{0:T(128)S(1)}, s32[4]{0:T(128)}, u32[]{:S(2)}) copy-start(s32[4]{0:T(128)} %constant.64.clone) | copy-start | bytes 52
  250.9 0.7 copy-start.1
  250.9 0.7 copy-start.2
  250.9 0.8 copy-start.3
  251.6 0.7 copy-start.4
  256.4 13.6 %collective-permute-start.5 = (f32[1152,128]{1,0:T(8,128)S(1)}, f32[1152,128]{1,0:T(8,128)S(1)}, u32[]{:S(2)}, u32[]{:S(2)}) collective-permute-start(f32[1152,128]{1,0:T(8,128)S(1)} %copy-done), channel_id=1, source_target_pairs={{0,3},{1,0},{2,1},{3,2},{4,7},{5,4},{6,5},{7,6},{8,11},{9,8},{10,9... | collective-permute-start | bytes 1769480 | tf_op jit(solution)/shard_map/ppermute | solution.py:386
  257.5 15.0 %collective-permute-start.4 = (f32[1152,128]{1,0:T(8,128)S(1)}, f32[1152,128]{1,0:T(8,128)S(1)}, u32[]{:S(2)}, u32[]{:S(2)}) collective-permute-start(f32[1152,128]{1,0:T(8,128)S(1)} %copy-done), channel_id=1, source_target_pairs={{0,1},{1,2},{2,3},{3,0},{4,5},{5,6},{6,7},{7,4},{8,9},{9,10},{10,1... | collective-permute-start | bytes 1769480 | tf_op jit(solution)/shard_map/ppermute | solution.py:385
  270.0 40.6 %copy-start.5 = (f32[1152,128]{1,0:T(8,128)}, f32[1152,128]{1,0:T(8,128)S(1)}, u32[]{:S(2)}) copy-start(f32[1152,128]{1,0:T(8,128)S(1)} %collective-permute-done.5.x2) | copy-start | bytes 1769476
  270.0 40.6 %collective-permute-start.7 = (f32[576,128]{1,0:T(8,128)S(1)}, f32[576,128]{1,0:T(8,128)S(1)}, u32[]{:S(2)}, u32[]{:S(2)}) collective-permute-start(f32[576,128]{1,0:T(8,128)S(1)} %slice.30), channel_id=1, source_target_pairs={{0,3},{1,0},{2,1},{3,2},{4,7},{5,4},{6,5},{7,6},{8,11},{9,8},{10,9... | collective-permute-start | bytes 884744 | tf_op jit(solution)/shard_map/ppermute | solution.py:388
  272.5 38.0 %copy-start.6 = (f32[1152,128]{1,0:T(8,128)}, f32[1152,128]{1,0:T(8,128)S(1)}, u32[]{:S(2)}) copy-start(f32[1152,128]{1,0:T(8,128)S(1)} %collective-permute-done.4.x1) | copy-start | bytes 1769476
  272.6 38.0 %collective-permute-start.6 = (f32[576,128]{1,0:T(8,128)S(1)}, f32[576,128]{1,0:T(8,128)S(1)}, u32[]{:S(2)}, u32[]{:S(2)}) collective-permute-start(f32[576,128]{1,0:T(8,128)S(1)} %slice.29), channel_id=1, source_target_pairs={{0,1},{1,2},{2,3},{3,0},{4,5},{5,6},{6,7},{7,4},{8,9},{9,10},{10,1... | collective-permute-start | bytes 884744 | tf_op jit(solution)/shard_map/ppermute | solution.py:387
Sparse Core Ops, SparseCore 0:
  139.8 31.9 all-gather.8
  256.5 34.6 all-gather.6

commit v2 on v1

v2 whole, which is shorter than its diff:
```python
import functools

import jax
import jax.numpy as jnp
from jax import lax
from jax.experimental import pallas as pl
from jax.experimental.pallas import tpu as pltpu
from jax.sharding import PartitionSpec as P

T = 128
F32 = jnp.float32
BF16 = jnp.bfloat16
HIGHEST = lax.Precision.HIGHEST
NT = (((1,), (1,)), ((), ()))
NN = (((1,), (0,)), ((), ()))
VM = functools.partial(pl.BlockSpec, memory_space=pltpu.VMEM)
ANY = functools.partial(pl.BlockSpec, memory_space=pl.ANY)
LIMIT = 60 * 1024 * 1024


def params():
    return pltpu.CompilerParams(vmem_limit_bytes=LIMIT)


def split(x):
    high = x.astype(BF16)
    low = (x - high.astype(F32)).astype(BF16)
    return high, low


def placed_block(block, rows, cols):
    inner = lax.broadcasted_iota(jnp.int32, (T, T), 0)
    row_hot = jnp.where(inner == rows, 1.0, 0.0).astype(BF16)
    col_hot = jnp.where(inner == cols, 1.0, 0.0).astype(BF16)
    high, low = split(block)
    x = lax.dot_general(
        jnp.concatenate([row_hot, row_hot], axis=1), jnp.concatenate([high, low], axis=0), NN, preferred_element_type=F32
    )
    high, low = split(x)
    return lax.dot_general(
        jnp.concatenate([high, low], axis=1), jnp.concatenate([col_hot, col_hot], axis=1), NT, preferred_element_type=F32
    )


def route_kernel(group, slot_total, owner_ref, slot_ref, blocks_ref, rows_ref, cols_ref, send_ref, meta, held, count, sem):
    owners = meta.shape[0]
    blocks = held.shape[0]
    step = pl.program_id(0)

    def at(g, o, k):
        return pltpu.make_async_copy(
            held.at[g], send_ref.at[o, pl.ds(pl.multiple_of(k * T, T), T), :], sem.at[g]
        )

    @pl.when(step == 0)
    def _():
        meta[...] = jnp.full(meta.shape, float(slot_total), F32)

        def clear(o, _):
            count[o] = 0
            return 0

        lax.fori_loop(0, owners, clear, 0)

    for q in range(group):
        g = step * group + q
        held[g] = placed_block(blocks_ref[q], rows_ref[pl.ds(g, 1), :], cols_ref[pl.ds(g, 1), :])
    for q in range(group):
        g = step * group + q
        o = owner_ref[g]
        k = jnp.minimum(count[o], 1)
        count[o] = k + 1
        meta[o, pl.ds(k, 1), :] = jnp.full((1, T), slot_ref[g], jnp.int32).astype(F32)
        at(g, o, k).start()

    @pl.when(step == pl.num_programs(0) - 1)
    def _():
        tail = pltpu.make_async_copy(meta, send_ref.at[:, pl.ds(2 * T, 8), :], sem.at[blocks])
        tail.start()

        def finish(g, _):
            at(g, 0, 0).wait()
            return 0

        lax.fori_loop(0, blocks, finish, 0)
        tail.wait()


def route(owner, slot, blocks, rows, cols, owners, slot_total):
    count = blocks.shape[0]
    group = 4
    whole = pl.BlockSpec((count, T), lambda i, *_: (0, 0))
    return pl.pallas_call(
        functools.partial(route_kernel, group, slot_total),
        out_shape=jax.ShapeDtypeStruct((owners, 2 * T + 8, T), F32),
        grid_spec=pltpu.PrefetchScalarGridSpec(
            num_scalar_prefetch=2,
            grid=(count // group,),
            in_specs=[pl.BlockSpec((group, T, T), lambda i, *_: (i, 0, 0)), whole, whole],
            out_specs=ANY(),
            scratch_shapes=[
                pltpu.VMEM((owners, 8, T), F32),
                pltpu.VMEM((count, T, T), F32),
                pltpu.SMEM((owners,), jnp.int32),
                pltpu.SemaphoreType.DMA((count + 1,)),
            ],
        ),
        compiler_params=params(),
        name="route",
    )(owner, slot, blocks, rows, cols)


def sub_row(x, k):
    return jnp.broadcast_to(x[k : k + 1, :], (8, T))


def lane_col(x, k):
    return jnp.broadcast_to(x[:, k : k + 1], (8, T))


def tree_sum(x):
    while len(x) > 1:
        x = [x[i] + x[i + 1] for i in range(0, len(x), 2)]
    return x[0]


def inverse_factor(s, out_ref):
    groups = T // 8
    lane = lax.broadcasted_iota(jnp.int32, (8, T), 1)
    sub = lax.broadcasted_iota(jnp.int32, (8, T), 0)
    m = [s[8 * g : 8 * g + 8, :] for g in range(groups)]
    e = [jnp.where(lane == sub + 8 * g, 1.0, 0.0).astype(F32) for g in range(groups)]
    for p in range(groups):
        v = [sub_row(m[p], k) for k in range(8)]
        x = [sub_row(e[p], k) for k in range(8)]
        column = [lane_col(m[p], 8 * p + c) for c in range(8)]
        d = [[sub_row(column[c], r) if c <= r else None for c in range(8)] for r in range(8)]
        below = {g: [lane_col(m[g], 8 * p + c) for c in range(8)] for g in range(p + 1, groups)}
        inv = [None] * 8
        low = [[None] * 8 for _ in range(8)]
        for k in range(8):
            inv[k] = 1.0 / d[k][k]
            for r in range(k + 1, 8):
                low[r][k] = d[r][k] * inv[k]
            for r in range(k + 1, 8):
                for c in range(k + 1, r + 1):
                    d[r][c] = d[r][c] - low[r][k] * d[c][k]
                v[r] = v[r] - low[r][k] * v[k]
                x[r] = x[r] - low[r][k] * x[k]
        for k in range(8):
            out_ref[8 * p + k : 8 * p + k + 1, :] = (x[k] * lax.sqrt(inv[k]))[0:1, :]
        if p == groups - 1:
            break
        v = [v[k] * inv[k] for k in range(8)]
        x = [x[k] * inv[k] for k in range(8)]
        for k in range(7, 0, -1):
            for j in range(k):
                v[j] = v[j] - low[k][j] * v[k]
                x[j] = x[j] - low[k][j] * x[k]
        for g in range(p + 1, groups):
            m[g] = m[g] - tree_sum([below[g][k] * v[k] for k in range(8)])
            e[g] = e[g] - tree_sum([below[g][k] * x[k] for k in range(8)])


def leading_kernel(lead_ref, high_ref, low_ref, s_ref, e_ref, w_ref):
    n = 4
    dot = functools.partial(lax.dot_general, precision=HIGHEST, preferred_element_type=F32)
    for i in range(n):
        for j in range(i + 1):
            s_ref[i, j] = 0.5 * (lead_ref[i, j] + lead_ref[j, i].T)
    e_ref[...] = jnp.zeros_like(e_ref)

    def step(k, _):
        inverse_factor(s_ref[k, k], w_ref)
        wk = w_ref[...]
        own = dot(wk, e_ref[k], NN)
        column = lax.broadcasted_iota(jnp.int32, (T, n * T), 1)
        spread = jnp.concatenate([wk] * n, axis=1)
        own = jnp.where(column // T == k, spread, own)
        for j in range(n):
            at = pl.ds(pl.multiple_of(k * T, T), T)
            high, low = split(own[:, j * T : (j + 1) * T].T)
            high_ref[j, :, at] = high
            low_ref[j, :, at] = low

        for i in range(1, n):
            @pl.when(i > k)
            def _():
                lik = dot(s_ref[i, k], wk, NT)
                s_ref[i, k] = lik
                e_ref[i] = e_ref[i] - dot(lik, own, NN)
                for j in range(1, i + 1):
                    @pl.when(j > k)
                    def _():
                        s_ref[i, j] = s_ref[i, j] - dot(lik, s_ref[j, k], NT)
        return 0

    lax.fori_loop(0, n, step, 0)


def leading_inverse(lead):
    return pl.pallas_call(
        leading_kernel,
        out_shape=(jax.ShapeDtypeStruct((4, T, 4 * T), BF16),) * 2,
        in_specs=[VM()],
        out_specs=(VM(), VM()),
        scratch_shapes=[
            pltpu.VMEM((4, 4, T, T), F32),
            pltpu.VMEM((4, T, 4 * T), F32),
            pltpu.VMEM((T, T), F32),
        ],
        compiler_params=params(),
        cost_estimate=pl.CostEstimate(flops=60_000_000_000, bytes_accessed=2_000_000, transcendentals=0),
        name="leading_inverse",
    )(lead)


def panel_kernel(tile_cols, slot_total, slot_ref, col_ref, got_ref, base_ref, out_ref, p0, p1, p2, p3, held, sem):
    total = slot_ref.shape[0]

    def wanted(n):
        slot = slot_ref[n]
        return (slot < slot_total) & (slot % tile_cols == 0)

    def copy(n):
        block = got_ref.at[n // 2, pl.ds(pl.multiple_of(n % 2 * T, T), T), :]
        return pltpu.make_async_copy(block, held.at[n], sem.at[n])

    def fetch(n, _):
        @pl.when(wanted(n))
        def _():
            copy(n).start()

        return 0

    lax.fori_loop(0, total, fetch, 0)
    out_ref[...] = base_ref[...]

    def add(n, _):
        @pl.when(wanted(n))
        def _():
            copy(n).wait()
            a = pl.ds(pl.multiple_of(slot_ref[n] // tile_cols * T, T), T)
            out_ref[a, :] = out_ref[a, :] + held[n]

        return 0

    lax.fori_loop(0, total, add, 0)
    quarter = T // 4
    for m, piece in enumerate((p0, p1, p2, p3)):
        first = lax.rem(col_ref[0] + m, 4) * quarter
        for a in range(out_ref.shape[0] // T):
            piece[a * quarter : (a + 1) * quarter, :] = out_ref[pl.ds(pl.multiple_of(a * T + first, quarter), quarter), :]


def panel(slots, col, got, base, tile_cols, slot_total):
    rows = base.shape[0]
    total = slots.shape[0]
    return pl.pallas_call(
        functools.partial(panel_kernel, tile_cols, slot_total),
        out_shape=(jax.ShapeDtypeStruct((rows, T), F32),) + (jax.ShapeDtypeStruct((rows // 4, T), F32),) * 4,
        grid_spec=pltpu.PrefetchScalarGridSpec(
            num_scalar_prefetch=2,
            grid=(),
            in_specs=[ANY(), VM()],
            out_specs=(VM(),) * 5,
            scratch_shapes=[pltpu.VMEM((total, T, T), F32), pltpu.SemaphoreType.DMA((total,))],
        ),
        compiler_params=params(),
        name="panel",
    )(slots, col, got, base)


def rest_kernel(tile_cols, slot_total, slot_ref, got_ref, base_ref, out_ref):
    a = pl.program_id(0)
    out_ref[...] = base_ref[...]

    def step(n, _):
        slot = slot_ref[n]
        b = slot - a * tile_cols

        @pl.when((b > 0) & (b < tile_cols))
        def _():
            at = pl.ds(b, T, stride=tile_cols)
            out_ref[at, :] = out_ref[at, :] + got_ref[n // 2, pl.ds(pl.multiple_of(n % 2 * T, T), T), :]

        return 0

    lax.fori_loop(0, slot_ref.shape[0], step, 0)


def rest(slots, got, base, tile_rows, tile_cols):
    size = T * tile_cols
    block = pl.BlockSpec((size, T), lambda a, s: (a, 0))
    return pl.pallas_call(
        functools.partial(rest_kernel, tile_cols, tile_rows * tile_cols),
        out_shape=jax.ShapeDtypeStruct(base.shape, F32),
        grid_spec=pltpu.PrefetchScalarGridSpec(
            num_scalar_prefetch=1,
            grid=(tile_rows,),
            in_specs=[pl.BlockSpec(got.shape, lambda a, s: (0, 0, 0)), block],
            out_specs=block,
        ),
        compiler_params=params(),
        cost_estimate=pl.CostEstimate(flops=10_000_000_000, bytes_accessed=26_000_000, transcendentals=0),
        name="rest",
    )(slots, got, base)


def load_rhs(order_ref, high_ref, low_ref, rhs_ref):
    for m in range(4):
        high, low = high_ref[order_ref[m]], low_ref[order_ref[m]]
        rhs_ref[m * T : (m + 1) * T, :] = high
        rhs_ref[(4 + m) * T : (5 + m) * T, :] = low
        rhs_ref[(8 + m) * T : (9 + m) * T, :] = high


def times_wt(parts, rhs_ref):
    pairs = [split(x) for x in parts]
    high, low = [p[0] for p in pairs], [p[1] for p in pairs]
    return lax.dot_general(
        jnp.concatenate(high + high + low, axis=1), rhs_ref[...], NN, preferred_element_type=F32
    )


def share_kernel(order_ref, x0, x1, x2, x3, high_ref, low_ref, out_ref, rhs_ref):
    load_rhs(order_ref, high_ref, low_ref, rhs_ref)
    out_ref[...] = times_wt([x[...] for x in (x0, x1, x2, x3)], rhs_ref)


def share_solve(order, parts, wt):
    return pl.pallas_call(
        share_kernel,
        out_shape=jax.ShapeDtypeStruct((parts[0].shape[0], 4 * T), F32),
        grid_spec=pltpu.PrefetchScalarGridSpec(
            num_scalar_prefetch=1,
            grid=(),
            in_specs=[VM()] * 6,
            out_specs=VM(),
            scratch_shapes=[pltpu.VMEM((12 * T, 4 * T), BF16)],
        ),
        compiler_params=params(),
        name="share_solve",
    )(order, *parts, *wt)


def rows_kernel(info_ref, x0, x1, x2, x3, high_ref, low_ref, lhs_ref, own_ref, rhs_ref):
    load_rhs(info_ref, high_ref, low_ref, rhs_ref)
    my_col, zero_first = info_ref[4], info_ref[5]
    chunk = 3 * T
    for c in range(x0.shape[0] // chunk):
        at = slice(c * chunk, (c + 1) * chunk)
        total = times_wt([x[at, :] for x in (x0, x1, x2, x3)], rhs_ref)
        for j in range(4):
            @pl.when(my_col == j)
            def _():
                own_ref[at, :] = total[:, j * T : (j + 1) * T]

        if c == 0:
            row = lax.broadcasted_iota(jnp.int32, total.shape, 0)
            total = jnp.where((row < T) & (zero_first == 1), 0.0, total)
        high, low = split(total)
        lhs_ref[at, 0:512] = high
        lhs_ref[at, 512:1024] = high
        lhs_ref[at, 1024:1536] = low


def rows_solve(info, parts, wt):
    rows = parts[0].shape[0]
    return pl.pallas_call(
        rows_kernel,
        out_shape=(jax.ShapeDtypeStruct((rows, 12 * T), BF16), jax.ShapeDtypeStruct((rows, T), F32)),
        grid_spec=pltpu.PrefetchScalarGridSpec(
            num_scalar_prefetch=1,
            grid=(),
            in_specs=[VM()] * 6,
            out_specs=(VM(), VM()),
            scratch_shapes=[pltpu.VMEM((12 * T, 4 * T), BF16)],
        ),
        compiler_params=params(),
        cost_estimate=pl.CostEstimate(flops=4_000_000_000, bytes_accessed=8_000_000, transcendentals=0),
        name="rows_solve",
    )(info, *parts, *wt)


def update_kernel(tile_cols, group, g_ref, lhs_ref, own_ref, base_ref, out_ref, rhs_ref):
    pairs = tile_cols // 2

    @pl.when(pl.program_id(0) == 0)
    def _():
        for q in range(pairs):
            x = g_ref[:, 32 * q : 32 * q + 32, :].reshape(2 * T, 4 * T)
            high, low = split(x)
            rhs_ref[q, :, 0:512] = high
            rhs_ref[q, :, 512:1024] = low
            rhs_ref[q, :, 1024:1536] = high

    for q in range(pairs):
        u = lax.dot_general(lhs_ref[...], rhs_ref[q], NT, preferred_element_type=F32)
        for a in range(group):
            for b in (2 * q, 2 * q + 1):
                at = pl.ds(a * T * tile_cols + b, T, stride=tile_cols)
                if b == 0:
                    out_ref[at, :] = own_ref[a * T : (a + 1) * T, :]
                else:
                    h = b - 2 * q
                    out_ref[at, :] = base_ref[at, :] - u[a * T : (a + 1) * T, h * T : (h + 1) * T]


def update(gathered, lhs, own, base, tile_rows, tile_cols):
    group = 3
    size = group * T * tile_cols
    return pl.pallas_call(
        functools.partial(update_kernel, tile_cols, group),
        out_shape=jax.ShapeDtypeStruct(base.shape, F32),
        grid=(tile_rows // group,),
        in_specs=[
            pl.BlockSpec(gathered.shape, lambda a: (0, 0, 0)),
            pl.BlockSpec((group * T, 12 * T), lambda a: (a, 0)),
            pl.BlockSpec((group * T, T), lambda a: (a, 0)),
            pl.BlockSpec((size, T), lambda a: (a, 0)),
        ],
        out_specs=pl.BlockSpec((size, T), lambda a: (a, 0)),
        scratch_shapes=[pltpu.VMEM((tile_cols // 2, 2 * T, 12 * T), BF16)],
        compiler_params=params(),
        name="update",
    )(gathered, lhs, own, base)


def local(front, child_updates, child_owner, child_rows, child_cols, child_slot):
    my_row = lax.axis_index("row")
    my_col = lax.axis_index("col")
    tile_rows, tile_cols = front.shape[1], front.shape[4]
    slot_total = tile_rows * tile_cols
    flat = front.reshape(tile_rows * T * tile_cols, T)
    base_panel = front[0, :, 0, :, 0, 0, :].reshape(tile_rows * T, T)

    send = route(child_owner[0, :, 0], child_slot[0], child_updates[0], child_rows[0], child_cols[0], 32, slot_total)
    got = lax.all_to_all(send, ("row", "col"), split_axis=0, concat_axis=0, tiled=True)

    lead = lax.all_gather(base_panel[:T], ("row", "col"), axis=0)
    lead = lead.reshape(8, 4, T, T)[:4]
    wt = leading_inverse(lead)

    slots = got[:, 2 * T : 2 * T + 2, 0].astype(jnp.int32).reshape(64)
    columns, *pieces = panel(slots, my_col.reshape(1), got, base_panel, tile_cols, slot_total)

    parts = []
    for m in range(4):
        moves = [
            ((4 * h + c) * 4 + j, (4 * h + (j + m) % 4) * 4 + c) for h in range(2) for c in range(4) for j in range(4)
        ]
        parts.append(lax.ppermute(pieces[m], ("row", "col"), moves))
    order = (my_row - jnp.arange(4, dtype=jnp.int32)) % 4
    share = share_solve(order, parts, wt)
    gathered = lax.all_gather(share, "row", axis=0)

    right = [(i, (i + 1) % 4) for i in range(4)]
    left = [(i, (i - 1) % 4) for i in range(4)]
    half = tile_rows * T // 2
    from_left = lax.ppermute(columns, "col", right)
    from_right = lax.ppermute(columns, "col", left)
    far_top = lax.ppermute(from_left[:half], "col", right)
    far_bottom = lax.ppermute(from_right[half:], "col", left)
    far = jnp.concatenate([far_top, far_bottom], axis=0)
    info = jnp.concatenate(
        [
            (my_col + jnp.array([0, -1, 1, 2], jnp.int32)) % 4,
            jnp.stack([my_col, (my_row < 4).astype(jnp.int32)]).astype(jnp.int32),
        ]
    )
    lhs, own = rows_solve(info, (columns, from_left, from_right, far), wt)
    base = rest(slots, got, flat, tile_rows, tile_cols)
    result = update(gathered, lhs, own, base, tile_rows, tile_cols)
    return result.reshape(front.shape)


def solution(mesh):
    in_specs = (
        P("front", None, "row", None, None, "col", None),
        P("front", ("row", "col"), None, None),
        P("front", ("row", "col"), None),
        P("front", ("row", "col"), None),
        P("front", ("row", "col"), None),
        P("front", ("row", "col")),
    )
    out_specs = P("front", None, "row", None, None, "col", None)
    return jax.shard_map(local, mesh=mesh, in_specs=in_specs, out_specs=out_specs, check_vma=False)
```

time: 345 us -> 215 us (0.62)
  the two profiles are of different devices: /device:TPU:27 before, /device:TPU:0 now
where the time goes in v2:
time: 215 us; the launch traced here: 213 us
  Pallas kernels  87.5 us (41%)
  waiting for transfers between devices  80.5 us (37%)
  starting transfers between devices  20.9 us (10%)
  between operations  13.5 us (6%)
  local copies, waits for them, and re-layouts  7.25 us (3%)
  other arithmetic  3.66 us (2%)
    all_gather x1, waiting for transfers between devices, local(): lead = lax.all_gather(base_panel[:T], ('row', 'col'), axis=0)  68.4 us
    pallas_call x1, Pallas kernels, leading_inverse(): pl.pallas_call(leading_kernel, out_shape=(jax.ShapeDtypeStruct((4, T, 4 *...  30.4 us
    pallas_call x1, Pallas kernels, rest(): pl.pallas_call(functools.partial(rest_kernel, tile_cols, tile_rows * tile...  16.8 us
    pallas_call x1, Pallas kernels, update(): pl.pallas_call(functools.partial(update_kernel, tile_cols, group), out_sh...  16.3 us
    ppermute x1, waiting for transfers between devices, local(): from_right = lax.ppermute(columns, 'col', left)  12 us
    all_to_all x1, starting transfers between devices, local(): lax.all_to_all(send, ('row', 'col'), split_axis=0, concat_axis=0, tiled=T...  8.54 us
    ppermute x4, starting transfers between devices, local(): parts.append(lax.ppermute(pieces[m], ('row', 'col'), moves))  8.07 us
    pallas_call x1, Pallas kernels, route(): pl.pallas_call(functools.partial(route_kernel, group, slot_total), out_sh...  8.03 us
  transfers between devices with their start and end apart: 11, of which 2 were waited for; matrix products, arithmetic and copies ran while one was open for 4% of the time, Pallas kernels for 26%

profile of v2, /device:TPU:0, one launch (start us, length us, event | category | flops | bytes accessed | tf_op | source)
XLA Modules:
  0.0 213.3 jit_solution(14170566913584945869)
XLA Ops:
  6.5 8.0 %route.1 = f32[32,264,128]{2,1,0:T(8,128)} custom-call(s32[32]{0:T(128)} %bitcast.21, s32[32]{0:T(128)} %bitcast.22, f32[32,128,128]{2,1,0:T(8,128)} %bitcast.15, s32[32,128]{1,0:T(8,128)} %bitcast.19, s32[32,128]{1,0:T(8,128)} %bitcast.20), custom_call_target="tpu_custom_call" | custom-call | tf_op jit(solution)/shard_map/route/pallas_call | solution.py:93
  14.6 8.5 %all-to-all-start = ((f32[32,264,128]{2,1,0:T(8,128)}), f32[32,264,128]{2,1,0:T(8,128)}, u32[]{:S(2)}, u32[]{:S(2)}) async-start(f32[32,264,128]{2,1,0:T(8,128)} %route.1), calls=%async_computation | async-start | bytes 8650752 | tf_op jit(solution)/shard_map/all_to_all | solution.py:439
  23.2 1.5 slice.25
  24.7 1.9 slice.24
  27.2 68.4 %all-gather.5.cloned.1.call-done = f32[32,1,1,128,1,1,128]{6,3,5,4,2,1,0:T(8,128)} async-done(((f32[1,1,1,128,1,1,128]{6,3,5,4,2,1,0:T(8,128)}), f32[32,1,1,128,1,1,128]{6,3,5,4,2,1,0:T(8,128)}) %all-gather.5.cloned.1.call-update) | async-done | bytes 2097168 | tf_op jit(solution)/shard_map/all_gather | solution.py:441
  95.6 2.3 %slice.32 = f32[16,1,1,128,1,1,128]{6,3,5,4,2,1,0:T(8,128)} slice(f32[32,1,1,128,1,1,128]{6,3,5,4,2,1,0:T(8,128)} %all-gather.5.cloned.1.call-done), slice={[0:16], [0:1], [0:1], [0:128], [0:1], [0:1], [0:128]} | slice | bytes 2097152 | tf_op jit(solution)/shard_map/slice | solution.py:442
  97.9 1.5 fusion
  99.5 0.7 convert_element_type.9.slot_ref
  100.2 4.9 %panel.1 = (f32[1152,128]{1,0:T(8,128)}, f32[288,128]{1,0:T(8,128)}, f32[288,128]{1,0:T(8,128)}, f32[288,128]{1,0:T(8,128)}, f32[288,128]{1,0:T(8,128)}) custom-call(s32[64]{0:T(128)} %convert_element_type.9.slot_ref, s32[1]{0:T(128)} %bitcast.5.col_ref, f32[32,264,128]{2,1,0:T(8,128)} %all-to-all-done.got_ref, f32[1152,128]{1,0:T(8,128)} %bitcast.14), custom_call_target="tpu_custom_call" | custom-call | tf_op jit(solution)/shard_map/panel/pallas_call | solution.py:259
  105.0 1.6 collective-permute-start
  106.6 1.8 collective-permute-start.1
  108.4 2.9 %collective-permute-start.2 = (f32[288,128]{1,0:T(8,128)}, f32[288,128]{1,0:T(8,128)S(1)}, u32[]{:S(2)}, u32[]{:S(2)}) collective-permute-start(f32[288,128]{1,0:T(8,128)} %get-tuple-element.16), channel_id=1, source_target_pairs={{0,8},{1,12},{2,0},{3,4},{4,9},{5,13},{6,1},{7,5},{8,10},{9,14},{1... | collective-permute-start | bytes 442376 | tf_op jit(solution)/shard_map/ppermute | solution.py:453
  111.3 1.8 collective-permute-start.3
  113.1 30.4 %leading_inverse.1 = (bf16[4,128,512]{2,1,0:T(8,128)(2,1)}, bf16[4,128,512]{2,1,0:T(8,128)(2,1)}) custom-call(f32[4,4,128,128]{3,2,1,0:T(8,128)} %bitcast.16), custom_call_target="tpu_custom_call" | custom-call | flops 60000002048 | bytes 2000000 | tf_op jit(solution)/shard_map/leading_inverse/pallas_call | solution.py:202
  144.4 3.6 %share_solve.1 = f32[288,512]{1,0:T(8,128)} custom-call(s32[4]{0:T(128)} %and_select_fusion.1.order_ref, f32[288,128]{1,0:T(8,128)} %copy-done, f32[288,128]{1,0:T(8,128)} %copy-done.1, f32[288,128]{1,0:T(8,128)} %copy-done.2, f32[288,128]{1,0:T(8,128)} %copy-done.3, bf16[4,128,512]{2,1,0:T(8,128)(2,1)} %get-tuple-element.18.high_ref, ...), custom_call_target="tpu_custom_call" | custom-call | tf_op jit(solution)/shard_map/share_solve/pallas_call | solution.py:332
  148.0 1.0 collective-permute-start.5
  149.0 1.1 collective-permute-start.4
  150.1 0.7 pad_add_fusion.info_ref
  150.8 12.0 %collective-permute-done.5.x2 = f32[1152,128]{1,0:T(8,128)S(1)} collective-permute-done((f32[1152,128]{1,0:T(8,128)S(1)}, f32[1152,128]{1,0:T(8,128)S(1)}, u32[]{:S(2)}, u32[]{:S(2)}) %collective-permute-start.5) | collective-permute-done | bytes 589856 | tf_op jit(solution)/shard_map/ppermute | solution.py:462
  162.9 1.8 collective-permute-start.7
  165.1 16.8 %rest.1.base_ref = f32[20736,128]{1,0:T(8,128)} custom-call(s32[64]{0:T(128)} %convert_element_type.9.slot_ref, f32[32,264,128]{2,1,0:T(8,128)} %all-to-all-done.got_ref, f32[20736,128]{1,0:T(8,128)} %bitcast.18), custom_call_target="tpu_custom_call" | custom-call | flops 10000000000 | bytes 26000000 | tf_op jit(solution)/shard_map/rest/pallas_call | solution.py:295
  181.9 0.9 pad_maximum_fusion.x3
  182.8 7.4 %rows_solve.1 = (bf16[1152,1536]{1,0:T(8,128)(2,1)}, f32[1152,128]{1,0:T(8,128)}) custom-call(s32[6]{0:T(128)} %pad_add_fusion.info_ref, f32[1152,128]{1,0:T(8,128)} %get-tuple-element.20.x0, f32[1152,128]{1,0:T(8,128)} %copy-done.5, f32[1152,128]{1,0:T(8,128)} %copy-done.4, f32[1152,128]{1,0:T(8,128)} %pad_maximum_fusion.x3, ...), custom_call_target="tpu_custom_call" | custom-call | flops 4000000000 | bytes 8000000 | tf_op jit(solution)/shard_map/rows_solve/pallas_call | solution.py:370
  190.2 16.3 %update.1 = f32[20736,128]{1,0:T(8,128)} custom-call(f32[8,288,512]{2,1,0:T(8,128)} %bitcast.13, bf16[1152,1536]{1,0:T(8,128)(2,1)} %get-tuple-element.21.lhs_ref, f32[1152,128]{1,0:T(8,128)} %get-tuple-element.22.own_ref, f32[20736,128]{1,0:T(8,128)} %rest.1.base_ref), custom_call_target="tpu_custom_call" | custom-call | tf_op jit(solution)/shard_map/update/pallas_call | solution.py:413
  (34 shorter events, 1.9 us)
Async XLA Ops:
  14.6 83.4 %all-to-all-start = ((f32[32,264,128]{2,1,0:T(8,128)}), f32[32,264,128]{2,1,0:T(8,128)}, u32[]{:S(2)}, u32[]{:S(2)}) async-start(f32[32,264,128]{2,1,0:T(8,128)} %route.1), calls=%async_computation | async-start | bytes 8650752 | tf_op jit(solution)/shard_map/all_to_all | solution.py:439
  23.1 72.5 %all-gather.5.cloned.1.call-start = ((), (), s32[]{:S(2)}) async-start(), calls=%async_computation.1 | async-start | bytes 2162688 | tf_op jit(solution)/shard_map/all_gather | solution.py:441
  24.7 165.6 %all-gather.7.cloned.1.call-start = ((), (), s32[]{:S(2)}) async-start(), calls=%async_computation.2 | async-start | bytes 5308416 | tf_op jit(solution)/shard_map/all_gather | solution.py:456
  105.0 38.5 %collective-permute-start = (f32[288,128]{1,0:T(8,128)}, f32[288,128]{1,0:T(8,128)S(1)}, u32[]{:S(2)}, u32[]{:S(2)}) collective-permute-start(f32[288,128]{1,0:T(8,128)} %get-tuple-element.14), channel_id=1, source_target_pairs={{0,0},{1,4},{2,8},{3,12},{4,1},{5,5},{6,9},{7,13},{8,2},{9,6},{10,... | collective-permute-start | bytes 442376 | tf_op jit(solution)/shard_map/ppermute | solution.py:453
  106.6 36.9 %collective-permute-start.1 = (f32[288,128]{1,0:T(8,128)}, f32[288,128]{1,0:T(8,128)S(1)}, u32[]{:S(2)}, u32[]{:S(2)}) collective-permute-start(f32[288,128]{1,0:T(8,128)} %get-tuple-element.15), channel_id=1, source_target_pairs={{0,4},{1,8},{2,12},{3,0},{4,5},{5,9},{6,13},{7,1},{8,6},{9,10},{10... | collective-permute-start | bytes 442376 | tf_op jit(solution)/shard_map/ppermute | solution.py:453
  108.4 35.2 %collective-permute-start.2 = (f32[288,128]{1,0:T(8,128)}, f32[288,128]{1,0:T(8,128)S(1)}, u32[]{:S(2)}, u32[]{:S(2)}) collective-permute-start(f32[288,128]{1,0:T(8,128)} %get-tuple-element.16), channel_id=1, source_target_pairs={{0,8},{1,12},{2,0},{3,4},{4,9},{5,13},{6,1},{7,5},{8,10},{9,14},{1... | collective-permute-start | bytes 442376 | tf_op jit(solution)/shard_map/ppermute | solution.py:453
  111.3 32.2 %collective-permute-start.3 = (f32[288,128]{1,0:T(8,128)}, f32[288,128]{1,0:T(8,128)S(1)}, u32[]{:S(2)}, u32[]{:S(2)}) collective-permute-start(f32[288,128]{1,0:T(8,128)} %get-tuple-element.17), channel_id=1, source_target_pairs={{0,12},{1,0},{2,4},{3,8},{4,13},{5,1},{6,5},{7,9},{8,14},{9,2},{10... | collective-permute-start | bytes 442376 | tf_op jit(solution)/shard_map/ppermute | solution.py:453
  113.1 34.9 %copy-start.6 = (f32[1152,128]{1,0:T(8,128)S(1)}, f32[1152,128]{1,0:T(8,128)}, u32[]{:S(2)}) copy-start(f32[1152,128]{1,0:T(8,128)} %get-tuple-element.20.x0) | copy-start | bytes 1769476
  113.1 37.0 %copy-start.7 = (s32[4]{0:T(128)S(1)}, s32[4]{0:T(128)}, u32[]{:S(2)}) copy-start(s32[4]{0:T(128)} %constant.31.clone) | copy-start | bytes 52
  143.5 0.7 copy-start
  143.6 0.7 copy-start.1
  143.6 0.7 copy-start.2
  143.6 0.8 copy-start.3
  148.0 14.8 %collective-permute-start.5 = (f32[1152,128]{1,0:T(8,128)S(1)}, f32[1152,128]{1,0:T(8,128)S(1)}, u32[]{:S(2)}, u32[]{:S(2)}) collective-permute-start(f32[1152,128]{1,0:T(8,128)S(1)} %copy-done.6), channel_id=1, source_target_pairs={{0,3},{1,0},{2,1},{3,2},{4,7},{5,4},{6,5},{7,6},{8,11},{9,8},{10,9... | collective-permute-start | bytes 1769480 | tf_op jit(solution)/shard_map/ppermute | solution.py:462
  149.0 15.7 %collective-permute-start.4 = (f32[1152,128]{1,0:T(8,128)S(1)}, f32[1152,128]{1,0:T(8,128)S(1)}, u32[]{:S(2)}, u32[]{:S(2)}) collective-permute-start(f32[1152,128]{1,0:T(8,128)S(1)} %copy-done.6), channel_id=1, source_target_pairs={{0,1},{1,2},{2,3},{3,0},{4,5},{5,6},{6,7},{7,4},{8,9},{9,10},{10,1... | collective-permute-start | bytes 1769480 | tf_op jit(solution)/shard_map/ppermute | solution.py:461
  162.8 19.1 %copy-start.4 = (f32[1152,128]{1,0:T(8,128)}, f32[1152,128]{1,0:T(8,128)S(1)}, u32[]{:S(2)}) copy-start(f32[1152,128]{1,0:T(8,128)S(1)} %collective-permute-done.5.x2) | copy-start | bytes 1769476
  162.9 19.0 %collective-permute-start.7 = (f32[576,128]{1,0:T(8,128)S(1)}, f32[576,128]{1,0:T(8,128)S(1)}, u32[]{:S(2)}, u32[]{:S(2)}) collective-permute-start(f32[576,128]{1,0:T(8,128)S(1)} %slice.34), channel_id=1, source_target_pairs={{0,3},{1,0},{2,1},{3,2},{4,7},{5,4},{6,5},{7,6},{8,11},{9,8},{10,9... | collective-permute-start | bytes 884744 | tf_op jit(solution)/shard_map/ppermute | solution.py:464
  164.7 17.2 %copy-start.5 = (f32[1152,128]{1,0:T(8,128)}, f32[1152,128]{1,0:T(8,128)S(1)}, u32[]{:S(2)}) copy-start(f32[1152,128]{1,0:T(8,128)S(1)} %collective-permute-done.4.x1) | copy-start | bytes 1769476
  164.7 17.2 %collective-permute-start.6 = (f32[576,128]{1,0:T(8,128)S(1)}, f32[576,128]{1,0:T(8,128)S(1)}, u32[]{:S(2)}, u32[]{:S(2)}) collective-permute-start(f32[576,128]{1,0:T(8,128)S(1)} %slice.33), channel_id=1, source_target_pairs={{0,1},{1,2},{2,3},{3,0},{4,5},{5,6},{6,7},{7,4},{8,9},{9,10},{10,1... | collective-permute-start | bytes 884744 | tf_op jit(solution)/shard_map/ppermute | solution.py:463
Sparse Core Ops, SparseCore 0:
  26.2 69.3 all-gather.4
  148.1 32.9 all-gather.6

commit v3 on v2

--- a/solution.py
+++ b/solution.py
@@ -165,9 +165,14 @@
 def leading_kernel(lead_ref, high_ref, low_ref, s_ref, e_ref, w_ref):
     n = 4
     dot = functools.partial(lax.dot_general, precision=HIGHEST, preferred_element_type=F32)
+
+
+    def tile(i, j):
+        return jnp.concatenate([lead_ref[4 * i + j], lead_ref[4 * (i + 4) + j]], axis=0)
+
     for i in range(n):
         for j in range(i + 1):
-            s_ref[i, j] = 0.5 * (lead_ref[i, j] + lead_ref[j, i].T)
+            s_ref[i, j] = 0.5 * (tile(i, j) + tile(j, i).T)
     e_ref[...] = jnp.zeros_like(e_ref)
 
     def step(k, _):
@@ -215,7 +220,7 @@
     )(lead)
 
 
-def panel_kernel(tile_cols, slot_total, slot_ref, col_ref, got_ref, base_ref, out_ref, p0, p1, p2, p3, held, sem):
+def panel_kernel(tile_cols, slot_total, slot_ref, col_ref, got_ref, base_ref, after_ref, out_ref, p0, p1, p2, p3, held, sem):
     total = slot_ref.shape[0]
 
     def wanted(n):
@@ -233,7 +238,7 @@
 
         return 0
 
-    lax.fori_loop(0, total, fetch, 0)
+    lax.fori_loop(0, total, fetch, 0, unroll=8)
     out_ref[...] = base_ref[...]
 
     def add(n, _):
@@ -245,7 +250,7 @@
 
         return 0
 
-    lax.fori_loop(0, total, add, 0)
+    lax.fori_loop(0, total, add, 0, unroll=8)
     quarter = T // 4
     for m, piece in enumerate((p0, p1, p2, p3)):
         first = lax.rem(col_ref[0] + m, 4) * quarter
@@ -253,7 +258,7 @@
             piece[a * quarter : (a + 1) * quarter, :] = out_ref[pl.ds(pl.multiple_of(a * T + first, quarter), quarter), :]
 
 
-def panel(slots, col, got, base, tile_cols, slot_total):
+def panel(slots, col, got, base, after, tile_cols, slot_total):
     rows = base.shape[0]
     total = slots.shape[0]
     return pl.pallas_call(
@@ -262,49 +267,13 @@
         grid_spec=pltpu.PrefetchScalarGridSpec(
             num_scalar_prefetch=2,
             grid=(),
-            in_specs=[ANY(), VM()],
+            in_specs=[ANY(), VM(), ANY()],
             out_specs=(VM(),) * 5,
             scratch_shapes=[pltpu.VMEM((total, T, T), F32), pltpu.SemaphoreType.DMA((total,))],
         ),
         compiler_params=params(),
         name="panel",
-    )(slots, col, got, base)
-
-
-def rest_kernel(tile_cols, slot_total, slot_ref, got_ref, base_ref, out_ref):
-    a = pl.program_id(0)
-    out_ref[...] = base_ref[...]
-
-    def step(n, _):
-        slot = slot_ref[n]
-        b = slot - a * tile_cols
-
-        @pl.when((b > 0) & (b < tile_cols))
-        def _():
-            at = pl.ds(b, T, stride=tile_cols)
-            out_ref[at, :] = out_ref[at, :] + got_ref[n // 2, pl.ds(pl.multiple_of(n % 2 * T, T), T), :]
-
-        return 0
-
-    lax.fori_loop(0, slot_ref.shape[0], step, 0)
-
-
-def rest(slots, got, base, tile_rows, tile_cols):
-    size = T * tile_cols
-    block = pl.BlockSpec((size, T), lambda a, s: (a, 0))
-    return pl.pallas_call(
-        functools.partial(rest_kernel, tile_cols, tile_rows * tile_cols),
-        out_shape=jax.ShapeDtypeStruct(base.shape, F32),
-        grid_spec=pltpu.PrefetchScalarGridSpec(
-            num_scalar_prefetch=1,
-            grid=(tile_rows,),
-            in_specs=[pl.BlockSpec(got.shape, lambda a, s: (0, 0, 0)), block],
-            out_specs=block,
-        ),
-        compiler_params=params(),
-        cost_estimate=pl.CostEstimate(flops=10_000_000_000, bytes_accessed=26_000_000, transcendentals=0),
-        name="rest",
-    )(slots, got, base)
+    )(slots, col, got, base, after)
 
 
 def load_rhs(order_ref, high_ref, low_ref, rhs_ref):
@@ -361,15 +330,14 @@
             total = jnp.where((row < T) & (zero_first == 1), 0.0, total)
         high, low = split(total)
         lhs_ref[at, 0:512] = high
-        lhs_ref[at, 512:1024] = high
-        lhs_ref[at, 1024:1536] = low
+        lhs_ref[at, 512:1024] = low
 
 
 def rows_solve(info, parts, wt):
     rows = parts[0].shape[0]
     return pl.pallas_call(
         rows_kernel,
-        out_shape=(jax.ShapeDtypeStruct((rows, 12 * T), BF16), jax.ShapeDtypeStruct((rows, T), F32)),
+        out_shape=(jax.ShapeDtypeStruct((rows, 8 * T), BF16), jax.ShapeDtypeStruct((rows, T), F32)),
         grid_spec=pltpu.PrefetchScalarGridSpec(
             num_scalar_prefetch=1,
             grid=(),
@@ -383,48 +351,122 @@
     )(info, *parts, *wt)
 
 
-def update_kernel(tile_cols, group, g_ref, lhs_ref, own_ref, base_ref, out_ref, rhs_ref):
-    pairs = tile_cols // 2
+def load_columns(k, pieces, rhs_ref):
+    for d, arrays in enumerate(pieces):
+        quarter = pl.multiple_of((k ^ d) * 32, 32)
+        for first, ref in arrays:
+            for q in range(ref.shape[0] // 32):
+                high, low = split(ref[32 * q : 32 * q + 32, :])
+                at = pl.ds((first + q) * T + quarter, 32)
+                rhs_ref[at, 0:512] = high
+                rhs_ref[at, 512:1024] = low
+
+
+def subtract(h, tile_cols, lhs_ref, rhs_ref, from_ref, out_ref):
+    tiles = tile_cols // 2
+    both = lhs_ref[...]
+    lhs = jnp.concatenate([both[:, 0:512], both], axis=1)
+    for q in range(0, tiles, 2):
+        width = min(2, tiles - q)
+        rhs = rhs_ref[q * T : (q + width) * T, :]
+        rhs = jnp.concatenate([rhs, rhs[:, 0:512]], axis=1)
+        u = lax.dot_general(lhs, rhs, NT, preferred_element_type=F32)
+        for a in range(lhs.shape[0] // T):
+            for w in range(width):
+                at = pl.ds(a * T * tile_cols + 2 * (q + w) + h, T, stride=tile_cols)
+                out_ref[at, :] = from_ref[at, :] - u[a * T : (a + 1) * T, w * T : (w + 1) * T]
+
+
+def first_kernel(tile_cols, group, slot_ref, row_ref, x0, x1, x2, x3, lhs_ref, got_ref, base_ref, out_ref, rhs_ref):
+    i = pl.program_id(0)
+    h, k = row_ref[0] // 4, row_ref[0] % 4
+
+    @pl.when(i == 0)
+    def _():
+        load_columns(k, [[(0, x)] for x in (x0, x1, x2, x3)], rhs_ref)
+
+    out_ref[...] = base_ref[...]
+    low = i * group * tile_cols
+
+    def step(n, _):
+        slot = slot_ref[n] - low
+
+        @pl.when((slot >= 0) & (slot < group * tile_cols))
+        def _():
+            at = pl.ds(slot // tile_cols * (T * tile_cols) + slot % tile_cols, T, stride=tile_cols)
+            out_ref[at, :] = out_ref[at, :] + got_ref[n // 2, pl.ds(pl.multiple_of(n % 2 * T, T), T), :]
+
+        return 0
+
+    lax.fori_loop(0, slot_ref.shape[0], step, 0, unroll=4)
+    subtract(h, tile_cols, lhs_ref, rhs_ref, out_ref, out_ref)
+
+
+def first_half(slots, row, pieces, lhs, got, base, tile_rows, tile_cols):
+    group = 3
+    size = group * T * tile_cols
+    block = pl.BlockSpec((size, T), lambda a, *_: (a, 0))
+    piece = pl.BlockSpec(pieces[0].shape, lambda a, *_: (0, 0))
+    return pl.pallas_call(
+        functools.partial(first_kernel, tile_cols, group),
+        out_shape=jax.ShapeDtypeStruct(base.shape, F32),
+        grid_spec=pltpu.PrefetchScalarGridSpec(
+            num_scalar_prefetch=2,
+            grid=(tile_rows // group,),
+            in_specs=[piece] * 4
+            + [
+                pl.BlockSpec((group * T, 8 * T), lambda a, *_: (a, 0)),
+                pl.BlockSpec(got.shape, lambda a, *_: (0, 0, 0)),
+                block,
+            ],
+            out_specs=block,
+            scratch_shapes=[pltpu.VMEM((tile_cols // 2 * T, 8 * T), BF16)],
+        ),
+        compiler_params=params(),
+        cost_estimate=pl.CostEstimate(flops=12_000_000_000, bytes_accessed=30_000_000, transcendentals=0),
+        name="first_half",
+    )(slots, row, *pieces, lhs, got, base)
+
+
+def second_kernel(tile_cols, group, row_ref, f0, f1, g0, g1, x2, x3, lhs_ref, own_ref, base_ref, out_ref, rhs_ref):
+    h, k = 1 - row_ref[0] // 4, row_ref[0] % 4
+    top = f0.shape[0] // 32
 
     @pl.when(pl.program_id(0) == 0)
     def _():
-        for q in range(pairs):
-            x = g_ref[:, 32 * q : 32 * q + 32, :].reshape(2 * T, 4 * T)
-            high, low = split(x)
-            rhs_ref[q, :, 0:512] = high
-            rhs_ref[q, :, 512:1024] = low
-            rhs_ref[q, :, 1024:1536] = high
-
-    for q in range(pairs):
-        u = lax.dot_general(lhs_ref[...], rhs_ref[q], NT, preferred_element_type=F32)
-        for a in range(group):
-            for b in (2 * q, 2 * q + 1):
-                at = pl.ds(a * T * tile_cols + b, T, stride=tile_cols)
-                if b == 0:
-                    out_ref[at, :] = own_ref[a * T : (a + 1) * T, :]
-                else:
-                    h = b - 2 * q
-                    out_ref[at, :] = base_ref[at, :] - u[a * T : (a + 1) * T, h * T : (h + 1) * T]
-
-
-def update(gathered, lhs, own, base, tile_rows, tile_cols):
+        load_columns(k, [[(0, f0), (top, f1)], [(0, g0), (top, g1)], [(0, x2)], [(0, x3)]], rhs_ref)
+
+    for a in range(group):
+        for q in range(tile_cols // 2):
+            at = pl.ds(a * T * tile_cols + 2 * q + 1 - h, T, stride=tile_cols)
+            out_ref[at, :] = base_ref[at, :]
+    subtract(h, tile_cols, lhs_ref, rhs_ref, base_ref, out_ref)
+    for a in range(group):
+        out_ref[pl.ds(a * T * tile_cols, T, stride=tile_cols), :] = own_ref[a * T : (a + 1) * T, :]
+
+
+def second_half(row, pieces, lhs, own, base, tile_rows, tile_cols):
     group = 3
     size = group * T * tile_cols
-    return pl.pallas_call(
-        functools.partial(update_kernel, tile_cols, group),
+    block = pl.BlockSpec((size, T), lambda a, *_: (a, 0))
+    return pl.pallas_call(
+        functools.partial(second_kernel, tile_cols, group),
         out_shape=jax.ShapeDtypeStruct(base.shape, F32),
-        grid=(tile_rows // group,),
-        in_specs=[
-            pl.BlockSpec(gathered.shape, lambda a: (0, 0, 0)),
-            pl.BlockSpec((group * T, 12 * T), lambda a: (a, 0)),
-            pl.BlockSpec((group * T, T), lambda a: (a, 0)),
-            pl.BlockSpec((size, T), lambda a: (a, 0)),
-        ],
-        out_specs=pl.BlockSpec((size, T), lambda a: (a, 0)),
-        scratch_shapes=[pltpu.VMEM((tile_cols // 2, 2 * T, 12 * T), BF16)],
-        compiler_params=params(),
-        name="update",
-    )(gathered, lhs, own, base)
+        grid_spec=pltpu.PrefetchScalarGridSpec(
+            num_scalar_prefetch=1,
+            grid=(tile_rows // group,),
+            in_specs=[pl.BlockSpec(x.shape, lambda a, *_: (0, 0)) for x in pieces]
+            + [
+                pl.BlockSpec((group * T, 8 * T), lambda a, *_: (a, 0)),
+                pl.BlockSpec((group * T, T), lambda a, *_: (a, 0)),
+                block,
+            ],
+            out_specs=block,
+            scratch_shapes=[pltpu.VMEM((tile_cols // 2 * T, 8 * T), BF16)],
+        ),
+        compiler_params=params(),
+        name="second_half",
+    )(row, *pieces, lhs, own, base)
 
 
 def local(front, child_updates, child_owner, child_rows, child_cols, child_slot):
@@ -438,12 +480,15 @@
     send = route(child_owner[0, :, 0], child_slot[0], child_updates[0], child_rows[0], child_cols[0], 32, slot_total)
     got = lax.all_to_all(send, ("row", "col"), split_axis=0, concat_axis=0, tiled=True)
 
-    lead = lax.all_gather(base_panel[:T], ("row", "col"), axis=0)
-    lead = lead.reshape(8, 4, T, T)[:4]
+    tile = base_panel[:T]
+    lower = lax.ppermute(tile[T // 2 :], "row", [(r, r + 4) for r in range(4)])
+    half = jnp.where(my_row < 4, tile[: T // 2], lower)
+    half = jnp.broadcast_to(half[None], (32, T // 2, T))
+    lead = lax.all_to_all(half, ("row", "col"), split_axis=0, concat_axis=0, tiled=True)
     wt = leading_inverse(lead)
 
     slots = got[:, 2 * T : 2 * T + 2, 0].astype(jnp.int32).reshape(64)
-    columns, *pieces = panel(slots, my_col.reshape(1), got, base_panel, tile_cols, slot_total)
+    columns, *pieces = panel(slots, my_col.reshape(1), got, base_panel, wt[1], tile_cols, slot_total)
 
     parts = []
     for m in range(4):
@@ -453,7 +498,17 @@
         parts.append(lax.ppermute(pieces[m], ("row", "col"), moves))
     order = (my_row - jnp.arange(4, dtype=jnp.int32)) % 4
     share = share_solve(order, parts, wt)
-    gathered = lax.all_gather(share, "row", axis=0)
+
+    def swap(x, bits):
+        return lax.ppermute(x, "row", [(r, r ^ bits) for r in range(8)])
+
+    cut = 5 * T // 4
+    near, far_side = swap(share, 2), swap(share, 6)
+    beside = swap(share, 1)
+    near_beside = swap(near, 1)
+    opposite = [swap(far_side[:cut], 2), swap(near[cut:], 6)]
+    far_beside = swap(far_side, 1)
+    opposite_beside = [swap(x, 1) for x in opposite]
 
     right = [(i, (i + 1) % 4) for i in range(4)]
     left = [(i, (i - 1) % 4) for i in range(4)]
@@ -470,8 +525,10 @@
         ]
     )
     lhs, own = rows_solve(info, (columns, from_left, from_right, far), wt)
-    base = rest(slots, got, flat, tile_rows, tile_cols)
-    result = update(gathered, lhs, own, base, tile_rows, tile_cols)
+    row = my_row.reshape(1)
+    base = first_half(slots, row, (share, beside, near, near_beside), lhs, got, flat, tile_rows, tile_cols)
+    others = (*opposite, *opposite_beside, far_side, far_beside)
+    result = second_half(row, others, lhs, own, base, tile_rows, tile_cols)
     return result.reshape(front.shape)
 
 

time: 215 us -> 193 us (0.90)
  waiting for transfers between devices: 80.5 us -> 55.6 us
  starting transfers between devices: 20.9 us -> 39 us
  between operations: 13.5 us -> 0.2 us
  Pallas kernels: 87.5 us -> 83.9 us
    all_gather x2 -> x0, waiting for transfers between devices: 68.4 us -> none  [the longest x1 68.4 us: local(): lead = lax.all_gather(base_panel[:T], ('row', 'col'), axis=0)]
    all_to_all x1, waiting for transfers between devices: 0.01 us -> 22.8 us  [local(): lax.all_to_all(send, ('row', 'col'), split_axis=0, concat_axis=0, tiled=T...]
    ppermute x0 -> x10, waiting for transfers between devices: none -> 13.5 us  [the longest x9 11.9 us: swap(): return lax.ppermute(x, 'row', [(r, r ^ bits) for r in range(8)])]
    ppermute x4, waiting for transfers between devices: 0.01 us -> 12.2 us  [local(): parts.append(lax.ppermute(pieces[m], ('row', 'col'), moves))]
    ppermute x1, waiting for transfers between devices: 12 us -> 0.01 us  [local(): from_right = lax.ppermute(columns, 'col', left)]
    all_to_all x0 -> x1, starting transfers between devices: none -> 8.96 us  [local(): lax.all_to_all(half, ('row', 'col'), split_axis=0, concat_axis=0, tiled=T...]
    ppermute x0 -> x10, starting transfers between devices: none -> 8.64 us  [the longest x1 5.17 us: local(): lower = lax.ppermute(tile[T // 2:], 'row', [(r, r + 4) for r in range(4)])]
    all_to_all x0 -> x1, waiting for transfers between devices: none -> 7.17 us  [local(): lax.all_to_all(half, ('row', 'col'), split_axis=0, concat_axis=0, tiled=T...]
  transfers between devices with their start and end apart: 11 -> 20, of which waited for: 2 -> 8; matrix products, arithmetic and copies ran while one was open for 4% -> 3% of each run, Pallas kernels for 26% -> 34%
where the time goes in v3:
time: 193 us; the launch traced here: 190 us
  Pallas kernels  83.9 us (43%)
  waiting for transfers between devices  55.6 us (29%)
  starting transfers between devices  39 us (20%)
  local copies, waits for them, and re-layouts  8.18 us (4%)
  other arithmetic  3.58 us (2%)
    pallas_call x1, Pallas kernels, leading_inverse(): pl.pallas_call(leading_kernel, out_shape=(jax.ShapeDtypeStruct((4, T, 4 *...  30.4 us
    all_to_all x1, waiting for transfers between devices, local(): lax.all_to_all(send, ('row', 'col'), split_axis=0, concat_axis=0, tiled=T...  22.8 us
    pallas_call x1, Pallas kernels, first_half(): pl.pallas_call(functools.partial(first_kernel, tile_cols, group), out_sha...  16.1 us
    pallas_call x1, Pallas kernels, second_half(): pl.pallas_call(functools.partial(second_kernel, tile_cols, group), out_sh...  13.9 us
    ppermute x4, waiting for transfers between devices, local(): parts.append(lax.ppermute(pieces[m], ('row', 'col'), moves))  12.2 us
    ppermute x9, waiting for transfers between devices, swap(): return lax.ppermute(x, 'row', [(r, r ^ bits) for r in range(8)])  11.9 us
    ppermute x4, starting transfers between devices, local(): parts.append(lax.ppermute(pieces[m], ('row', 'col'), moves))  10.6 us
    all_to_all x1, starting transfers between devices, local(): lax.all_to_all(half, ('row', 'col'), split_axis=0, concat_axis=0, tiled=T...  8.96 us
  transfers between devices with their start and end apart: 20, of which 8 were waited for; matrix products, arithmetic and copies ran while one was open for 3% of the time, Pallas kernels for 34%

profile of v3, /device:TPU:0, one launch (start us, length us, event | category | flops | bytes accessed | tf_op | source)
XLA Modules:
  0.0 190.5 jit_solution(8924883662934739363)
XLA Ops:
  0.8 5.2 %collective-permute-start = (f32[64,128]{1,0:T(8,128)S(1)}, f32[64,128]{1,0:T(8,128)S(1)}, u32[]{:S(2)}, u32[]{:S(2)}) collective-permute-start(f32[64,128]{1,0:T(8,128)S(1)} %bitcast.19), channel_id=1, source_target_pairs={{0,16},{4,20},{8,24},{12,28},{1,17},{5,21},{9,25},{13,29},{2,18},{... | collective-permute-start | bytes 98312 | tf_op jit(solution)/shard_map/ppermute | solution.py:484
  6.0 1.6 collective-permute-done
  8.6 9.0 %all-to-all-start.1 = ((f32[32,64,128]{2,1,0:T(8,128)}), f32[32,64,128]{2,1,0:T(8,128)S(1)}, u32[]{:S(2)}, u32[]{:S(2)}) async-start(f32[32,64,128]{2,1,0:T(8,128)} %broadcast_in_dim.2), calls=%async_computation.1 | async-start | bytes 2097152 | tf_op jit(solution)/shard_map/all_to_all | solution.py:487
  17.6 1.9 %slice.36 = f32[1,9,1,128,1,1,128]{6,5,4,3,2,1,0:T(1,128)} slice(f32[1,9,1,128,18,1,128]{6,5,4,3,2,1,0:T(1,128)} %param.7), slice={[0:1], [0:9], [0:1], [0:128], [0:1], [0:1], [0:128]} | slice | bytes 1179648 | tf_op jit(solution)/shard_map/slice | solution.py:478
  19.5 8.0 %route.1 = f32[32,264,128]{2,1,0:T(8,128)} custom-call(s32[32]{0:T(128)} %bitcast.22, s32[32]{0:T(128)} %bitcast.23, f32[32,128,128]{2,1,0:T(8,128)} %bitcast.16, s32[32,128]{1,0:T(8,128)} %bitcast.20, s32[32,128]{1,0:T(8,128)} %bitcast.21), custom_call_target="tpu_custom_call" | custom-call | tf_op jit(solution)/shard_map/route/pallas_call | solution.py:93
  27.6 7.2 %all-to-all-done.1.lead_ref = f32[32,64,128]{2,1,0:T(8,128)S(1)} async-done(((f32[32,64,128]{2,1,0:T(8,128)}), f32[32,64,128]{2,1,0:T(8,128)S(1)}, u32[]{:S(2)}, u32[]{:S(2)}) %all-to-all-start.1) | async-done | bytes 1048608 | tf_op jit(solution)/shard_map/all_to_all | solution.py:487
  35.7 4.8 %all-to-all-start = ((f32[32,264,128]{2,1,0:T(8,128)}), f32[32,264,128]{2,1,0:T(8,128)}, u32[]{:S(2)}, u32[]{:S(2)}) async-start(f32[32,264,128]{2,1,0:T(8,128)} %route.1), calls=%async_computation | async-start | bytes 8650752 | tf_op jit(solution)/shard_map/all_to_all | solution.py:481
  40.6 30.4 %leading_inverse.1 = (bf16[4,128,512]{2,1,0:T(8,128)(2,1)}, bf16[4,128,512]{2,1,0:T(8,128)(2,1)}) custom-call(f32[32,64,128]{2,1,0:T(8,128)} %copy-done.1), custom_call_target="tpu_custom_call" | custom-call | flops 60000002048 | bytes 2000000 | tf_op jit(solution)/shard_map/leading_inverse/pallas_call | solution.py:207
  70.9 22.8 %all-to-all-done.got_ref = f32[32,264,128]{2,1,0:T(8,128)} async-done(((f32[32,264,128]{2,1,0:T(8,128)}), f32[32,264,128]{2,1,0:T(8,128)}, u32[]{:S(2)}, u32[]{:S(2)}) %all-to-all-start) | async-done | bytes 4325408 | tf_op jit(solution)/shard_map/all_to_all | solution.py:481
  93.7 1.5 fusion
  95.9 5.0 %panel.1 = (f32[1152,128]{1,0:T(8,128)}, f32[288,128]{1,0:T(8,128)}, f32[288,128]{1,0:T(8,128)}, f32[288,128]{1,0:T(8,128)}, f32[288,128]{1,0:T(8,128)}) custom-call(s32[64]{0:T(128)} %convert_element_type.9.slot_ref, s32[1]{0:T(128)} %bitcast.6.col_ref, f32[32,264,128]{2,1,0:T(8,128)} %all-to-all-done.got_ref, f32[1152,128]{1,0:T(8,128)} %bitcast.15, ...), custom_call_target="tpu_custom_call" | custom-call | tf_op jit(solution)/shard_map/panel/pallas_call | solution.py:264
  100.9 3.7 %collective-permute-start.13 = (f32[1152,128]{1,0:T(8,128)}, f32[1152,128]{1,0:T(8,128)S(1)}, u32[]{:S(2)}, u32[]{:S(2)}) collective-permute-start(f32[1152,128]{1,0:T(8,128)} %get-tuple-element.20.x0), channel_id=1, source_target_pairs={{0,3},{1,0},{2,1},{3,2},{4,7},{5,4},{6,5},{7,6},{8,11},{9,8},{10,9... | collective-permute-start | bytes 1769480 | tf_op jit(solution)/shard_map/ppermute | solution.py:517
  104.5 1.6 collective-permute-start.1
  106.1 3.5 %collective-permute-start.3 = (f32[288,128]{1,0:T(8,128)}, f32[288,128]{1,0:T(8,128)S(1)}, u32[]{:S(2)}, u32[]{:S(2)}) collective-permute-start(f32[288,128]{1,0:T(8,128)} %get-tuple-element.17), channel_id=1, source_target_pairs={{0,8},{1,12},{2,0},{3,4},{4,9},{5,13},{6,1},{7,5},{8,10},{9,14},{1... | collective-permute-start | bytes 442376 | tf_op jit(solution)/shard_map/ppermute | solution.py:498
  109.6 5.5 %collective-permute-start.4 = (f32[288,128]{1,0:T(8,128)}, f32[288,128]{1,0:T(8,128)S(1)}, u32[]{:S(2)}, u32[]{:S(2)}) collective-permute-start(f32[288,128]{1,0:T(8,128)} %get-tuple-element.18), channel_id=1, source_target_pairs={{0,12},{1,0},{2,4},{3,8},{4,13},{5,1},{6,5},{7,9},{8,14},{9,2},{10... | collective-permute-start | bytes 442376 | tf_op jit(solution)/shard_map/ppermute | solution.py:498
  115.7 8.2 %collective-permute-done.2.x1 = f32[288,128]{1,0:T(8,128)S(1)} collective-permute-done((f32[288,128]{1,0:T(8,128)}, f32[288,128]{1,0:T(8,128)S(1)}, u32[]{:S(2)}, u32[]{:S(2)}) %collective-permute-start.2) | collective-permute-done | bytes 147488 | tf_op jit(solution)/shard_map/ppermute | solution.py:498
  123.9 4.0 %collective-permute-done.4.x3 = f32[288,128]{1,0:T(8,128)S(1)} collective-permute-done((f32[288,128]{1,0:T(8,128)}, f32[288,128]{1,0:T(8,128)S(1)}, u32[]{:S(2)}, u32[]{:S(2)}) %collective-permute-start.4) | collective-permute-done | bytes 147488 | tf_op jit(solution)/shard_map/ppermute | solution.py:498
  128.5 3.6 %share_solve.1.x0 = f32[288,512]{1,0:T(8,128)} custom-call(s32[4]{0:T(128)} %and_select_fusion.1.order_ref, f32[288,128]{1,0:T(8,128)} %copy-done.7, f32[288,128]{1,0:T(8,128)} %copy-done.8, f32[288,128]{1,0:T(8,128)} %copy-done.9, f32[288,128]{1,0:T(8,128)} %copy-done.10, bf16[4,128,512]{2,1,0:T(8,128)(2,1)} %get-tuple-element.19.high_ref, ...), custom_call_target="tpu_custom_call" | custom-call | tf_op jit(solution)/shard_map/share_solve/pallas_call | solution.py:301
  133.6 1.8 collective-permute-start.14
  136.0 1.1 collective-permute-start.16
  137.1 11.2 %collective-permute-done.7.x2 = f32[288,512]{1,0:T(8,128)} collective-permute-done((f32[288,512]{1,0:T(8,128)}, f32[288,512]{1,0:T(8,128)}, u32[]{:S(2)}, u32[]{:S(2)}) %collective-permute-start.7) | collective-permute-done | bytes 589856 | tf_op jit(solution)/shard_map/ppermute | solution.py:503
  151.7 6.8 %rows_solve.1 = (bf16[1152,1024]{1,0:T(8,128)(2,1)}, f32[1152,128]{1,0:T(8,128)}) custom-call(s32[6]{0:T(128)} %pad_add_fusion.info_ref, f32[1152,128]{1,0:T(8,128)} %get-tuple-element.20.x0, f32[1152,128]{1,0:T(8,128)} %copy-done.12, f32[1152,128]{1,0:T(8,128)} %copy-done.11, f32[1152,128]{1,0:T(8,128)} %pad_maximum_fusion.x3, ...), custom_call_target="tpu_custom_call" | custom-call | flops 4000000000 | bytes 8000000 | tf_op jit(solution)/shard_map/rows_solve/pallas_call | solution.py:338
  159.3 16.1 %first_half.1.base_ref = f32[20736,128]{1,0:T(8,128)} custom-call(s32[64]{0:T(128)} %convert_element_type.9.slot_ref, s32[1]{0:T(128)} %bitcast.row_ref, f32[288,512]{1,0:T(8,128)} %share_solve.1.x0, f32[288,512]{1,0:T(8,128)} %collective-permute-done.16.x1, f32[288,512]{1,0:T(8,128)} %collective-permute-done.7.x2, f32[288,512]{1,0:T(8,128)} %collective-permute-done.17.x3, ...), custom_call_target="tpu_custom_call" | custom-call | flops 12000000000 | bytes 30000000 | tf_op jit(solution)/shard_map/first_half/pallas_call | solution.py:410
  176.5 13.9 %second_half.1 = f32[20736,128]{1,0:T(8,128)} custom-call(s32[1]{0:T(128)} %bitcast.row_ref, f32[160,512]{1,0:T(8,128)} %copy-done.3, f32[128,512]{1,0:T(8,128)} %copy-done.5, f32[160,512]{1,0:T(8,128)} %copy-done.4, f32[128,512]{1,0:T(8,128)} %copy-done.6, f32[288,512]{1,0:T(8,128)} %copy-done, f32[288,512]{1,0:T(8,128)} %copy-done.2, ...), custom_call_target="tpu_custom_call" | custom-call | tf_op jit(solution)/shard_map/second_half/pallas_call | solution.py:452
  (65 shorter events, 12.0 us)
Async XLA Ops:
  0.8 6.8 %collective-permute-start = (f32[64,128]{1,0:T(8,128)S(1)}, f32[64,128]{1,0:T(8,128)S(1)}, u32[]{:S(2)}, u32[]{:S(2)}) collective-permute-start(f32[64,128]{1,0:T(8,128)S(1)} %bitcast.19), channel_id=1, source_target_pairs={{0,16},{4,20},{8,24},{12,28},{1,17},{5,21},{9,25},{13,29},{2,18},{... | collective-permute-start | bytes 98312 | tf_op jit(solution)/shard_map/ppermute | solution.py:484
  8.6 26.1 %all-to-all-start.1 = ((f32[32,64,128]{2,1,0:T(8,128)}), f32[32,64,128]{2,1,0:T(8,128)S(1)}, u32[]{:S(2)}, u32[]{:S(2)}) async-start(f32[32,64,128]{2,1,0:T(8,128)} %broadcast_in_dim.2), calls=%async_computation.1 | async-start | bytes 2097152 | tf_op jit(solution)/shard_map/all_to_all | solution.py:487
  35.7 58.0 %all-to-all-start = ((f32[32,264,128]{2,1,0:T(8,128)}), f32[32,264,128]{2,1,0:T(8,128)}, u32[]{:S(2)}, u32[]{:S(2)}) async-start(f32[32,264,128]{2,1,0:T(8,128)} %route.1), calls=%async_computation | async-start | bytes 8650752 | tf_op jit(solution)/shard_map/all_to_all | solution.py:481
  95.9 39.5 %copy-start.13 = (s32[4]{0:T(128)S(1)}, s32[4]{0:T(128)}, u32[]{:S(2)}) copy-start(s32[4]{0:T(128)} %constant.31.clone) | copy-start | bytes 52
  100.9 32.1 %collective-permute-start.13 = (f32[1152,128]{1,0:T(8,128)}, f32[1152,128]{1,0:T(8,128)S(1)}, u32[]{:S(2)}, u32[]{:S(2)}) collective-permute-start(f32[1152,128]{1,0:T(8,128)} %get-tuple-element.20.x0), channel_id=1, source_target_pairs={{0,3},{1,0},{2,1},{3,2},{4,7},{5,4},{6,5},{7,6},{8,11},{9,8},{10,9... | collective-permute-start | bytes 1769480 | tf_op jit(solution)/shard_map/ppermute | solution.py:517
  104.5 29.1 %collective-permute-start.12 = (f32[1152,128]{1,0:T(8,128)}, f32[1152,128]{1,0:T(8,128)S(1)}, u32[]{:S(2)}, u32[]{:S(2)}) collective-permute-start(f32[1152,128]{1,0:T(8,128)} %get-tuple-element.20.x0), channel_id=1, source_target_pairs={{0,1},{1,2},{2,3},{3,0},{4,5},{5,6},{6,7},{7,4},{8,9},{9,10},{10,1... | collective-permute-start | bytes 1769480 | tf_op jit(solution)/shard_map/ppermute | solution.py:516
  104.5 5.1 %collective-permute-start.1 = (f32[288,128]{1,0:T(8,128)}, f32[288,128]{1,0:T(8,128)S(1)}, u32[]{:S(2)}, u32[]{:S(2)}) collective-permute-start(f32[288,128]{1,0:T(8,128)} %get-tuple-element.15), channel_id=1, source_target_pairs={{0,0},{1,4},{2,8},{3,12},{4,1},{5,5},{6,9},{7,13},{8,2},{9,6},{10,... | collective-permute-start | bytes 442376 | tf_op jit(solution)/shard_map/ppermute | solution.py:498
  106.1 17.7 %collective-permute-start.2 = (f32[288,128]{1,0:T(8,128)}, f32[288,128]{1,0:T(8,128)S(1)}, u32[]{:S(2)}, u32[]{:S(2)}) collective-permute-start(f32[288,128]{1,0:T(8,128)} %get-tuple-element.16), channel_id=1, source_target_pairs={{0,4},{1,8},{2,12},{3,0},{4,5},{5,9},{6,13},{7,1},{8,6},{9,10},{10... | collective-permute-start | bytes 442376 | tf_op jit(solution)/shard_map/ppermute | solution.py:498
  106.1 17.8 %collective-permute-start.3 = (f32[288,128]{1,0:T(8,128)}, f32[288,128]{1,0:T(8,128)S(1)}, u32[]{:S(2)}, u32[]{:S(2)}) collective-permute-start(f32[288,128]{1,0:T(8,128)} %get-tuple-element.17), channel_id=1, source_target_pairs={{0,8},{1,12},{2,0},{3,4},{4,9},{5,13},{6,1},{7,5},{8,10},{9,14},{1... | collective-permute-start | bytes 442376 | tf_op jit(solution)/shard_map/ppermute | solution.py:498
  109.6 18.3 %copy-start.7 = (f32[288,128]{1,0:T(8,128)}, f32[288,128]{1,0:T(8,128)S(1)}, u32[]{:S(2)}) copy-start(f32[288,128]{1,0:T(8,128)S(1)} %collective-permute-done.1.x0) | copy-start | bytes 442372
  109.6 18.2 %collective-permute-start.4 = (f32[288,128]{1,0:T(8,128)}, f32[288,128]{1,0:T(8,128)S(1)}, u32[]{:S(2)}, u32[]{:S(2)}) collective-permute-start(f32[288,128]{1,0:T(8,128)} %get-tuple-element.18), channel_id=1, source_target_pairs={{0,12},{1,0},{2,4},{3,8},{4,13},{5,1},{6,5},{7,9},{8,14},{9,2},{10... | collective-permute-start | bytes 442376 | tf_op jit(solution)/shard_map/ppermute | solution.py:498
  132.1 16.2 %collective-permute-start.7 = (f32[288,512]{1,0:T(8,128)}, f32[288,512]{1,0:T(8,128)}, u32[]{:S(2)}, u32[]{:S(2)}) collective-permute-start(f32[288,512]{1,0:T(8,128)} %share_solve.1.x0), channel_id=1, source_target_pairs={{0,8},{4,12},{8,0},{12,4},{16,24},{20,28},{24,16},{28,20},{1,9},{5... | collective-permute-start | bytes 1769480 | tf_op jit(solution)/shard_map/ppermute | solution.py:503
  132.1 18.0 %collective-permute-start.5 = (f32[288,512]{1,0:T(8,128)}, f32[288,512]{1,0:T(8,128)S(1)}, u32[]{:S(2)}, u32[]{:S(2)}) collective-permute-start(f32[288,512]{1,0:T(8,128)} %share_solve.1.x0), channel_id=1, source_target_pairs={{0,24},{4,28},{8,16},{12,20},{16,8},{20,12},{24,0},{28,4},{1,25},{... | collective-permute-start | bytes 1769480 | tf_op jit(solution)/shard_map/ppermute | solution.py:503
  133.0 18.7 %copy-start.11 = (f32[1152,128]{1,0:T(8,128)}, f32[1152,128]{1,0:T(8,128)S(1)}, u32[]{:S(2)}) copy-start(f32[1152,128]{1,0:T(8,128)S(1)} %collective-permute-done.13.x2) | copy-start | bytes 1769476
  133.0 17.2 %collective-permute-start.15 = (f32[576,128]{1,0:T(8,128)S(1)}, f32[576,128]{1,0:T(8,128)S(1)}, u32[]{:S(2)}, u32[]{:S(2)}) collective-permute-start(f32[576,128]{1,0:T(8,128)S(1)} %slice.49), channel_id=1, source_target_pairs={{0,3},{1,0},{2,1},{3,2},{4,7},{5,4},{6,5},{7,6},{8,11},{9,8},{10,9... | collective-permute-start | bytes 884744 | tf_op jit(solution)/shard_map/ppermute | solution.py:519
  133.6 18.1 %copy-start.12 = (f32[1152,128]{1,0:T(8,128)}, f32[1152,128]{1,0:T(8,128)S(1)}, u32[]{:S(2)}) copy-start(f32[1152,128]{1,0:T(8,128)S(1)} %collective-permute-done.12.x1) | copy-start | bytes 1769476
  133.6 16.7 %collective-permute-start.14 = (f32[576,128]{1,0:T(8,128)S(1)}, f32[576,128]{1,0:T(8,128)S(1)}, u32[]{:S(2)}, u32[]{:S(2)}) collective-permute-start(f32[576,128]{1,0:T(8,128)S(1)} %slice.48), channel_id=1, source_target_pairs={{0,1},{1,2},{2,3},{3,0},{4,5},{5,6},{6,7},{7,4},{8,9},{9,10},{10,1... | collective-permute-start | bytes 884744 | tf_op jit(solution)/shard_map/ppermute | solution.py:518
  136.0 23.3 %collective-permute-start.16 = (f32[288,512]{1,0:T(8,128)}, f32[288,512]{1,0:T(8,128)}, u32[]{:S(2)}, u32[]{:S(2)}) collective-permute-start(f32[288,512]{1,0:T(8,128)} %share_solve.1.x0), channel_id=1, source_target_pairs={{0,4},{4,0},{8,12},{12,8},{16,20},{20,16},{24,28},{28,24},{1,5},{5... | collective-permute-start | bytes 1769480 | tf_op jit(solution)/shard_map/ppermute | solution.py:503
  149.4 9.3 %collective-permute-start.8 = (f32[128,512]{1,0:T(8,128)S(1)}, f32[128,512]{1,0:T(8,128)S(1)}, u32[]{:S(2)}, u32[]{:S(2)}) collective-permute-start(f32[128,512]{1,0:T(8,128)S(1)} %slice.47), channel_id=1, source_target_pairs={{0,24},{4,28},{8,16},{12,20},{16,8},{20,12},{24,0},{28,4},{1,25},{... | collective-permute-start | bytes 786440 | tf_op jit(solution)/shard_map/ppermute | solution.py:503
  150.1 9.1 %collective-permute-start.6 = (f32[160,512]{1,0:T(8,128)S(1)}, f32[160,512]{1,0:T(8,128)S(1)}, u32[]{:S(2)}, u32[]{:S(2)}) collective-permute-start(f32[160,512]{1,0:T(8,128)S(1)} %slice.46), channel_id=1, source_target_pairs={{0,8},{4,12},{8,0},{12,4},{16,24},{20,28},{24,16},{28,20},{1,9},{5... | collective-permute-start | bytes 983048 | tf_op jit(solution)/shard_map/ppermute | solution.py:503
  150.2 9.0 %collective-permute-start.17 = (f32[288,512]{1,0:T(8,128)}, f32[288,512]{1,0:T(8,128)}, u32[]{:S(2)}, u32[]{:S(2)}) collective-permute-start(f32[288,512]{1,0:T(8,128)} %collective-permute-done.7.x2), channel_id=1, source_target_pairs={{0,4},{4,0},{8,12},{12,8},{16,20},{20,16},{24,28},{28,24},{1,5},{5... | collective-permute-start | bytes 1769480 | tf_op jit(solution)/shard_map/ppermute | solution.py:503
  150.4 25.1 %collective-permute-start.11 = (f32[288,512]{1,0:T(8,128)S(1)}, f32[288,512]{1,0:T(8,128)S(1)}, u32[]{:S(2)}, u32[]{:S(2)}) collective-permute-start(f32[288,512]{1,0:T(8,128)S(1)} %collective-permute-done.5.x2), channel_id=1, source_target_pairs={{0,4},{4,0},{8,12},{12,8},{16,20},{20,16},{24,28},{28,24},{1,5},{5... | collective-permute-start | bytes 1769480 | tf_op jit(solution)/shard_map/ppermute | solution.py:503
  158.7 16.8 %collective-permute-start.10 = (f32[128,512]{1,0:T(8,128)S(1)}, f32[128,512]{1,0:T(8,128)S(1)}, u32[]{:S(2)}, u32[]{:S(2)}) collective-permute-start(f32[128,512]{1,0:T(8,128)S(1)} %collective-permute-done.8.f1), channel_id=1, source_target_pairs={{0,4},{4,0},{8,12},{12,8},{16,20},{20,16},{24,28},{28,24},{1,5},{5... | collective-permute-start | bytes 786440 | tf_op jit(solution)/shard_map/ppermute | solution.py:503
  159.3 16.2 %collective-permute-start.9 = (f32[160,512]{1,0:T(8,128)S(1)}, f32[160,512]{1,0:T(8,128)S(1)}, u32[]{:S(2)}, u32[]{:S(2)}) collective-permute-start(f32[160,512]{1,0:T(8,128)S(1)} %collective-permute-done.6.f0), channel_id=1, source_target_pairs={{0,4},{4,0},{8,12},{12,8},{16,20},{20,16},{24,28},{28,24},{1,5},{5... | collective-permute-start | bytes 983048 | tf_op jit(solution)/shard_map/ppermute | solution.py:503
  (10 other events, 53.7 us)

commit v4 on v3

--- a/solution.py
+++ b/solution.py
@@ -15,11 +15,10 @@
 NN = (((1,), (0,)), ((), ()))
 VM = functools.partial(pl.BlockSpec, memory_space=pltpu.VMEM)
 ANY = functools.partial(pl.BlockSpec, memory_space=pl.ANY)
-LIMIT = 60 * 1024 * 1024
-
-
-def params():
-    return pltpu.CompilerParams(vmem_limit_bytes=LIMIT)
+
+
+def params(mebibytes=60):
+    return pltpu.CompilerParams(vmem_limit_bytes=mebibytes * 1024 * 1024)
 
 
 def split(x):
@@ -105,7 +104,7 @@
                 pltpu.SemaphoreType.DMA((count + 1,)),
             ],
         ),
-        compiler_params=params(),
+        compiler_params=params(16),
         name="route",
     )(owner, slot, blocks, rows, cols)
 
@@ -162,13 +161,15 @@
             e[g] = e[g] - tree_sum([below[g][k] * x[k] for k in range(8)])
 
 
-def leading_kernel(lead_ref, high_ref, low_ref, s_ref, e_ref, w_ref):
+def leading_kernel(core_ref, mine_ref, other_ref, high_ref, low_ref, s_ref, e_ref, w_ref):
     n = 4
     dot = functools.partial(lax.dot_general, precision=HIGHEST, preferred_element_type=F32)
 
 
     def tile(i, j):
-        return jnp.concatenate([lead_ref[4 * i + j], lead_ref[4 * (i + 4) + j]], axis=0)
+        mine, other = mine_ref[4 * i + j], other_ref[4 * i + j]
+        first = core_ref[0] == 0
+        return jnp.concatenate([jnp.where(first, mine, other), jnp.where(first, other, mine)], axis=0)
 
     for i in range(n):
         for j in range(i + 1):
@@ -203,21 +204,25 @@
     lax.fori_loop(0, n, step, 0)
 
 
-def leading_inverse(lead):
+def leading_inverse(core, mine, other):
     return pl.pallas_call(
         leading_kernel,
         out_shape=(jax.ShapeDtypeStruct((4, T, 4 * T), BF16),) * 2,
-        in_specs=[VM()],
-        out_specs=(VM(), VM()),
-        scratch_shapes=[
-            pltpu.VMEM((4, 4, T, T), F32),
-            pltpu.VMEM((4, T, 4 * T), F32),
-            pltpu.VMEM((T, T), F32),
-        ],
-        compiler_params=params(),
+        grid_spec=pltpu.PrefetchScalarGridSpec(
+            num_scalar_prefetch=1,
+            grid=(),
+            in_specs=[VM(), VM()],
+            out_specs=(VM(), VM()),
+            scratch_shapes=[
+                pltpu.VMEM((4, 4, T, T), F32),
+                pltpu.VMEM((4, T, 4 * T), F32),
+                pltpu.VMEM((T, T), F32),
+            ],
+        ),
+        compiler_params=params(16),
         cost_estimate=pl.CostEstimate(flops=60_000_000_000, bytes_accessed=2_000_000, transcendentals=0),
         name="leading_inverse",
-    )(lead)
+    )(core, mine, other)
 
 
 def panel_kernel(tile_cols, slot_total, slot_ref, col_ref, got_ref, base_ref, after_ref, out_ref, p0, p1, p2, p3, held, sem):
@@ -271,7 +276,7 @@
             out_specs=(VM(),) * 5,
             scratch_shapes=[pltpu.VMEM((total, T, T), F32), pltpu.SemaphoreType.DMA((total,))],
         ),
-        compiler_params=params(),
+        compiler_params=params(16),
         name="panel",
     )(slots, col, got, base, after)
 
@@ -292,25 +297,25 @@
     )
 
 
-def share_kernel(order_ref, x0, x1, x2, x3, high_ref, low_ref, out_ref, rhs_ref):
+def share_kernel(order_ref, x0, x1, x2, x3, high_ref, low_ref, after_ref, out_ref, rhs_ref):
     load_rhs(order_ref, high_ref, low_ref, rhs_ref)
     out_ref[...] = times_wt([x[...] for x in (x0, x1, x2, x3)], rhs_ref)
 
 
-def share_solve(order, parts, wt):
+def share_solve(order, parts, wt, after):
     return pl.pallas_call(
         share_kernel,
         out_shape=jax.ShapeDtypeStruct((parts[0].shape[0], 4 * T), F32),
         grid_spec=pltpu.PrefetchScalarGridSpec(
             num_scalar_prefetch=1,
             grid=(),
-            in_specs=[VM()] * 6,
+            in_specs=[VM()] * 6 + [ANY()],
             out_specs=VM(),
             scratch_shapes=[pltpu.VMEM((12 * T, 4 * T), BF16)],
         ),
-        compiler_params=params(),
+        compiler_params=params(16),
         name="share_solve",
-    )(order, *parts, *wt)
+    )(order, *parts, *wt, after)
 
 
 def rows_kernel(info_ref, x0, x1, x2, x3, high_ref, low_ref, lhs_ref, own_ref, rhs_ref):
@@ -345,51 +350,18 @@
             out_specs=(VM(), VM()),
             scratch_shapes=[pltpu.VMEM((12 * T, 4 * T), BF16)],
         ),
-        compiler_params=params(),
+        compiler_params=params(28),
         cost_estimate=pl.CostEstimate(flops=4_000_000_000, bytes_accessed=8_000_000, transcendentals=0),
         name="rows_solve",
     )(info, *parts, *wt)
 
 
-def load_columns(k, pieces, rhs_ref):
-    for d, arrays in enumerate(pieces):
-        quarter = pl.multiple_of((k ^ d) * 32, 32)
-        for first, ref in arrays:
-            for q in range(ref.shape[0] // 32):
-                high, low = split(ref[32 * q : 32 * q + 32, :])
-                at = pl.ds((first + q) * T + quarter, 32)
-                rhs_ref[at, 0:512] = high
-                rhs_ref[at, 512:1024] = low
-
-
-def subtract(h, tile_cols, lhs_ref, rhs_ref, from_ref, out_ref):
-    tiles = tile_cols // 2
-    both = lhs_ref[...]
-    lhs = jnp.concatenate([both[:, 0:512], both], axis=1)
-    for q in range(0, tiles, 2):
-        width = min(2, tiles - q)
-        rhs = rhs_ref[q * T : (q + width) * T, :]
-        rhs = jnp.concatenate([rhs, rhs[:, 0:512]], axis=1)
-        u = lax.dot_general(lhs, rhs, NT, preferred_element_type=F32)
-        for a in range(lhs.shape[0] // T):
-            for w in range(width):
-                at = pl.ds(a * T * tile_cols + 2 * (q + w) + h, T, stride=tile_cols)
-                out_ref[at, :] = from_ref[at, :] - u[a * T : (a + 1) * T, w * T : (w + 1) * T]
-
-
-def first_kernel(tile_cols, group, slot_ref, row_ref, x0, x1, x2, x3, lhs_ref, got_ref, base_ref, out_ref, rhs_ref):
-    i = pl.program_id(0)
-    h, k = row_ref[0] // 4, row_ref[0] % 4
-
-    @pl.when(i == 0)
-    def _():
-        load_columns(k, [[(0, x)] for x in (x0, x1, x2, x3)], rhs_ref)
-
+def rest_kernel(tile_cols, group, slot_ref, got_ref, base_ref, out_ref):
     out_ref[...] = base_ref[...]
-    low = i * group * tile_cols
+    first = pl.program_id(0) * group * tile_cols
 
     def step(n, _):
-        slot = slot_ref[n] - low
+        slot = slot_ref[n] - first
 
         @pl.when((slot >= 0) & (slot < group * tile_cols))
         def _():
@@ -399,58 +371,68 @@
         return 0
 
     lax.fori_loop(0, slot_ref.shape[0], step, 0, unroll=4)
-    subtract(h, tile_cols, lhs_ref, rhs_ref, out_ref, out_ref)
-
-
-def first_half(slots, row, pieces, lhs, got, base, tile_rows, tile_cols):
+
+
+def rest(slots, got, base, tile_rows, tile_cols):
+    group = 3
+    size = group * T * tile_cols
+    block = pl.BlockSpec((size, T), lambda a, s: (a, 0))
+    return pl.pallas_call(
+        functools.partial(rest_kernel, tile_cols, group),
+        out_shape=jax.ShapeDtypeStruct(base.shape, F32),
+        grid_spec=pltpu.PrefetchScalarGridSpec(
+            num_scalar_prefetch=1,
+            grid=(tile_rows // group,),
+            in_specs=[pl.BlockSpec(got.shape, lambda a, s: (0, 0, 0)), block],
+            out_specs=block,
+        ),
+        compiler_params=params(40),
+        cost_estimate=pl.CostEstimate(flops=10_000_000_000, bytes_accessed=26_000_000, transcendentals=0),
+        name="rest",
+    )(slots, got, base)
+
+
+def load_columns(h, k, pieces, rhs_ref):
+    for d, arrays in enumerate(pieces):
+        quarter = (k ^ d) * 32 + h * T
+        for first, ref in arrays:
+            for q in range(ref.shape[0] // 32):
+                high, low = split(ref[32 * q : 32 * q + 32, :])
+                at = pl.ds(pl.multiple_of((first + q) * 2 * T + quarter, 32), 32)
+                rhs_ref[at, 0:512] = high
+                rhs_ref[at, 512:1024] = low
+
+
+def update_kernel(tile_cols, group, row_ref, s0, s1, s2, s3, f0, f1, g0, g1, t2, t3, lhs_ref, own_ref, base_ref, out_ref, rhs_ref):
+    h, k = row_ref[0] // 4, row_ref[0] % 4
+    top = f0.shape[0] // 32
+
+    @pl.when(pl.program_id(0) == 0)
+    def _():
+        load_columns(h, k, [[(0, x)] for x in (s0, s1, s2, s3)], rhs_ref)
+        load_columns(1 - h, k, [[(0, f0), (top, f1)], [(0, g0), (top, g1)], [(0, t2)], [(0, t3)]], rhs_ref)
+
+    both = lhs_ref[...]
+    lhs = jnp.concatenate([both[:, 0:512], both], axis=1)
+    for q in range(0, tile_cols, 2):
+        rhs = rhs_ref[q * T : (q + 2) * T, :]
+        rhs = jnp.concatenate([rhs, rhs[:, 0:512]], axis=1)
+        u = lax.dot_general(lhs, rhs, NT, preferred_element_type=F32)
+        for a in range(group):
+            for b in (q, q + 1):
+                at = pl.ds(a * T * tile_cols + b, T, stride=tile_cols)
+                if b == 0:
+                    out_ref[at, :] = own_ref[a * T : (a + 1) * T, :]
+                else:
+                    out_ref[at, :] = base_ref[at, :] - u[a * T : (a + 1) * T, (b - q) * T : (b - q + 1) * T]
+
+
+def update(row, pieces, lhs, own, base, tile_rows, tile_cols):
     group = 3
     size = group * T * tile_cols
     block = pl.BlockSpec((size, T), lambda a, *_: (a, 0))
-    piece = pl.BlockSpec(pieces[0].shape, lambda a, *_: (0, 0))
-    return pl.pallas_call(
-        functools.partial(first_kernel, tile_cols, group),
-        out_shape=jax.ShapeDtypeStruct(base.shape, F32),
-        grid_spec=pltpu.PrefetchScalarGridSpec(
-            num_scalar_prefetch=2,
-            grid=(tile_rows // group,),
-            in_specs=[piece] * 4
-            + [
-                pl.BlockSpec((group * T, 8 * T), lambda a, *_: (a, 0)),
-                pl.BlockSpec(got.shape, lambda a, *_: (0, 0, 0)),
-                block,
-            ],
-            out_specs=block,
-            scratch_shapes=[pltpu.VMEM((tile_cols // 2 * T, 8 * T), BF16)],
-        ),
-        compiler_params=params(),
-        cost_estimate=pl.CostEstimate(flops=12_000_000_000, bytes_accessed=30_000_000, transcendentals=0),
-        name="first_half",
-    )(slots, row, *pieces, lhs, got, base)
-
-
-def second_kernel(tile_cols, group, row_ref, f0, f1, g0, g1, x2, x3, lhs_ref, own_ref, base_ref, out_ref, rhs_ref):
-    h, k = 1 - row_ref[0] // 4, row_ref[0] % 4
-    top = f0.shape[0] // 32
-
-    @pl.when(pl.program_id(0) == 0)
-    def _():
-        load_columns(k, [[(0, f0), (top, f1)], [(0, g0), (top, g1)], [(0, x2)], [(0, x3)]], rhs_ref)
-
-    for a in range(group):
-        for q in range(tile_cols // 2):
-            at = pl.ds(a * T * tile_cols + 2 * q + 1 - h, T, stride=tile_cols)
-            out_ref[at, :] = base_ref[at, :]
-    subtract(h, tile_cols, lhs_ref, rhs_ref, base_ref, out_ref)
-    for a in range(group):
-        out_ref[pl.ds(a * T * tile_cols, T, stride=tile_cols), :] = own_ref[a * T : (a + 1) * T, :]
-
-
-def second_half(row, pieces, lhs, own, base, tile_rows, tile_cols):
-    group = 3
-    size = group * T * tile_cols
-    block = pl.BlockSpec((size, T), lambda a, *_: (a, 0))
-    return pl.pallas_call(
-        functools.partial(second_kernel, tile_cols, group),
+    return pl.pallas_call(
+        functools.partial(update_kernel, tile_cols, group),
         out_shape=jax.ShapeDtypeStruct(base.shape, F32),
         grid_spec=pltpu.PrefetchScalarGridSpec(
             num_scalar_prefetch=1,
@@ -462,10 +444,10 @@
                 block,
             ],
             out_specs=block,
-            scratch_shapes=[pltpu.VMEM((tile_cols // 2 * T, 8 * T), BF16)],
-        ),
-        compiler_params=params(),
-        name="second_half",
+            scratch_shapes=[pltpu.VMEM((tile_cols * T, 8 * T), BF16)],
+        ),
+        compiler_params=params(44),
+        name="update",
     )(row, *pieces, lhs, own, base)
 
 
@@ -478,14 +460,14 @@
     base_panel = front[0, :, 0, :, 0, 0, :].reshape(tile_rows * T, T)
 
     send = route(child_owner[0, :, 0], child_slot[0], child_updates[0], child_rows[0], child_cols[0], 32, slot_total)
+
+    tile = base_panel[:T].reshape(1, 2, 1, T // 2, T)
+    halves = jnp.broadcast_to(tile, (4, 2, 4, T // 2, T)).reshape(32, T // 2, T)
+    mine = lax.all_to_all(halves, ("row", "col"), split_axis=0, concat_axis=0, tiled=True)[:16]
+    mine, send = lax.optimization_barrier((mine, send))
+    other = lax.ppermute(mine, "row", [(r, r ^ 1) for r in range(8)])
     got = lax.all_to_all(send, ("row", "col"), split_axis=0, concat_axis=0, tiled=True)
-
-    tile = base_panel[:T]
-    lower = lax.ppermute(tile[T // 2 :], "row", [(r, r + 4) for r in range(4)])
-    half = jnp.where(my_row < 4, tile[: T // 2], lower)
-    half = jnp.broadcast_to(half[None], (32, T // 2, T))
-    lead = lax.all_to_all(half, ("row", "col"), split_axis=0, concat_axis=0, tiled=True)
-    wt = leading_inverse(lead)
+    wt = leading_inverse((my_row % 2).reshape(1), mine, other)
 
     slots = got[:, 2 * T : 2 * T + 2, 0].astype(jnp.int32).reshape(64)
     columns, *pieces = panel(slots, my_col.reshape(1), got, base_panel, wt[1], tile_cols, slot_total)
@@ -497,7 +479,8 @@
         ]
         parts.append(lax.ppermute(pieces[m], ("row", "col"), moves))
     order = (my_row - jnp.arange(4, dtype=jnp.int32)) % 4
-    share = share_solve(order, parts, wt)
+    base = rest(slots, got, flat, tile_rows, tile_cols)
+    share = share_solve(order, parts, wt, base)
 
     def swap(x, bits):
         return lax.ppermute(x, "row", [(r, r ^ bits) for r in range(8)])
@@ -510,6 +493,7 @@
     far_beside = swap(far_side, 1)
     opposite_beside = [swap(x, 1) for x in opposite]
 
+    columns, base, *_ = lax.optimization_barrier((columns, base, *parts))
     right = [(i, (i + 1) % 4) for i in range(4)]
     left = [(i, (i - 1) % 4) for i in range(4)]
     half = tile_rows * T // 2
@@ -526,9 +510,8 @@
     )
     lhs, own = rows_solve(info, (columns, from_left, from_right, far), wt)
     row = my_row.reshape(1)
-    base = first_half(slots, row, (share, beside, near, near_beside), lhs, got, flat, tile_rows, tile_cols)
-    others = (*opposite, *opposite_beside, far_side, far_beside)
-    result = second_half(row, others, lhs, own, base, tile_rows, tile_cols)
+    pieces = (share, beside, near, near_beside, *opposite, *opposite_beside, far_side, far_beside)
+    result = update(row, pieces, lhs, own, base, tile_rows, tile_cols)
     return result.reshape(front.shape)
 
 

time: 193 us -> 167 us (0.87)
  Pallas kernels: 83.9 us -> 71.5 us
  waiting for transfers between devices: 55.6 us -> 45.5 us
  starting transfers between devices: 39 us -> 33.5 us
  local copies, waits for them, and re-layouts: 8.18 us -> 13.2 us
  other arithmetic: 3.58 us -> 1.65 us
    ppermute x4, waiting for transfers between devices: 12.2 us -> 0.01 us  [local(): parts.append(lax.ppermute(pieces[m], ('row', 'col'), moves))]
    unnamed x28 -> x16, local copies, waits for them, and re-layouts: 2.66 us -> 8.81 us
    ppermute x1, starting transfers between devices: 5.17 us -> 0.09 us  [local(): other = lax.ppermute(mine, 'row', [(r, r ^ 1) for r in range(8)])]
    pallas_call x2, Pallas kernels: 30.1 us -> 26.1 us  [the longest x1 13.6 us: update(): pl.pallas_call(functools.partial(update_kernel, tile_cols, group), out_sh...]
    ppermute x4, starting transfers between devices: 10.6 us -> 7.41 us  [local(): parts.append(lax.ppermute(pieces[m], ('row', 'col'), moves))]
    ppermute x1, waiting for transfers between devices: 0.01 us -> 2.77 us  [local(): far_top = lax.ppermute(from_left[:half], 'col', right)]
    pallas_call x1, Pallas kernels: 3.62 us -> 1.16 us  [share_solve(): pl.pallas_call(share_kernel, out_shape=jax.ShapeDtypeStruct((parts[0].sha...]
    ppermute x1, starting transfers between devices: 0.56 us -> 2.89 us  [local(): far_bottom = lax.ppermute(from_right[half:], 'col', left)]
  transfers between devices with their start and end apart: 20 -> 20, of which waited for: 8 -> 5; matrix products, arithmetic and copies ran while one was open for 3% -> 1% of each run, Pallas kernels for 34% -> 32%
where the time goes in v4:
time: 167 us; the launch traced here: 166 us
  Pallas kernels  71.5 us (43%)
  waiting for transfers between devices  45.5 us (27%)
  starting transfers between devices  33.5 us (20%)
  local copies, waits for them, and re-layouts  13.2 us (8%)
    pallas_call x1, Pallas kernels, leading_inverse(): pl.pallas_call(leading_kernel, out_shape=(jax.ShapeDtypeStruct((4, T, 4 *...  28.2 us
    all_to_all x1, waiting for transfers between devices, local(): lax.all_to_all(send, ('row', 'col'), split_axis=0, concat_axis=0, tiled=T...  24.9 us
    pallas_call x1, Pallas kernels, update(): pl.pallas_call(functools.partial(update_kernel, tile_cols, group), out_sh...  13.6 us
    ppermute x9, waiting for transfers between devices, swap(): return lax.ppermute(x, 'row', [(r, r ^ bits) for r in range(8)])  12.9 us
    pallas_call x1, Pallas kernels, rest(): pl.pallas_call(functools.partial(rest_kernel, tile_cols, group), out_shap...  12.6 us
    unnamed x16, local copies, waits for them, and re-layouts  8.81 us
    all_to_all x1, starting transfers between devices, local(): lax.all_to_all(halves, ('row', 'col'), split_axis=0, concat_axis=0, tiled...  8.42 us
    ppermute x4, starting transfers between devices, local(): parts.append(lax.ppermute(pieces[m], ('row', 'col'), moves))  7.41 us
  transfers between devices with their start and end apart: 20, of which 5 were waited for; matrix products, arithmetic and copies ran while one was open for 1% of the time, Pallas kernels for 32%

profile of v4, /device:TPU:0, one launch (start us, length us, event | category | flops | bytes accessed | tf_op | source)
XLA Modules:
  0.0 165.6 jit_solution(11568055266126351355)
XLA Ops:
  2.1 8.4 %all-to-all-start = ((f32[32,64,128]{2,1,0:T(8,128)}), f32[32,64,128]{2,1,0:T(8,128)S(1)}, u32[]{:S(2)}, u32[]{:S(2)}) async-start(f32[32,64,128]{2,1,0:T(8,128)} %bitcast.2), calls=%async_computation | async-start | bytes 2097152 | tf_op jit(solution)/shard_map/all_to_all | solution.py:466
  13.3 7.3 %route.1 = f32[32,264,128]{2,1,0:T(8,128)S(1)} custom-call(s32[32]{0:T(128)S(1)} %bitcast.18, s32[32]{0:T(128)S(1)} %bitcast.19, f32[32,128,128]{2,1,0:T(8,128)S(1)} %bitcast.15, s32[32,128]{1,0:T(8,128)S(1)} %bitcast.16, s32[32,128]{1,0:T(8,128)S(1)} %bitcast.17), custom_call_target="tpu_custom_call" | custom-call | tf_op jit(solution)/shard_map/route/pallas_call | solution.py:92
  20.7 2.0 %copy-done.1 = f32[32,264,128]{2,1,0:T(8,128)} copy-done((f32[32,264,128]{2,1,0:T(8,128)}, f32[32,264,128]{2,1,0:T(8,128)S(1)}, u32[]{:S(2)}) %copy-start.1) | copy-done | bytes 4325400
  22.7 5.0 %all-to-all-done = f32[32,64,128]{2,1,0:T(8,128)S(1)} async-done(((f32[32,64,128]{2,1,0:T(8,128)}), f32[32,64,128]{2,1,0:T(8,128)S(1)}, u32[]{:S(2)}, u32[]{:S(2)}) %all-to-all-start) | async-done | bytes 1048608 | tf_op jit(solution)/shard_map/all_to_all | solution.py:466
  28.9 4.9 %all-to-all-start.1 = ((f32[32,264,128]{2,1,0:T(8,128)}), f32[32,264,128]{2,1,0:T(8,128)}, u32[]{:S(2)}, u32[]{:S(2)}) async-start(f32[32,264,128]{2,1,0:T(8,128)} %copy-done.1), calls=%async_computation.1 | async-start | bytes 8650752 | tf_op jit(solution)/shard_map/all_to_all | solution.py:469
  33.8 28.2 %leading_inverse.1 = (bf16[4,128,512]{2,1,0:T(8,128)(2,1)S(1)}, bf16[4,128,512]{2,1,0:T(8,128)(2,1)S(1)}) custom-call(s32[1]{0:T(128)} %bitcast.10.core_ref, f32[16,64,128]{2,1,0:T(8,128)S(1)} %slice.34.mine_ref, f32[16,64,128]{2,1,0:T(8,128)S(1)} %collective-permute-done.other_ref), custom_call_target="tpu_custom_call" | custom-call | flops 60000002048 | bytes 2000000 | tf_op jit(solution)/shard_map/leading_inverse/pallas_call | solution.py:208
  62.1 24.9 %all-to-all-done.1.got_ref = f32[32,264,128]{2,1,0:T(8,128)} async-done(((f32[32,264,128]{2,1,0:T(8,128)}), f32[32,264,128]{2,1,0:T(8,128)}, u32[]{:S(2)}, u32[]{:S(2)}) %all-to-all-start.1) | async-done | bytes 4325408 | tf_op jit(solution)/shard_map/all_to_all | solution.py:469
  87.0 1.5 fusion
  88.6 4.0 %panel.1 = (f32[1152,128]{1,0:T(8,128)}, f32[288,128]{1,0:T(8,128)S(1)}, f32[288,128]{1,0:T(8,128)S(1)}, f32[288,128]{1,0:T(8,128)S(1)}, f32[288,128]{1,0:T(8,128)S(1)}) custom-call(s32[64]{0:T(128)S(1)} %convert_element_type.9.slot_ref, s32[1]{0:T(128)} %bitcast.8.col_ref, f32[32,264,128]{2,1,0:T(8,128)} %all-to-all-done.1.got_ref, ...), custom_call_target="tpu_custom_call" | custom-call | tf_op jit(solution)/shard_map/panel/pallas_call | solution.py:269
  93.3 2.3 %collective-permute-start.2 = (f32[288,128]{1,0:T(8,128)S(1)}, f32[288,128]{1,0:T(8,128)S(1)}, u32[]{:S(2)}, u32[]{:S(2)}) collective-permute-start(f32[288,128]{1,0:T(8,128)S(1)} %get-tuple-element.22), channel_id=1, source_target_pairs={{0,4},{1,8},{2,12},{3,0},{4,5},{5,9},{6,13},{7,1},{8,6},{9,10},{10... | collective-permute-start | bytes 442376 | tf_op jit(solution)/shard_map/ppermute | solution.py:480
  95.6 3.2 %collective-permute-start.3 = (f32[288,128]{1,0:T(8,128)S(1)}, f32[288,128]{1,0:T(8,128)S(1)}, u32[]{:S(2)}, u32[]{:S(2)}) collective-permute-start(f32[288,128]{1,0:T(8,128)S(1)} %get-tuple-element.23), channel_id=1, source_target_pairs={{0,8},{1,12},{2,0},{3,4},{4,9},{5,13},{6,1},{7,5},{8,10},{9,14},{1... | collective-permute-start | bytes 442376 | tf_op jit(solution)/shard_map/ppermute | solution.py:480
  98.8 1.2 collective-permute-start.4
  100.0 12.6 %rest.1.after_ref.base_ref = f32[20736,128]{1,0:T(8,128)} custom-call(s32[64]{0:T(128)S(1)} %convert_element_type.9.slot_ref, f32[32,264,128]{2,1,0:T(8,128)} %all-to-all-done.1.got_ref, f32[20736,128]{1,0:T(8,128)} %bitcast.21), custom_call_target="tpu_custom_call" | custom-call | flops 10000000000 | bytes 26000000 | tf_op jit(solution)/shard_map/rest/pallas_call | solution.py:380
  112.6 4.0 %copy-done = f32[20736,128]{1,0:T(8,128)S(1)} copy-done((f32[20736,128]{1,0:T(8,128)S(1)}, f32[20736,128]{1,0:T(8,128)}, u32[]{:S(2)}) %copy-start) | copy-done | bytes 10616856
  116.6 1.2 share_solve.1.s0
  117.8 1.2 collective-permute-start.6
  119.0 4.0 %collective-permute-start.15 = (f32[1152,128]{1,0:T(8,128)}, f32[1152,128]{1,0:T(8,128)S(1)}, u32[]{:S(2)}, u32[]{:S(2)}) collective-permute-start(f32[1152,128]{1,0:T(8,128)} %get-tuple-element.27.x0), channel_id=1, source_target_pairs={{0,3},{1,0},{2,1},{3,2},{4,7},{5,4},{6,5},{7,6},{8,11},{9,8},{10,9... | collective-permute-start | bytes 1769480 | tf_op jit(solution)/shard_map/ppermute | solution.py:501
  123.0 1.8 %collective-permute-start.8 = (f32[288,512]{1,0:T(8,128)S(1)}, f32[288,512]{1,0:T(8,128)S(1)}, u32[]{:S(2)}, u32[]{:S(2)}) collective-permute-start(f32[288,512]{1,0:T(8,128)S(1)} %share_solve.1.s0), channel_id=1, source_target_pairs={{0,24},{4,28},{8,16},{12,20},{16,8},{20,12},{24,0},{28,4},{1,25},{... | collective-permute-start | bytes 1769480 | tf_op jit(solution)/shard_map/ppermute | solution.py:486
  124.8 9.1 %collective-permute-done.6.s2 = f32[288,512]{1,0:T(8,128)S(1)} collective-permute-done((f32[288,512]{1,0:T(8,128)S(1)}, f32[288,512]{1,0:T(8,128)S(1)}, u32[]{:S(2)}, u32[]{:S(2)}) %collective-permute-start.6) | collective-permute-done | bytes 589856 | tf_op jit(solution)/shard_map/ppermute | solution.py:486
  134.9 2.9 %collective-permute-start.17 = (f32[576,128]{1,0:T(8,128)S(1)}, f32[576,128]{1,0:T(8,128)S(1)}, u32[]{:S(2)}, u32[]{:S(2)}) collective-permute-start(f32[576,128]{1,0:T(8,128)S(1)} %slice.39), channel_id=1, source_target_pairs={{0,3},{1,0},{2,1},{3,2},{4,7},{5,4},{6,5},{7,6},{8,11},{9,8},{10,9... | collective-permute-start | bytes 884744 | tf_op jit(solution)/shard_map/ppermute | solution.py:503
  139.7 3.8 %collective-permute-done.10.f1 = f32[128,512]{1,0:T(8,128)S(1)} collective-permute-done((f32[128,512]{1,0:T(8,128)S(1)}, f32[128,512]{1,0:T(8,128)S(1)}, u32[]{:S(2)}, u32[]{:S(2)}) %collective-permute-start.10) | collective-permute-done | bytes 262176 | tf_op jit(solution)/shard_map/ppermute | solution.py:486
  144.0 2.8 %collective-permute-done.16 = f32[576,128]{1,0:T(8,128)S(1)} collective-permute-done((f32[576,128]{1,0:T(8,128)S(1)}, f32[576,128]{1,0:T(8,128)S(1)}, u32[]{:S(2)}, u32[]{:S(2)}) %collective-permute-start.16) | collective-permute-done | bytes 294944 | tf_op jit(solution)/shard_map/ppermute | solution.py:502
  147.4 4.6 %rows_solve.1 = (bf16[1152,1024]{1,0:T(8,128)(2,1)S(1)}, f32[1152,128]{1,0:T(8,128)S(1)}) custom-call(s32[6]{0:T(128)S(1)} %pad_add_fusion.info_ref, f32[1152,128]{1,0:T(8,128)} %get-tuple-element.27.x0, f32[1152,128]{1,0:T(8,128)} %collective-permute-done.14.x1, f32[1152,128]{1,0:T(8,128)S(1)} %collective-permute-done.15.x2, ...), custom_call_target="tpu_custom_call" | custom-call | flops 4000000000 | bytes 8000000 | tf_op jit(solution)/shard_map/rows_solve/pallas_call | solution.py:343
  152.0 13.6 %update.1 = f32[20736,128]{1,0:T(8,128)} custom-call(s32[1]{0:T(128)} %bitcast.row_ref, f32[288,512]{1,0:T(8,128)S(1)} %share_solve.1.s0, f32[288,512]{1,0:T(8,128)S(1)} %collective-permute-done.5.s1, f32[288,512]{1,0:T(8,128)S(1)} %collective-permute-done.6.s2, f32[288,512]{1,0:T(8,128)S(1)} %collective-permute-done.7.s3, ...), custom_call_target="tpu_custom_call" | custom-call | tf_op jit(solution)/shard_map/update/pallas_call | solution.py:434
  (53 shorter events, 10.9 us)
Async XLA Ops:
  0.0 10.5 %copy-start.2 = (f32[1,32,128,128]{3,2,1,0:T(8,128)S(1)}, f32[1,32,128,128]{3,2,1,0:T(8,128)}, u32[]{:S(2)}) copy-start(f32[1,32,128,128]{3,2,1,0:T(8,128)} %param.8) | copy-start | bytes 6291460
  2.1 25.6 %all-to-all-start = ((f32[32,64,128]{2,1,0:T(8,128)}), f32[32,64,128]{2,1,0:T(8,128)S(1)}, u32[]{:S(2)}, u32[]{:S(2)}) async-start(f32[32,64,128]{2,1,0:T(8,128)} %bitcast.2), calls=%async_computation | async-start | bytes 2097152 | tf_op jit(solution)/shard_map/all_to_all | solution.py:466
  20.6 2.1 %copy-start.1 = (f32[32,264,128]{2,1,0:T(8,128)}, f32[32,264,128]{2,1,0:T(8,128)S(1)}, u32[]{:S(2)}) copy-start(f32[32,264,128]{2,1,0:T(8,128)S(1)} %route.1) | copy-start | bytes 12976132
  27.7 6.1 %collective-permute-start = (f32[16,64,128]{2,1,0:T(8,128)S(1)}, f32[16,64,128]{2,1,0:T(8,128)S(1)}, u32[]{:S(2)}, u32[]{:S(2)}) collective-permute-start(f32[16,64,128]{2,1,0:T(8,128)S(1)} %slice.34.mine_ref), channel_id=1, source_target_pairs={{0,4},{4,0},{8,12},{12,8},{16,20},{20,16},{24,28},{28,24},{1,5},{5... | collective-permute-start | bytes 1572872 | tf_op jit(solution)/shard_map/ppermute | solution.py:468
  28.9 58.0 %all-to-all-start.1 = ((f32[32,264,128]{2,1,0:T(8,128)}), f32[32,264,128]{2,1,0:T(8,128)}, u32[]{:S(2)}, u32[]{:S(2)}) async-start(f32[32,264,128]{2,1,0:T(8,128)} %copy-done.1), calls=%async_computation.1 | async-start | bytes 8650752 | tf_op jit(solution)/shard_map/all_to_all | solution.py:469
  92.6 20.0 %collective-permute-start.1 = (f32[288,128]{1,0:T(8,128)S(1)}, f32[288,128]{1,0:T(8,128)S(1)}, u32[]{:S(2)}, u32[]{:S(2)}) collective-permute-start(f32[288,128]{1,0:T(8,128)S(1)} %get-tuple-element.21), channel_id=1, source_target_pairs={{0,0},{1,4},{2,8},{3,12},{4,1},{5,5},{6,9},{7,13},{8,2},{9,6},{10,... | collective-permute-start | bytes 442376 | tf_op jit(solution)/shard_map/ppermute | solution.py:480
  93.3 19.3 %collective-permute-start.2 = (f32[288,128]{1,0:T(8,128)S(1)}, f32[288,128]{1,0:T(8,128)S(1)}, u32[]{:S(2)}, u32[]{:S(2)}) collective-permute-start(f32[288,128]{1,0:T(8,128)S(1)} %get-tuple-element.22), channel_id=1, source_target_pairs={{0,4},{1,8},{2,12},{3,0},{4,5},{5,9},{6,13},{7,1},{8,6},{9,10},{10... | collective-permute-start | bytes 442376 | tf_op jit(solution)/shard_map/ppermute | solution.py:480
  95.6 17.0 %collective-permute-start.3 = (f32[288,128]{1,0:T(8,128)S(1)}, f32[288,128]{1,0:T(8,128)S(1)}, u32[]{:S(2)}, u32[]{:S(2)}) collective-permute-start(f32[288,128]{1,0:T(8,128)S(1)} %get-tuple-element.23), channel_id=1, source_target_pairs={{0,8},{1,12},{2,0},{3,4},{4,9},{5,13},{6,1},{7,5},{8,10},{9,14},{1... | collective-permute-start | bytes 442376 | tf_op jit(solution)/shard_map/ppermute | solution.py:480
  98.8 13.8 %collective-permute-start.4 = (f32[288,128]{1,0:T(8,128)S(1)}, f32[288,128]{1,0:T(8,128)S(1)}, u32[]{:S(2)}, u32[]{:S(2)}) collective-permute-start(f32[288,128]{1,0:T(8,128)S(1)} %get-tuple-element.24), channel_id=1, source_target_pairs={{0,12},{1,0},{2,4},{3,8},{4,13},{5,1},{6,5},{7,9},{8,14},{9,2},{10... | collective-permute-start | bytes 442376 | tf_op jit(solution)/shard_map/ppermute | solution.py:480
  112.6 4.0 %copy-start = (f32[20736,128]{1,0:T(8,128)S(1)}, f32[20736,128]{1,0:T(8,128)}, u32[]{:S(2)}) copy-start(f32[20736,128]{1,0:T(8,128)} %rest.1.after_ref.base_ref) | copy-start | bytes 31850500
  116.6 22.2 %copy-start.7 = (s32[4]{0:T(128)S(1)}, s32[4]{0:T(128)}, u32[]{:S(2)}) copy-start(s32[4]{0:T(128)} %constant.43.clone) | copy-start | bytes 52
  117.8 16.1 %collective-permute-start.6 = (f32[288,512]{1,0:T(8,128)S(1)}, f32[288,512]{1,0:T(8,128)S(1)}, u32[]{:S(2)}, u32[]{:S(2)}) collective-permute-start(f32[288,512]{1,0:T(8,128)S(1)} %share_solve.1.s0), channel_id=1, source_target_pairs={{0,8},{4,12},{8,0},{12,4},{16,24},{20,28},{24,16},{28,20},{1,9},{5... | collective-permute-start | bytes 1769480 | tf_op jit(solution)/shard_map/ppermute | solution.py:486
  119.0 15.8 %collective-permute-start.15 = (f32[1152,128]{1,0:T(8,128)}, f32[1152,128]{1,0:T(8,128)S(1)}, u32[]{:S(2)}, u32[]{:S(2)}) collective-permute-start(f32[1152,128]{1,0:T(8,128)} %get-tuple-element.27.x0), channel_id=1, source_target_pairs={{0,3},{1,0},{2,1},{3,2},{4,7},{5,4},{6,5},{7,6},{8,11},{9,8},{10,9... | collective-permute-start | bytes 1769480 | tf_op jit(solution)/shard_map/ppermute | solution.py:501
  123.0 14.7 %collective-permute-start.14 = (f32[1152,128]{1,0:T(8,128)}, f32[1152,128]{1,0:T(8,128)}, u32[]{:S(2)}, u32[]{:S(2)}) collective-permute-start(f32[1152,128]{1,0:T(8,128)} %get-tuple-element.27.x0), channel_id=1, source_target_pairs={{0,1},{1,2},{2,3},{3,0},{4,5},{5,6},{6,7},{7,4},{8,9},{9,10},{10,1... | collective-permute-start | bytes 1769480 | tf_op jit(solution)/shard_map/ppermute | solution.py:500
  123.0 15.8 %collective-permute-start.8 = (f32[288,512]{1,0:T(8,128)S(1)}, f32[288,512]{1,0:T(8,128)S(1)}, u32[]{:S(2)}, u32[]{:S(2)}) collective-permute-start(f32[288,512]{1,0:T(8,128)S(1)} %share_solve.1.s0), channel_id=1, source_target_pairs={{0,24},{4,28},{8,16},{12,20},{16,8},{20,12},{24,0},{28,4},{1,25},{... | collective-permute-start | bytes 1769480 | tf_op jit(solution)/shard_map/ppermute | solution.py:486
  133.9 9.5 %collective-permute-start.10 = (f32[128,512]{1,0:T(8,128)S(1)}, f32[128,512]{1,0:T(8,128)S(1)}, u32[]{:S(2)}, u32[]{:S(2)}) collective-permute-start(f32[128,512]{1,0:T(8,128)S(1)} %slice.37), channel_id=1, source_target_pairs={{0,24},{4,28},{8,16},{12,20},{16,8},{20,12},{24,0},{28,4},{1,25},{... | collective-permute-start | bytes 786440 | tf_op jit(solution)/shard_map/ppermute | solution.py:486
  134.9 8.6 %collective-permute-start.17 = (f32[576,128]{1,0:T(8,128)S(1)}, f32[576,128]{1,0:T(8,128)S(1)}, u32[]{:S(2)}, u32[]{:S(2)}) collective-permute-start(f32[576,128]{1,0:T(8,128)S(1)} %slice.39), channel_id=1, source_target_pairs={{0,3},{1,0},{2,1},{3,2},{4,7},{5,4},{6,5},{7,6},{8,11},{9,8},{10,9... | collective-permute-start | bytes 884744 | tf_op jit(solution)/shard_map/ppermute | solution.py:503
  138.8 8.0 %collective-permute-start.16 = (f32[576,128]{1,0:T(8,128)S(1)}, f32[576,128]{1,0:T(8,128)S(1)}, u32[]{:S(2)}, u32[]{:S(2)}) collective-permute-start(f32[576,128]{1,0:T(8,128)S(1)} %slice.38), channel_id=1, source_target_pairs={{0,1},{1,2},{2,3},{3,0},{4,5},{5,6},{6,7},{7,4},{8,9},{9,10},{10,1... | collective-permute-start | bytes 884744 | tf_op jit(solution)/shard_map/ppermute | solution.py:502
  138.9 7.9 %collective-permute-start.9 = (f32[160,512]{1,0:T(8,128)S(1)}, f32[160,512]{1,0:T(8,128)S(1)}, u32[]{:S(2)}, u32[]{:S(2)}) collective-permute-start(f32[160,512]{1,0:T(8,128)S(1)} %slice.36), channel_id=1, source_target_pairs={{0,8},{4,12},{8,0},{12,4},{16,24},{20,28},{24,16},{28,20},{1,9},{5... | collective-permute-start | bytes 983048 | tf_op jit(solution)/shard_map/ppermute | solution.py:486
  139.7 12.3 %collective-permute-start.5 = (f32[288,512]{1,0:T(8,128)S(1)}, f32[288,512]{1,0:T(8,128)S(1)}, u32[]{:S(2)}, u32[]{:S(2)}) collective-permute-start(f32[288,512]{1,0:T(8,128)S(1)} %share_solve.1.s0), channel_id=1, source_target_pairs={{0,4},{4,0},{8,12},{12,8},{16,20},{20,16},{24,28},{28,24},{1,5},{5... | collective-permute-start | bytes 1769480 | tf_op jit(solution)/shard_map/ppermute | solution.py:486
  143.5 8.5 %collective-permute-start.13 = (f32[288,512]{1,0:T(8,128)S(1)}, f32[288,512]{1,0:T(8,128)S(1)}, u32[]{:S(2)}, u32[]{:S(2)}) collective-permute-start(f32[288,512]{1,0:T(8,128)S(1)} %collective-permute-done.8.t2), channel_id=1, source_target_pairs={{0,4},{4,0},{8,12},{12,8},{16,20},{20,16},{24,28},{28,24},{1,5},{5... | collective-permute-start | bytes 1769480 | tf_op jit(solution)/shard_map/ppermute | solution.py:486
  143.5 8.5 %collective-permute-start.7 = (f32[288,512]{1,0:T(8,128)S(1)}, f32[288,512]{1,0:T(8,128)S(1)}, u32[]{:S(2)}, u32[]{:S(2)}) collective-permute-start(f32[288,512]{1,0:T(8,128)S(1)} %collective-permute-done.6.s2), channel_id=1, source_target_pairs={{0,4},{4,0},{8,12},{12,8},{16,20},{20,16},{24,28},{28,24},{1,5},{5... | collective-permute-start | bytes 1769480 | tf_op jit(solution)/shard_map/ppermute | solution.py:486
  146.8 5.2 %collective-permute-start.12 = (f32[128,512]{1,0:T(8,128)S(1)}, f32[128,512]{1,0:T(8,128)S(1)}, u32[]{:S(2)}, u32[]{:S(2)}) collective-permute-start(f32[128,512]{1,0:T(8,128)S(1)} %collective-permute-done.10.f1), channel_id=1, source_target_pairs={{0,4},{4,0},{8,12},{12,8},{16,20},{20,16},{24,28},{28,24},{1,5},{5... | collective-permute-start | bytes 786440 | tf_op jit(solution)/shard_map/ppermute | solution.py:486
  146.8 5.2 %collective-permute-start.11 = (f32[160,512]{1,0:T(8,128)S(1)}, f32[160,512]{1,0:T(8,128)S(1)}, u32[]{:S(2)}, u32[]{:S(2)}) collective-permute-start(f32[160,512]{1,0:T(8,128)S(1)} %collective-permute-done.9.f0), channel_id=1, source_target_pairs={{0,4},{4,0},{8,12},{12,8},{16,20},{20,16},{24,28},{28,24},{1,5},{5... | collective-permute-start | bytes 983048 | tf_op jit(solution)/shard_map/ppermute | solution.py:486
  (4 other events, 2.7 us)

commit v5 on v4

--- a/solution.py
+++ b/solution.py
@@ -41,7 +41,7 @@
     )
 
 
-def route_kernel(group, slot_total, owner_ref, slot_ref, blocks_ref, rows_ref, cols_ref, send_ref, meta, held, count, sem):
+def route_kernel(group, slot_total, tile_cols, owner_ref, slot_ref, blocks_ref, rows_ref, cols_ref, send_ref, meta, held, count, sem):
     owners = meta.shape[0]
     blocks = held.shape[0]
     step = pl.program_id(0)
@@ -69,7 +69,11 @@
         o = owner_ref[g]
         k = jnp.minimum(count[o], 1)
         count[o] = k + 1
-        meta[o, pl.ds(k, 1), :] = jnp.full((1, T), slot_ref[g], jnp.int32).astype(F32)
+        slot = slot_ref[g]
+        panel_row = jnp.where(lax.rem(slot, tile_cols) == 0, lax.div(slot, tile_cols), slot_total)
+        lane = lax.broadcasted_iota(jnp.int32, (1, T), 1)
+        marks = jnp.where(lane == k, slot, panel_row).astype(F32)
+        meta[o, 0:1, :] = jnp.where((lane == k) | (lane == k + 2), marks, meta[o, 0:1, :])
         at(g, o, k).start()
 
     @pl.when(step == pl.num_programs(0) - 1)
@@ -85,12 +89,12 @@
         tail.wait()
 
 
-def route(owner, slot, blocks, rows, cols, owners, slot_total):
+def route(owner, slot, blocks, rows, cols, owners, slot_total, tile_cols):
     count = blocks.shape[0]
     group = 4
     whole = pl.BlockSpec((count, T), lambda i, *_: (0, 0))
     return pl.pallas_call(
-        functools.partial(route_kernel, group, slot_total),
+        functools.partial(route_kernel, group, slot_total, tile_cols),
         out_shape=jax.ShapeDtypeStruct((owners, 2 * T + 8, T), F32),
         grid_spec=pltpu.PrefetchScalarGridSpec(
             num_scalar_prefetch=2,
@@ -225,12 +229,19 @@
     )(core, mine, other)
 
 
-def panel_kernel(tile_cols, slot_total, slot_ref, col_ref, got_ref, base_ref, after_ref, out_ref, p0, p1, p2, p3, held, sem):
-    total = slot_ref.shape[0]
+def panel_kernel(col_ref, got_ref, base_ref, after_ref, out_ref, p0, p1, p2, p3, held, places, sem):
+    total = held.shape[0]
+    tile_rows = out_ref.shape[0] // T
+    look = pltpu.make_async_copy(got_ref.at[:, 2 * T, :], places, sem.at[total])
+    look.start()
+    out_ref[...] = base_ref[...]
+    look.wait()
+
+    def tile_row(n):
+        return places[n // 2, n % 2 + 2]
 
     def wanted(n):
-        slot = slot_ref[n]
-        return (slot < slot_total) & (slot % tile_cols == 0)
+        return tile_row(n) < tile_rows
 
     def copy(n):
         block = got_ref.at[n // 2, pl.ds(pl.multiple_of(n % 2 * T, T), T), :]
@@ -244,13 +255,12 @@
         return 0
 
     lax.fori_loop(0, total, fetch, 0, unroll=8)
-    out_ref[...] = base_ref[...]
 
     def add(n, _):
         @pl.when(wanted(n))
         def _():
             copy(n).wait()
-            a = pl.ds(pl.multiple_of(slot_ref[n] // tile_cols * T, T), T)
+            a = pl.ds(pl.multiple_of(tile_row(n).astype(jnp.int32) * T, T), T)
             out_ref[a, :] = out_ref[a, :] + held[n]
 
         return 0
@@ -263,22 +273,26 @@
             piece[a * quarter : (a + 1) * quarter, :] = out_ref[pl.ds(pl.multiple_of(a * T + first, quarter), quarter), :]
 
 
-def panel(slots, col, got, base, after, tile_cols, slot_total):
+def panel(col, got, base, after):
     rows = base.shape[0]
-    total = slots.shape[0]
-    return pl.pallas_call(
-        functools.partial(panel_kernel, tile_cols, slot_total),
+    total = 2 * got.shape[0]
+    return pl.pallas_call(
+        panel_kernel,
         out_shape=(jax.ShapeDtypeStruct((rows, T), F32),) + (jax.ShapeDtypeStruct((rows // 4, T), F32),) * 4,
         grid_spec=pltpu.PrefetchScalarGridSpec(
-            num_scalar_prefetch=2,
+            num_scalar_prefetch=1,
             grid=(),
             in_specs=[ANY(), VM(), ANY()],
             out_specs=(VM(),) * 5,
-            scratch_shapes=[pltpu.VMEM((total, T, T), F32), pltpu.SemaphoreType.DMA((total,))],
+            scratch_shapes=[
+                pltpu.VMEM((total, T, T), F32),
+                pltpu.SMEM((total // 2, T), F32),
+                pltpu.SemaphoreType.DMA((total + 1,)),
+            ],
         ),
         compiler_params=params(16),
         name="panel",
-    )(slots, col, got, base, after)
+    )(col, got, base, after)
 
 
 def load_rhs(order_ref, high_ref, low_ref, rhs_ref):
@@ -297,25 +311,25 @@
     )
 
 
-def share_kernel(order_ref, x0, x1, x2, x3, high_ref, low_ref, after_ref, out_ref, rhs_ref):
+def share_kernel(order_ref, x0, x1, x2, x3, high_ref, low_ref, out_ref, rhs_ref):
     load_rhs(order_ref, high_ref, low_ref, rhs_ref)
     out_ref[...] = times_wt([x[...] for x in (x0, x1, x2, x3)], rhs_ref)
 
 
-def share_solve(order, parts, wt, after):
+def share_solve(order, parts, wt):
     return pl.pallas_call(
         share_kernel,
         out_shape=jax.ShapeDtypeStruct((parts[0].shape[0], 4 * T), F32),
         grid_spec=pltpu.PrefetchScalarGridSpec(
             num_scalar_prefetch=1,
             grid=(),
-            in_specs=[VM()] * 6 + [ANY()],
+            in_specs=[VM()] * 6,
             out_specs=VM(),
             scratch_shapes=[pltpu.VMEM((12 * T, 4 * T), BF16)],
         ),
         compiler_params=params(16),
         name="share_solve",
-    )(order, *parts, *wt, after)
+    )(order, *parts, *wt)
 
 
 def rows_kernel(info_ref, x0, x1, x2, x3, high_ref, low_ref, lhs_ref, own_ref, rhs_ref):
@@ -386,7 +400,7 @@
             in_specs=[pl.BlockSpec(got.shape, lambda a, s: (0, 0, 0)), block],
             out_specs=block,
         ),
-        compiler_params=params(40),
+        compiler_params=params(28),
         cost_estimate=pl.CostEstimate(flops=10_000_000_000, bytes_accessed=26_000_000, transcendentals=0),
         name="rest",
     )(slots, got, base)
@@ -446,7 +460,7 @@
             out_specs=block,
             scratch_shapes=[pltpu.VMEM((tile_cols * T, 8 * T), BF16)],
         ),
-        compiler_params=params(44),
+        compiler_params=params(36),
         name="update",
     )(row, *pieces, lhs, own, base)
 
@@ -459,7 +473,7 @@
     flat = front.reshape(tile_rows * T * tile_cols, T)
     base_panel = front[0, :, 0, :, 0, 0, :].reshape(tile_rows * T, T)
 
-    send = route(child_owner[0, :, 0], child_slot[0], child_updates[0], child_rows[0], child_cols[0], 32, slot_total)
+    send = route(child_owner[0, :, 0], child_slot[0], child_updates[0], child_rows[0], child_cols[0], 32, slot_total, tile_cols)
 
     tile = base_panel[:T].reshape(1, 2, 1, T // 2, T)
     halves = jnp.broadcast_to(tile, (4, 2, 4, T // 2, T)).reshape(32, T // 2, T)
@@ -469,8 +483,7 @@
     got = lax.all_to_all(send, ("row", "col"), split_axis=0, concat_axis=0, tiled=True)
     wt = leading_inverse((my_row % 2).reshape(1), mine, other)
 
-    slots = got[:, 2 * T : 2 * T + 2, 0].astype(jnp.int32).reshape(64)
-    columns, *pieces = panel(slots, my_col.reshape(1), got, base_panel, wt[1], tile_cols, slot_total)
+    columns, *pieces = panel(my_col.reshape(1), got, base_panel, wt[1])
 
     parts = []
     for m in range(4):
@@ -479,8 +492,8 @@
         ]
         parts.append(lax.ppermute(pieces[m], ("row", "col"), moves))
     order = (my_row - jnp.arange(4, dtype=jnp.int32)) % 4
-    base = rest(slots, got, flat, tile_rows, tile_cols)
-    share = share_solve(order, parts, wt, base)
+    share = share_solve(order, parts, wt)
+    got, share = lax.optimization_barrier((got, share))
 
     def swap(x, bits):
         return lax.ppermute(x, "row", [(r, r ^ bits) for r in range(8)])
@@ -488,12 +501,15 @@
     cut = 5 * T // 4
     near, far_side = swap(share, 2), swap(share, 6)
     beside = swap(share, 1)
+    columns, beside = lax.optimization_barrier((columns, beside))
     near_beside = swap(near, 1)
+    slots = got[:, 2 * T, 0:2].astype(jnp.int32).reshape(64)
+    base = rest(slots, got, flat, tile_rows, tile_cols)
+    near, far_side, base = lax.optimization_barrier((near, far_side, base))
     opposite = [swap(far_side[:cut], 2), swap(near[cut:], 6)]
     far_beside = swap(far_side, 1)
     opposite_beside = [swap(x, 1) for x in opposite]
 
-    columns, base, *_ = lax.optimization_barrier((columns, base, *parts))
     right = [(i, (i + 1) % 4) for i in range(4)]
     left = [(i, (i - 1) % 4) for i in range(4)]
     half = tile_rows * T // 2

time: 167 us -> 157 us (0.940)
  Pallas kernels: 71.5 us -> 63.3 us
  starting transfers between devices: 33.5 us -> 30.9 us
  local copies, waits for them, and re-layouts: 13.2 us -> 15 us
    ppermute x4, waiting for transfers between devices: 0.01 us -> 6.6 us  [local(): parts.append(lax.ppermute(pieces[m], ('row', 'col'), moves))]
    pallas_call x1, Pallas kernels: 12.6 us -> 6.15 us  [rest(): pl.pallas_call(functools.partial(rest_kernel, tile_cols, group), out_shap...]
    ppermute x9, waiting for transfers between devices: 12.9 us -> 7.36 us  [swap(): return lax.ppermute(x, 'row', [(r, r ^ bits) for r in range(8)])]
    ppermute x1, starting transfers between devices: 4.01 us -> 1.89 us  [local(): from_right = lax.ppermute(columns, 'col', left)]
    slice x2, local copies, waits for them, and re-layouts: 0.04 us -> 1.96 us  [local(): opposite = [swap(far_side[:cut], 2), swap(near[cut:], 6)]]
    unnamed x16 -> x28, local copies, waits for them, and re-layouts: 8.81 us -> 9.65 us
  transfers between devices with their start and end apart: 20 -> 20, of which waited for: 5 -> 9; matrix products, arithmetic and copies ran while one was open for 1% -> 3% of each run, Pallas kernels for 32% -> 29%
where the time goes in v5:
time: 157 us; the launch traced here: 156 us
  Pallas kernels  63.3 us (40%)
  waiting for transfers between devices  45.2 us (29%)
  starting transfers between devices  30.9 us (20%)
  local copies, waits for them, and re-layouts  15 us (10%)
    pallas_call x1, Pallas kernels, leading_inverse(): pl.pallas_call(leading_kernel, out_shape=(jax.ShapeDtypeStruct((4, T, 4 *...  28.2 us
    all_to_all x1, waiting for transfers between devices, local(): lax.all_to_all(send, ('row', 'col'), split_axis=0, concat_axis=0, tiled=T...  24.9 us
    pallas_call x1, Pallas kernels, update(): pl.pallas_call(functools.partial(update_kernel, tile_cols, group), out_sh...  12.8 us
    unnamed x28, local copies, waits for them, and re-layouts  9.65 us
    all_to_all x1, starting transfers between devices, local(): lax.all_to_all(halves, ('row', 'col'), split_axis=0, concat_axis=0, tiled...  8.42 us
    pallas_call x1, Pallas kernels, route(): pl.pallas_call(functools.partial(route_kernel, group, slot_total, tile_co...  7.45 us
    ppermute x4, starting transfers between devices, local(): parts.append(lax.ppermute(pieces[m], ('row', 'col'), moves))  7.44 us
    ppermute x9, waiting for transfers between devices, swap(): return lax.ppermute(x, 'row', [(r, r ^ bits) for r in range(8)])  7.36 us
  transfers between devices with their start and end apart: 20, of which 9 were waited for; matrix products, arithmetic and copies ran while one was open for 3% of the time, Pallas kernels for 29%

profile of v5, /device:TPU:0, one launch (start us, length us, event | category | flops | bytes accessed | tf_op | source)
XLA Modules:
  0.0 155.7 jit_solution(5851345442563709271)
XLA Ops:
  2.1 8.4 %all-to-all-start = ((f32[32,64,128]{2,1,0:T(8,128)}), f32[32,64,128]{2,1,0:T(8,128)S(1)}, u32[]{:S(2)}, u32[]{:S(2)}) async-start(f32[32,64,128]{2,1,0:T(8,128)} %bitcast.2), calls=%async_computation | async-start | bytes 2097152 | tf_op jit(solution)/shard_map/all_to_all | solution.py:480
  13.3 7.5 %route.1 = f32[32,264,128]{2,1,0:T(8,128)S(1)} custom-call(s32[32]{0:T(128)S(1)} %bitcast.19, s32[32]{0:T(128)S(1)} %bitcast.20, f32[32,128,128]{2,1,0:T(8,128)S(1)} %bitcast.15, s32[32,128]{1,0:T(8,128)S(1)} %bitcast.17, s32[32,128]{1,0:T(8,128)S(1)} %bitcast.18), custom_call_target="tpu_custom_call" | custom-call | tf_op jit(solution)/shard_map/route/pallas_call | solution.py:96
  20.8 2.0 %copy-done = f32[32,264,128]{2,1,0:T(8,128)} copy-done((f32[32,264,128]{2,1,0:T(8,128)}, f32[32,264,128]{2,1,0:T(8,128)S(1)}, u32[]{:S(2)}) %copy-start) | copy-done | bytes 4325400
  22.8 4.8 %all-to-all-done = f32[32,64,128]{2,1,0:T(8,128)S(1)} async-done(((f32[32,64,128]{2,1,0:T(8,128)}), f32[32,64,128]{2,1,0:T(8,128)S(1)}, u32[]{:S(2)}, u32[]{:S(2)}) %all-to-all-start) | async-done | bytes 1048608 | tf_op jit(solution)/shard_map/all_to_all | solution.py:480
  28.9 4.9 %all-to-all-start.1 = ((f32[32,264,128]{2,1,0:T(8,128)}), f32[32,264,128]{2,1,0:T(8,128)}, u32[]{:S(2)}, u32[]{:S(2)}) async-start(f32[32,264,128]{2,1,0:T(8,128)} %copy-done), calls=%async_computation.1 | async-start | bytes 8650752 | tf_op jit(solution)/shard_map/all_to_all | solution.py:483
  33.8 28.2 %leading_inverse.1 = (bf16[4,128,512]{2,1,0:T(8,128)(2,1)S(1)}, bf16[4,128,512]{2,1,0:T(8,128)(2,1)S(1)}) custom-call(s32[1]{0:T(128)} %bitcast.10.core_ref, f32[16,64,128]{2,1,0:T(8,128)S(1)} %slice.34.mine_ref, f32[16,64,128]{2,1,0:T(8,128)S(1)} %collective-permute-done.other_ref), custom_call_target="tpu_custom_call" | custom-call | flops 60000002048 | bytes 2000000 | tf_op jit(solution)/shard_map/leading_inverse/pallas_call | solution.py:212
  62.1 24.9 %all-to-all-done.1.got_ref = f32[32,264,128]{2,1,0:T(8,128)} async-done(((f32[32,264,128]{2,1,0:T(8,128)}), f32[32,264,128]{2,1,0:T(8,128)}, u32[]{:S(2)}, u32[]{:S(2)}) %all-to-all-start.1) | async-done | bytes 4325408 | tf_op jit(solution)/shard_map/all_to_all | solution.py:483
  86.9 3.4 %panel.1 = (f32[1152,128]{1,0:T(8,128)S(1)}, f32[288,128]{1,0:T(8,128)S(1)}, f32[288,128]{1,0:T(8,128)S(1)}, f32[288,128]{1,0:T(8,128)S(1)}, f32[288,128]{1,0:T(8,128)S(1)}) custom-call(s32[1]{0:T(128)} %bitcast.8.col_ref, f32[32,264,128]{2,1,0:T(8,128)} %all-to-all-done.1.got_ref, f32[1152,128]{1,0:T(8,128)S(1)} %bitcast.14, ...), custom_call_target="tpu_custom_call" | custom-call | tf_op jit(solution)/shard_map/panel/pallas_call | solution.py:279
  91.0 2.3 %collective-permute-start.2 = (f32[288,128]{1,0:T(8,128)S(1)}, f32[288,128]{1,0:T(8,128)S(1)}, u32[]{:S(2)}, u32[]{:S(2)}) collective-permute-start(f32[288,128]{1,0:T(8,128)S(1)} %get-tuple-element.27), channel_id=1, source_target_pairs={{0,4},{1,8},{2,12},{3,0},{4,5},{5,9},{6,13},{7,1},{8,6},{9,10},{10... | collective-permute-start | bytes 442376 | tf_op jit(solution)/shard_map/ppermute | solution.py:493
  93.3 3.2 %collective-permute-start.3 = (f32[288,128]{1,0:T(8,128)S(1)}, f32[288,128]{1,0:T(8,128)S(1)}, u32[]{:S(2)}, u32[]{:S(2)}) collective-permute-start(f32[288,128]{1,0:T(8,128)S(1)} %get-tuple-element.28), channel_id=1, source_target_pairs={{0,8},{1,12},{2,0},{3,4},{4,9},{5,13},{6,1},{7,5},{8,10},{9,14},{1... | collective-permute-start | bytes 442376 | tf_op jit(solution)/shard_map/ppermute | solution.py:493
  97.7 1.6 %collective-permute-done.2.x1 = f32[288,128]{1,0:T(8,128)S(1)} collective-permute-done((f32[288,128]{1,0:T(8,128)S(1)}, f32[288,128]{1,0:T(8,128)S(1)}, u32[]{:S(2)}, u32[]{:S(2)}) %collective-permute-start.2) | collective-permute-done | bytes 147488 | tf_op jit(solution)/shard_map/ppermute | solution.py:493
  99.3 5.0 %collective-permute-done.3.x2 = f32[288,128]{1,0:T(8,128)S(1)} collective-permute-done((f32[288,128]{1,0:T(8,128)S(1)}, f32[288,128]{1,0:T(8,128)S(1)}, u32[]{:S(2)}, u32[]{:S(2)}) %collective-permute-start.3) | collective-permute-done | bytes 147488 | tf_op jit(solution)/shard_map/ppermute | solution.py:493
  104.3 2.0 %share_solve.1.s0 = f32[288,512]{1,0:T(8,128)} custom-call(s32[4]{0:T(128)S(1)} %and_select_fusion.1.order_ref, f32[288,128]{1,0:T(8,128)S(1)} %collective-permute-done.1.x0, f32[288,128]{1,0:T(8,128)S(1)} %collective-permute-done.2.x1, f32[288,128]{1,0:T(8,128)S(1)} %collective-permute-done.3.x2, f32[288,128]{1,0:T(8,128)S(1)} %collective-permute-done.4.x3, ...), custom_call_target="tpu_custom_call" | custom-call | tf_op jit(solution)/shard_map/share_solve/pallas_call | solution.py:320
  106.3 1.4 collective-permute-start.5
  111.3 1.9 %collective-permute-start.15 = (f32[1152,128]{1,0:T(8,128)S(1)}, f32[1152,128]{1,0:T(8,128)S(1)}, u32[]{:S(2)}, u32[]{:S(2)}) collective-permute-start(f32[1152,128]{1,0:T(8,128)S(1)} %get-tuple-element.37.x0), channel_id=1, source_target_pairs={{0,3},{1,0},{2,1},{3,2},{4,7},{5,4},{6,5},{7,6},{8,11},{9,8},{10,9... | collective-permute-start | bytes 1769480 | tf_op jit(solution)/shard_map/ppermute | solution.py:517
  113.4 4.0 %copy-done.8 = f32[1,9,1,128,18,1,128]{6,5,4,3,2,1,0:T(1,128)S(1)} copy-done((f32[1,9,1,128,18,1,128]{6,5,4,3,2,1,0:T(1,128)S(1)}, f32[1,9,1,128,18,1,128]{6,5,4,3,2,1,0:T(1,128)}, u32[]{:S(2)}) %copy-start.8) | copy-done | bytes 10616856
  117.4 6.1 %rest.1.base_ref = f32[20736,128]{1,0:T(8,128)S(1)} custom-call(s32[64]{0:T(128)S(1)} %convert_element_type.9.slot_ref, f32[32,264,128]{2,1,0:T(8,128)} %all-to-all-done.1.got_ref, f32[20736,128]{1,0:T(8,128)S(1)} %bitcast.16), custom_call_target="tpu_custom_call" | custom-call | flops 10000000000 | bytes 26000000 | tf_op jit(solution)/shard_map/rest/pallas_call | solution.py:394
  125.8 1.6 %collective-permute-start.10 = (f32[128,512]{1,0:T(8,128)S(1)}, f32[128,512]{1,0:T(8,128)S(1)}, u32[]{:S(2)}, u32[]{:S(2)}) collective-permute-start(f32[128,512]{1,0:T(8,128)S(1)} %slice.31), channel_id=1, source_target_pairs={{0,24},{4,28},{8,16},{12,20},{16,8},{20,12},{24,0},{28,4},{1,25},{... | collective-permute-start | bytes 786440 | tf_op jit(solution)/shard_map/ppermute | solution.py:499
  128.7 2.4 %collective-permute-start.17 = (f32[576,128]{1,0:T(8,128)S(1)}, f32[576,128]{1,0:T(8,128)S(1)}, u32[]{:S(2)}, u32[]{:S(2)}) collective-permute-start(f32[576,128]{1,0:T(8,128)S(1)} %slice.36), channel_id=1, source_target_pairs={{0,3},{1,0},{2,1},{3,2},{4,7},{5,4},{6,5},{7,6},{8,11},{9,8},{10,9... | collective-permute-start | bytes 884744 | tf_op jit(solution)/shard_map/ppermute | solution.py:519
  131.4 3.3 %collective-permute-done.10.f1 = f32[128,512]{1,0:T(8,128)S(1)} collective-permute-done((f32[128,512]{1,0:T(8,128)S(1)}, f32[128,512]{1,0:T(8,128)S(1)}, u32[]{:S(2)}, u32[]{:S(2)}) %collective-permute-start.10) | collective-permute-done | bytes 262176 | tf_op jit(solution)/shard_map/ppermute | solution.py:499
  134.7 2.8 %collective-permute-done.9.f0 = f32[160,512]{1,0:T(8,128)S(1)} collective-permute-done((f32[160,512]{1,0:T(8,128)S(1)}, f32[160,512]{1,0:T(8,128)S(1)}, u32[]{:S(2)}, u32[]{:S(2)}) %collective-permute-start.9) | collective-permute-done | bytes 327712 | tf_op jit(solution)/shard_map/ppermute | solution.py:499
  138.0 1.5 collective-permute-done.16
  139.5 3.4 %rows_solve.1 = (bf16[1152,1024]{1,0:T(8,128)(2,1)S(1)}, f32[1152,128]{1,0:T(8,128)S(1)}) custom-call(s32[6]{0:T(128)S(1)} %pad_add_fusion.info_ref, f32[1152,128]{1,0:T(8,128)S(1)} %get-tuple-element.37.x0, f32[1152,128]{1,0:T(8,128)S(1)} %collective-permute-done.14.x1, f32[1152,128]{1,0:T(8,128)S(1)} %collective-permute-done.15.x2, ...), custom_call_target="tpu_custom_call" | custom-call | flops 4000000000 | bytes 8000000 | tf_op jit(solution)/shard_map/rows_solve/pallas_call | solution.py:357
  143.0 12.8 %update.1 = f32[20736,128]{1,0:T(8,128)} custom-call(s32[1]{0:T(128)} %bitcast.row_ref, f32[288,512]{1,0:T(8,128)} %share_solve.1.s0, f32[288,512]{1,0:T(8,128)S(1)} %copy-done.5, f32[288,512]{1,0:T(8,128)} %collective-permute-done.6.s2, f32[288,512]{1,0:T(8,128)S(1)} %collective-permute-done.8.s3, f32[160,512]{1,0:T(8,128)S(1)} %collective-permute-done.9.f0, ...), custom_call_target="tpu_custom_call" | custom-call | tf_op jit(solution)/shard_map/update/pallas_call | solution.py:448
  (65 shorter events, 16.1 us)
Async XLA Ops:
  2.1 25.6 %all-to-all-start = ((f32[32,64,128]{2,1,0:T(8,128)}), f32[32,64,128]{2,1,0:T(8,128)S(1)}, u32[]{:S(2)}, u32[]{:S(2)}) async-start(f32[32,64,128]{2,1,0:T(8,128)} %bitcast.2), calls=%async_computation | async-start | bytes 2097152 | tf_op jit(solution)/shard_map/all_to_all | solution.py:480
  27.7 6.1 %collective-permute-start = (f32[16,64,128]{2,1,0:T(8,128)S(1)}, f32[16,64,128]{2,1,0:T(8,128)S(1)}, u32[]{:S(2)}, u32[]{:S(2)}) collective-permute-start(f32[16,64,128]{2,1,0:T(8,128)S(1)} %slice.34.mine_ref), channel_id=1, source_target_pairs={{0,4},{4,0},{8,12},{12,8},{16,20},{20,16},{24,28},{28,24},{1,5},{5... | collective-permute-start | bytes 1572872 | tf_op jit(solution)/shard_map/ppermute | solution.py:482
  28.9 58.0 %all-to-all-start.1 = ((f32[32,264,128]{2,1,0:T(8,128)}), f32[32,264,128]{2,1,0:T(8,128)}, u32[]{:S(2)}, u32[]{:S(2)}) async-start(f32[32,264,128]{2,1,0:T(8,128)} %copy-done), calls=%async_computation.1 | async-start | bytes 8650752 | tf_op jit(solution)/shard_map/all_to_all | solution.py:483
  62.0 51.3 %copy-start.2 = (bf16[4,128,512]{2,1,0:T(8,128)(2,1)}, bf16[4,128,512]{2,1,0:T(8,128)(2,1)S(1)}, u32[]{:S(2)}) copy-start(bf16[4,128,512]{2,1,0:T(8,128)(2,1)S(1)} %get-tuple-element.25.after_ref.low_ref) | copy-start | bytes 1572868
  62.0 51.3 %copy-start.6 = (bf16[4,128,512]{2,1,0:T(8,128)(2,1)}, bf16[4,128,512]{2,1,0:T(8,128)(2,1)S(1)}, u32[]{:S(2)}) copy-start(bf16[4,128,512]{2,1,0:T(8,128)(2,1)S(1)} %get-tuple-element.30.high_ref) | copy-start | bytes 1572868
  90.3 7.5 %collective-permute-start.1 = (f32[288,128]{1,0:T(8,128)S(1)}, f32[288,128]{1,0:T(8,128)S(1)}, u32[]{:S(2)}, u32[]{:S(2)}) collective-permute-start(f32[288,128]{1,0:T(8,128)S(1)} %get-tuple-element.26), channel_id=1, source_target_pairs={{0,0},{1,4},{2,8},{3,12},{4,1},{5,5},{6,9},{7,13},{8,2},{9,6},{10,... | collective-permute-start | bytes 442376 | tf_op jit(solution)/shard_map/ppermute | solution.py:493
  91.0 8.4 %collective-permute-start.2 = (f32[288,128]{1,0:T(8,128)S(1)}, f32[288,128]{1,0:T(8,128)S(1)}, u32[]{:S(2)}, u32[]{:S(2)}) collective-permute-start(f32[288,128]{1,0:T(8,128)S(1)} %get-tuple-element.27), channel_id=1, source_target_pairs={{0,4},{1,8},{2,12},{3,0},{4,5},{5,9},{6,13},{7,1},{8,6},{9,10},{10... | collective-permute-start | bytes 442376 | tf_op jit(solution)/shard_map/ppermute | solution.py:493
  93.3 11.1 %collective-permute-start.3 = (f32[288,128]{1,0:T(8,128)S(1)}, f32[288,128]{1,0:T(8,128)S(1)}, u32[]{:S(2)}, u32[]{:S(2)}) collective-permute-start(f32[288,128]{1,0:T(8,128)S(1)} %get-tuple-element.28), channel_id=1, source_target_pairs={{0,8},{1,12},{2,0},{3,4},{4,9},{5,13},{6,1},{7,5},{8,10},{9,14},{1... | collective-permute-start | bytes 442376 | tf_op jit(solution)/shard_map/ppermute | solution.py:493
  96.5 7.9 %collective-permute-start.4 = (f32[288,128]{1,0:T(8,128)S(1)}, f32[288,128]{1,0:T(8,128)S(1)}, u32[]{:S(2)}, u32[]{:S(2)}) collective-permute-start(f32[288,128]{1,0:T(8,128)S(1)} %get-tuple-element.29), channel_id=1, source_target_pairs={{0,12},{1,0},{2,4},{3,8},{4,13},{5,1},{6,5},{7,9},{8,14},{9,2},{10... | collective-permute-start | bytes 442376 | tf_op jit(solution)/shard_map/ppermute | solution.py:493
  106.3 4.2 %collective-permute-start.5 = (f32[288,512]{1,0:T(8,128)}, f32[288,512]{1,0:T(8,128)S(1)}, u32[]{:S(2)}, u32[]{:S(2)}) collective-permute-start(f32[288,512]{1,0:T(8,128)} %share_solve.1.s0), channel_id=1, source_target_pairs={{0,4},{4,0},{8,12},{12,8},{16,20},{20,16},{24,28},{28,24},{1,5},{5... | collective-permute-start | bytes 1769480 | tf_op jit(solution)/shard_map/ppermute | solution.py:499
  107.7 16.8 %collective-permute-start.7 = (f32[288,512]{1,0:T(8,128)}, f32[288,512]{1,0:T(8,128)}, u32[]{:S(2)}, u32[]{:S(2)}) collective-permute-start(f32[288,512]{1,0:T(8,128)} %share_solve.1.s0), channel_id=1, source_target_pairs={{0,24},{4,28},{8,16},{12,20},{16,8},{20,12},{24,0},{28,4},{1,25},{... | collective-permute-start | bytes 1769480 | tf_op jit(solution)/shard_map/ppermute | solution.py:499
  109.0 15.8 %collective-permute-start.6 = (f32[288,512]{1,0:T(8,128)}, f32[288,512]{1,0:T(8,128)}, u32[]{:S(2)}, u32[]{:S(2)}) collective-permute-start(f32[288,512]{1,0:T(8,128)} %share_solve.1.s0), channel_id=1, source_target_pairs={{0,8},{4,12},{8,0},{12,4},{16,24},{20,28},{24,16},{28,20},{1,9},{5... | collective-permute-start | bytes 1769480 | tf_op jit(solution)/shard_map/ppermute | solution.py:499
  111.3 17.3 %collective-permute-start.15 = (f32[1152,128]{1,0:T(8,128)S(1)}, f32[1152,128]{1,0:T(8,128)S(1)}, u32[]{:S(2)}, u32[]{:S(2)}) collective-permute-start(f32[1152,128]{1,0:T(8,128)S(1)} %get-tuple-element.37.x0), channel_id=1, source_target_pairs={{0,3},{1,0},{2,1},{3,2},{4,7},{5,4},{6,5},{7,6},{8,11},{9,8},{10,9... | collective-permute-start | bytes 1769480 | tf_op jit(solution)/shard_map/ppermute | solution.py:517
  113.2 17.9 %collective-permute-start.14 = (f32[1152,128]{1,0:T(8,128)S(1)}, f32[1152,128]{1,0:T(8,128)S(1)}, u32[]{:S(2)}, u32[]{:S(2)}) collective-permute-start(f32[1152,128]{1,0:T(8,128)S(1)} %get-tuple-element.37.x0), channel_id=1, source_target_pairs={{0,1},{1,2},{2,3},{3,0},{4,5},{5,6},{6,7},{7,4},{8,9},{9,10},{10,1... | collective-permute-start | bytes 1769480 | tf_op jit(solution)/shard_map/ppermute | solution.py:516
  117.4 22.1 %copy-start.3 = (bf16[4,128,512]{2,1,0:T(8,128)(2,1)S(1)}, bf16[4,128,512]{2,1,0:T(8,128)(2,1)}, u32[]{:S(2)}) copy-start(bf16[4,128,512]{2,1,0:T(8,128)(2,1)} %copy-done.2) | copy-start | bytes 1572868
  117.4 22.1 %copy-start.7 = (bf16[4,128,512]{2,1,0:T(8,128)(2,1)S(1)}, bf16[4,128,512]{2,1,0:T(8,128)(2,1)}, u32[]{:S(2)}) copy-start(bf16[4,128,512]{2,1,0:T(8,128)(2,1)} %copy-done.6) | copy-start | bytes 1572868
  125.8 8.9 %collective-permute-start.10 = (f32[128,512]{1,0:T(8,128)S(1)}, f32[128,512]{1,0:T(8,128)S(1)}, u32[]{:S(2)}, u32[]{:S(2)}) collective-permute-start(f32[128,512]{1,0:T(8,128)S(1)} %slice.31), channel_id=1, source_target_pairs={{0,24},{4,28},{8,16},{12,20},{16,8},{20,12},{24,0},{28,4},{1,25},{... | collective-permute-start | bytes 786440 | tf_op jit(solution)/shard_map/ppermute | solution.py:499
  128.3 9.1 %collective-permute-start.9 = (f32[160,512]{1,0:T(8,128)S(1)}, f32[160,512]{1,0:T(8,128)S(1)}, u32[]{:S(2)}, u32[]{:S(2)}) collective-permute-start(f32[160,512]{1,0:T(8,128)S(1)} %slice.30), channel_id=1, source_target_pairs={{0,8},{4,12},{8,0},{12,4},{16,24},{20,28},{24,16},{28,20},{1,9},{5... | collective-permute-start | bytes 983048 | tf_op jit(solution)/shard_map/ppermute | solution.py:499
  128.7 8.8 %collective-permute-start.17 = (f32[576,128]{1,0:T(8,128)S(1)}, f32[576,128]{1,0:T(8,128)S(1)}, u32[]{:S(2)}, u32[]{:S(2)}) collective-permute-start(f32[576,128]{1,0:T(8,128)S(1)} %slice.36), channel_id=1, source_target_pairs={{0,3},{1,0},{2,1},{3,2},{4,7},{5,4},{6,5},{7,6},{8,11},{9,8},{10,9... | collective-permute-start | bytes 884744 | tf_op jit(solution)/shard_map/ppermute | solution.py:519
  131.1 8.3 %collective-permute-start.16 = (f32[576,128]{1,0:T(8,128)S(1)}, f32[576,128]{1,0:T(8,128)S(1)}, u32[]{:S(2)}, u32[]{:S(2)}) collective-permute-start(f32[576,128]{1,0:T(8,128)S(1)} %slice.35), channel_id=1, source_target_pairs={{0,1},{1,2},{2,3},{3,0},{4,5},{5,6},{6,7},{7,4},{8,9},{9,10},{10,1... | collective-permute-start | bytes 884744 | tf_op jit(solution)/shard_map/ppermute | solution.py:518
  131.3 11.6 %collective-permute-start.13 = (f32[288,512]{1,0:T(8,128)}, f32[288,512]{1,0:T(8,128)S(1)}, u32[]{:S(2)}, u32[]{:S(2)}) collective-permute-start(f32[288,512]{1,0:T(8,128)} %collective-permute-done.7.t2), channel_id=1, source_target_pairs={{0,4},{4,0},{8,12},{12,8},{16,20},{20,16},{24,28},{28,24},{1,5},{5... | collective-permute-start | bytes 1769480 | tf_op jit(solution)/shard_map/ppermute | solution.py:499
  134.7 8.3 %collective-permute-start.8 = (f32[288,512]{1,0:T(8,128)}, f32[288,512]{1,0:T(8,128)S(1)}, u32[]{:S(2)}, u32[]{:S(2)}) collective-permute-start(f32[288,512]{1,0:T(8,128)} %collective-permute-done.6.s2), channel_id=1, source_target_pairs={{0,4},{4,0},{8,12},{12,8},{16,20},{20,16},{24,28},{28,24},{1,5},{5... | collective-permute-start | bytes 1769480 | tf_op jit(solution)/shard_map/ppermute | solution.py:499
  137.5 5.5 %collective-permute-start.12 = (f32[128,512]{1,0:T(8,128)S(1)}, f32[128,512]{1,0:T(8,128)S(1)}, u32[]{:S(2)}, u32[]{:S(2)}) collective-permute-start(f32[128,512]{1,0:T(8,128)S(1)} %collective-permute-done.10.f1), channel_id=1, source_target_pairs={{0,4},{4,0},{8,12},{12,8},{16,20},{20,16},{24,28},{28,24},{1,5},{5... | collective-permute-start | bytes 786440 | tf_op jit(solution)/shard_map/ppermute | solution.py:499
  137.5 5.5 %collective-permute-start.11 = (f32[160,512]{1,0:T(8,128)S(1)}, f32[160,512]{1,0:T(8,128)S(1)}, u32[]{:S(2)}, u32[]{:S(2)}) collective-permute-start(f32[160,512]{1,0:T(8,128)S(1)} %collective-permute-done.9.f0), channel_id=1, source_target_pairs={{0,4},{4,0},{8,12},{12,8},{16,20},{20,16},{24,28},{28,24},{1,5},{5... | collective-permute-start | bytes 983048 | tf_op jit(solution)/shard_map/ppermute | solution.py:499
  (10 other events, 37.4 us)

commit v6 on v5

--- a/solution.py
+++ b/solution.py
@@ -108,7 +108,7 @@
                 pltpu.SemaphoreType.DMA((count + 1,)),
             ],
         ),
-        compiler_params=params(16),
+        compiler_params=params(),
         name="route",
     )(owner, slot, blocks, rows, cols)
 
@@ -400,31 +400,29 @@
             in_specs=[pl.BlockSpec(got.shape, lambda a, s: (0, 0, 0)), block],
             out_specs=block,
         ),
-        compiler_params=params(28),
+        compiler_params=params(54),
         cost_estimate=pl.CostEstimate(flops=10_000_000_000, bytes_accessed=26_000_000, transcendentals=0),
         name="rest",
     )(slots, got, base)
 
 
 def load_columns(h, k, pieces, rhs_ref):
-    for d, arrays in enumerate(pieces):
+    for d, ref in enumerate(pieces):
         quarter = (k ^ d) * 32 + h * T
-        for first, ref in arrays:
-            for q in range(ref.shape[0] // 32):
-                high, low = split(ref[32 * q : 32 * q + 32, :])
-                at = pl.ds(pl.multiple_of((first + q) * 2 * T + quarter, 32), 32)
-                rhs_ref[at, 0:512] = high
-                rhs_ref[at, 512:1024] = low
-
-
-def update_kernel(tile_cols, group, row_ref, s0, s1, s2, s3, f0, f1, g0, g1, t2, t3, lhs_ref, own_ref, base_ref, out_ref, rhs_ref):
+        for q in range(ref.shape[0] // 32):
+            high, low = split(ref[32 * q : 32 * q + 32, :])
+            at = pl.ds(pl.multiple_of(q * 2 * T + quarter, 32), 32)
+            rhs_ref[at, 0:512] = high
+            rhs_ref[at, 512:1024] = low
+
+
+def update_kernel(tile_cols, group, row_ref, s0, s1, s2, s3, t0, t1, t2, t3, lhs_ref, own_ref, base_ref, out_ref, rhs_ref):
     h, k = row_ref[0] // 4, row_ref[0] % 4
-    top = f0.shape[0] // 32
 
     @pl.when(pl.program_id(0) == 0)
     def _():
-        load_columns(h, k, [[(0, x)] for x in (s0, s1, s2, s3)], rhs_ref)
-        load_columns(1 - h, k, [[(0, f0), (top, f1)], [(0, g0), (top, g1)], [(0, t2)], [(0, t3)]], rhs_ref)
+        load_columns(h, k, (s0, s1, s2, s3), rhs_ref)
+        load_columns(1 - h, k, (t0, t1, t2, t3), rhs_ref)
 
     both = lhs_ref[...]
     lhs = jnp.concatenate([both[:, 0:512], both], axis=1)
@@ -492,32 +490,32 @@
         ]
         parts.append(lax.ppermute(pieces[m], ("row", "col"), moves))
     order = (my_row - jnp.arange(4, dtype=jnp.int32)) % 4
+    first_core = my_row % 2 == 0
+    columns, parts[0] = lax.optimization_barrier((columns, parts[0]))
+    from_left = lax.ppermute(columns, "col", [(c, (c + 1) % 4) for c in range(4)])
+    from_right = lax.ppermute(columns, "col", [(c, (c - 1) % 4) for c in range(4)])
+    far = lax.ppermute(
+        jnp.where(first_core, from_left, from_right),
+        ("row", "col"),
+        [(r * 4 + c, r * 4 + (c + 1 - 2 * (r % 2)) % 4) for r in range(8) for c in range(4)],
+    )
+
     share = share_solve(order, parts, wt)
     got, share = lax.optimization_barrier((got, share))
 
     def swap(x, bits):
         return lax.ppermute(x, "row", [(r, r ^ bits) for r in range(8)])
 
-    cut = 5 * T // 4
     near, far_side = swap(share, 2), swap(share, 6)
     beside = swap(share, 1)
-    columns, beside = lax.optimization_barrier((columns, beside))
-    near_beside = swap(near, 1)
     slots = got[:, 2 * T, 0:2].astype(jnp.int32).reshape(64)
     base = rest(slots, got, flat, tile_rows, tile_cols)
     near, far_side, base = lax.optimization_barrier((near, far_side, base))
-    opposite = [swap(far_side[:cut], 2), swap(near[cut:], 6)]
-    far_beside = swap(far_side, 1)
-    opposite_beside = [swap(x, 1) for x in opposite]
-
-    right = [(i, (i + 1) % 4) for i in range(4)]
-    left = [(i, (i - 1) % 4) for i in range(4)]
-    half = tile_rows * T // 2
-    from_left = lax.ppermute(columns, "col", right)
-    from_right = lax.ppermute(columns, "col", left)
-    far_top = lax.ppermute(from_left[:half], "col", right)
-    far_bottom = lax.ppermute(from_right[half:], "col", left)
-    far = jnp.concatenate([far_top, far_bottom], axis=0)
+    opposite = lax.ppermute(
+        jnp.where(first_core, far_side, near), "row", [(r, r ^ (2 if r % 2 == 0 else 6)) for r in range(8)]
+    )
+    near_beside, far_beside, opposite_beside = swap(near, 1), swap(far_side, 1), swap(opposite, 1)
+
     info = jnp.concatenate(
         [
             (my_col + jnp.array([0, -1, 1, 2], jnp.int32)) % 4,
@@ -526,7 +524,7 @@
     )
     lhs, own = rows_solve(info, (columns, from_left, from_right, far), wt)
     row = my_row.reshape(1)
-    pieces = (share, beside, near, near_beside, *opposite, *opposite_beside, far_side, far_beside)
+    pieces = (share, beside, near, near_beside, opposite, opposite_beside, far_side, far_beside)
     result = update(row, pieces, lhs, own, base, tile_rows, tile_cols)
     return result.reshape(front.shape)
 

time: 157 us -> 160 us (1.019)
  local copies, waits for them, and re-layouts: 15 us -> 4.85 us
  Pallas kernels: 63.3 us -> 72 us
  waiting for transfers between devices: 45.2 us -> 49.7 us
    unnamed x28 -> x8, local copies, waits for them, and re-layouts: 9.65 us -> 1.05 us
    ppermute x4, waiting for transfers between devices: 1.5 us -> 9.19 us  [the longest x1 5.59 us: local(): lax.ppermute(jnp.where(first_core, far_side, near), 'row', [(r, r ^ (2 if...]
    ppermute x9 -> x6, waiting for transfers between devices: 7.36 us -> 0.02 us  [swap(): return lax.ppermute(x, 'row', [(r, r ^ bits) for r in range(8)])]
    pallas_call x1, Pallas kernels: 6.15 us -> 12.7 us  [rest(): pl.pallas_call(functools.partial(rest_kernel, tile_cols, group), out_shap...]
    all_to_all x1, waiting for transfers between devices: 4.84 us -> 9.07 us  [local(): lax.all_to_all(halves, ('row', 'col'), split_axis=0, concat_axis=0, tiled...]
    slice x4 -> x0, local copies, waits for them, and re-layouts: 2 us -> none  [the longest x2 1.96 us: local(): opposite = [swap(far_side[:cut], 2), swap(near[cut:], 6)]]
    ppermute x9 -> x6, starting transfers between devices: 5.57 us -> 4.85 us  [swap(): return lax.ppermute(x, 'row', [(r, r ^ bits) for r in range(8)])]
  transfers between devices with their start and end apart: 20 -> 17, of which waited for: 9 -> 6; matrix products, arithmetic and copies ran while one was open for 3% -> 2% of each run, Pallas kernels for 29% -> 34%
where the time goes in v6:
time: 160 us; the launch traced here: 159 us
  Pallas kernels  72 us (45%)
  waiting for transfers between devices  49.7 us (31%)
  starting transfers between devices  30 us (19%)
  local copies, waits for them, and re-layouts  4.85 us (3%)
  other arithmetic  2.02 us (1%)
    pallas_call x1, Pallas kernels, leading_inverse(): pl.pallas_call(leading_kernel, out_shape=(jax.ShapeDtypeStruct((4, T, 4 *...  28.2 us
    all_to_all x1, waiting for transfers between devices, local(): lax.all_to_all(send, ('row', 'col'), split_axis=0, concat_axis=0, tiled=T...  24.9 us
    pallas_call x1, Pallas kernels, update(): pl.pallas_call(functools.partial(update_kernel, tile_cols, group), out_sh...  13.1 us
    pallas_call x1, Pallas kernels, rest(): pl.pallas_call(functools.partial(rest_kernel, tile_cols, group), out_shap...  12.7 us
    all_to_all x1, waiting for transfers between devices, local(): lax.all_to_all(halves, ('row', 'col'), split_axis=0, concat_axis=0, tiled...  9.07 us
    all_to_all x1, starting transfers between devices, local(): lax.all_to_all(halves, ('row', 'col'), split_axis=0, concat_axis=0, tiled...  8.42 us
    pallas_call x1, Pallas kernels, route(): pl.pallas_call(functools.partial(route_kernel, group, slot_total, tile_co...  8.05 us
    ppermute x4, starting transfers between devices, local(): parts.append(lax.ppermute(pieces[m], ('row', 'col'), moves))  7.49 us
  transfers between devices with their start and end apart: 17, of which 6 were waited for; matrix products, arithmetic and copies ran while one was open for 2% of the time, Pallas kernels for 34%

profile of v6, /device:TPU:0, one launch (start us, length us, event | category | flops | bytes accessed | tf_op | source)
XLA Modules:
  0.0 158.7 jit_solution(16104538581986924427)
XLA Ops:
  0.8 1.1 broadcast_in_dim.8
  2.0 8.4 %all-to-all-start = ((f32[32,64,128]{2,1,0:T(8,128)}), f32[32,64,128]{2,1,0:T(8,128)S(1)}, u32[]{:S(2)}, u32[]{:S(2)}) async-start(f32[32,64,128]{2,1,0:T(8,128)} %bitcast.2), calls=%async_computation | async-start | bytes 2097152 | tf_op jit(solution)/shard_map/all_to_all | solution.py:478
  10.4 8.0 %route.1 = f32[32,264,128]{2,1,0:T(8,128)} custom-call(s32[32]{0:T(128)} %bitcast.20, s32[32]{0:T(128)} %bitcast.21, f32[32,128,128]{2,1,0:T(8,128)} %bitcast.15, s32[32,128]{1,0:T(8,128)} %bitcast.18, s32[32,128]{1,0:T(8,128)} %bitcast.19), custom_call_target="tpu_custom_call" | custom-call | tf_op jit(solution)/shard_map/route/pallas_call | solution.py:96
  18.4 9.1 %all-to-all-done = f32[32,64,128]{2,1,0:T(8,128)S(1)} async-done(((f32[32,64,128]{2,1,0:T(8,128)}), f32[32,64,128]{2,1,0:T(8,128)S(1)}, u32[]{:S(2)}, u32[]{:S(2)}) %all-to-all-start) | async-done | bytes 1048608 | tf_op jit(solution)/shard_map/all_to_all | solution.py:478
  27.7 1.1 slice.16
  28.8 4.9 %all-to-all-start.1 = ((f32[32,264,128]{2,1,0:T(8,128)}), f32[32,264,128]{2,1,0:T(8,128)}, u32[]{:S(2)}, u32[]{:S(2)}) async-start(f32[32,264,128]{2,1,0:T(8,128)} %route.1), calls=%async_computation.1 | async-start | bytes 8650752 | tf_op jit(solution)/shard_map/all_to_all | solution.py:481
  33.7 28.2 %leading_inverse.1 = (bf16[4,128,512]{2,1,0:T(8,128)(2,1)S(1)}, bf16[4,128,512]{2,1,0:T(8,128)(2,1)S(1)}) custom-call(s32[1]{0:T(128)} %bitcast.10.core_ref, f32[16,64,128]{2,1,0:T(8,128)S(1)} %slice.18.mine_ref, f32[16,64,128]{2,1,0:T(8,128)S(1)} %collective-permute-done.other_ref), custom_call_target="tpu_custom_call" | custom-call | flops 60000002048 | bytes 2000000 | tf_op jit(solution)/shard_map/leading_inverse/pallas_call | solution.py:212
  61.9 24.9 %all-to-all-done.1.got_ref = f32[32,264,128]{2,1,0:T(8,128)} async-done(((f32[32,264,128]{2,1,0:T(8,128)}), f32[32,264,128]{2,1,0:T(8,128)}, u32[]{:S(2)}, u32[]{:S(2)}) %all-to-all-start.1) | async-done | bytes 4325408 | tf_op jit(solution)/shard_map/all_to_all | solution.py:481
  86.8 4.1 %panel.1 = (f32[1152,128]{1,0:T(8,128)}, f32[288,128]{1,0:T(8,128)S(1)}, f32[288,128]{1,0:T(8,128)S(1)}, f32[288,128]{1,0:T(8,128)S(1)}, f32[288,128]{1,0:T(8,128)S(1)}) custom-call(s32[1]{0:T(128)} %bitcast.8.col_ref, f32[32,264,128]{2,1,0:T(8,128)} %all-to-all-done.1.got_ref, f32[1152,128]{1,0:T(8,128)S(1)} %bitcast.14, ...), custom_call_target="tpu_custom_call" | custom-call | tf_op jit(solution)/shard_map/panel/pallas_call | solution.py:279
  91.6 2.4 %collective-permute-start.2 = (f32[288,128]{1,0:T(8,128)S(1)}, f32[288,128]{1,0:T(8,128)S(1)}, u32[]{:S(2)}, u32[]{:S(2)}) collective-permute-start(f32[288,128]{1,0:T(8,128)S(1)} %get-tuple-element.29), channel_id=1, source_target_pairs={{0,4},{1,8},{2,12},{3,0},{4,5},{5,9},{6,13},{7,1},{8,6},{9,10},{10... | collective-permute-start | bytes 442376 | tf_op jit(solution)/shard_map/ppermute | solution.py:491
  94.0 3.2 %collective-permute-start.3 = (f32[288,128]{1,0:T(8,128)S(1)}, f32[288,128]{1,0:T(8,128)S(1)}, u32[]{:S(2)}, u32[]{:S(2)}) collective-permute-start(f32[288,128]{1,0:T(8,128)S(1)} %get-tuple-element.30), channel_id=1, source_target_pairs={{0,8},{1,12},{2,0},{3,4},{4,9},{5,13},{6,1},{7,5},{8,10},{9,14},{1... | collective-permute-start | bytes 442376 | tf_op jit(solution)/shard_map/ppermute | solution.py:491
  97.1 1.3 collective-permute-start.4
  98.4 1.5 collective-permute-done.2.x1
  99.9 5.0 %collective-permute-done.3.x2 = f32[288,128]{1,0:T(8,128)S(1)} collective-permute-done((f32[288,128]{1,0:T(8,128)S(1)}, f32[288,128]{1,0:T(8,128)S(1)}, u32[]{:S(2)}, u32[]{:S(2)}) %collective-permute-start.3) | collective-permute-done | bytes 147488 | tf_op jit(solution)/shard_map/ppermute | solution.py:491
  104.9 1.2 share_solve.1.s0
  106.1 2.7 %collective-permute-start.7 = (f32[288,512]{1,0:T(8,128)S(1)}, f32[288,512]{1,0:T(8,128)S(1)}, u32[]{:S(2)}, u32[]{:S(2)}) collective-permute-start(f32[288,512]{1,0:T(8,128)S(1)} %share_solve.1.s0), channel_id=1, source_target_pairs={{0,24},{4,28},{8,16},{12,20},{16,8},{20,12},{24,0},{28,4},{1,25},{... | collective-permute-start | bytes 1769480 | tf_op jit(solution)/shard_map/ppermute | solution.py:507
  108.8 2.0 %collective-permute-start.12 = (f32[1152,128]{1,0:T(8,128)}, f32[1152,128]{1,0:T(8,128)S(1)}, u32[]{:S(2)}, u32[]{:S(2)}) collective-permute-start(f32[1152,128]{1,0:T(8,128)} %get-tuple-element.37.x0), channel_id=1, source_target_pairs={{0,1},{1,2},{2,3},{3,0},{4,5},{5,6},{6,7},{7,4},{8,9},{9,10},{10,1... | collective-permute-start | bytes 1769480 | tf_op jit(solution)/shard_map/ppermute | solution.py:495
  112.5 12.7 %rest.1.base_ref = f32[20736,128]{1,0:T(8,128)} custom-call(s32[64]{0:T(128)} %convert_element_type.9.slot_ref, f32[32,264,128]{2,1,0:T(8,128)} %all-to-all-done.1.got_ref, f32[20736,128]{1,0:T(8,128)} %bitcast.17), custom_call_target="tpu_custom_call" | custom-call | flops 10000000000 | bytes 26000000 | tf_op jit(solution)/shard_map/rest/pallas_call | solution.py:394
  125.3 2.2 %collective-permute-start.9 = (f32[288,512]{1,0:T(8,128)S(1)}, f32[288,512]{1,0:T(8,128)}, u32[]{:S(2)}, u32[]{:S(2)}) collective-permute-start(f32[288,512]{1,0:T(8,128)S(1)} %broadcast_select_fusion.1), channel_id=1, source_target_pairs={{0,8},{4,28},{8,0},{12,20},{16,24},{20,12},{24,16},{28,4},{1,9},{5... | collective-permute-start | bytes 1769480 | tf_op jit(solution)/shard_map/ppermute | solution.py:514
  128.4 1.1 collective-permute-start.5
  130.0 5.6 %collective-permute-done.9.t0 = f32[288,512]{1,0:T(8,128)} collective-permute-done((f32[288,512]{1,0:T(8,128)S(1)}, f32[288,512]{1,0:T(8,128)}, u32[]{:S(2)}, u32[]{:S(2)}) %collective-permute-start.9) | collective-permute-done | bytes 589856 | tf_op jit(solution)/shard_map/ppermute | solution.py:514
  136.3 3.6 %collective-permute-done.14.x3 = f32[1152,128]{1,0:T(8,128)} collective-permute-done((f32[1152,128]{1,0:T(8,128)}, f32[1152,128]{1,0:T(8,128)}, u32[]{:S(2)}, u32[]{:S(2)}) %collective-permute-start.14) | collective-permute-done | bytes 589856 | tf_op jit(solution)/shard_map/ppermute | solution.py:497
  140.9 4.6 %rows_solve.1 = (bf16[1152,1024]{1,0:T(8,128)(2,1)S(1)}, f32[1152,128]{1,0:T(8,128)S(1)}) custom-call(s32[6]{0:T(128)S(1)} %pad_add_fusion.info_ref, f32[1152,128]{1,0:T(8,128)} %get-tuple-element.37.x0, f32[1152,128]{1,0:T(8,128)S(1)} %collective-permute-done.12.x1, f32[1152,128]{1,0:T(8,128)S(1)} %collective-permute-done.13.x2, ...), custom_call_target="tpu_custom_call" | custom-call | flops 4000000000 | bytes 8000000 | tf_op jit(solution)/shard_map/rows_solve/pallas_call | solution.py:357
  145.5 13.1 %update.1 = f32[20736,128]{1,0:T(8,128)} custom-call(s32[1]{0:T(128)} %bitcast.row_ref, f32[288,512]{1,0:T(8,128)S(1)} %share_solve.1.s0, f32[288,512]{1,0:T(8,128)} %collective-permute-done.5.s1, f32[288,512]{1,0:T(8,128)S(1)} %collective-permute-done.6.s2, f32[288,512]{1,0:T(8,128)} %collective-permute-done.8.s3, f32[288,512]{1,0:T(8,128)} %collective-permute-done.9.t0, ...), custom_call_target="tpu_custom_call" | custom-call | tf_op jit(solution)/shard_map/update/pallas_call | solution.py:446
  (36 shorter events, 6.5 us)
Async XLA Ops:
  2.0 25.5 %all-to-all-start = ((f32[32,64,128]{2,1,0:T(8,128)}), f32[32,64,128]{2,1,0:T(8,128)S(1)}, u32[]{:S(2)}, u32[]{:S(2)}) async-start(f32[32,64,128]{2,1,0:T(8,128)} %bitcast.2), calls=%async_computation | async-start | bytes 2097152 | tf_op jit(solution)/shard_map/all_to_all | solution.py:478
  27.6 6.1 %collective-permute-start = (f32[16,64,128]{2,1,0:T(8,128)S(1)}, f32[16,64,128]{2,1,0:T(8,128)S(1)}, u32[]{:S(2)}, u32[]{:S(2)}) collective-permute-start(f32[16,64,128]{2,1,0:T(8,128)S(1)} %slice.18.mine_ref), channel_id=1, source_target_pairs={{0,4},{4,0},{8,12},{12,8},{16,20},{20,16},{24,28},{28,24},{1,5},{5... | collective-permute-start | bytes 1572872 | tf_op jit(solution)/shard_map/ppermute | solution.py:480
  28.8 58.0 %all-to-all-start.1 = ((f32[32,264,128]{2,1,0:T(8,128)}), f32[32,264,128]{2,1,0:T(8,128)}, u32[]{:S(2)}, u32[]{:S(2)}) async-start(f32[32,264,128]{2,1,0:T(8,128)} %route.1), calls=%async_computation.1 | async-start | bytes 8650752 | tf_op jit(solution)/shard_map/all_to_all | solution.py:481
  61.9 43.0 %copy-start.1 = (bf16[4,128,512]{2,1,0:T(8,128)(2,1)}, bf16[4,128,512]{2,1,0:T(8,128)(2,1)S(1)}, u32[]{:S(2)}) copy-start(bf16[4,128,512]{2,1,0:T(8,128)(2,1)S(1)} %get-tuple-element.32.high_ref) | copy-start | bytes 1572868
  90.9 7.5 %collective-permute-start.1 = (f32[288,128]{1,0:T(8,128)S(1)}, f32[288,128]{1,0:T(8,128)S(1)}, u32[]{:S(2)}, u32[]{:S(2)}) collective-permute-start(f32[288,128]{1,0:T(8,128)S(1)} %get-tuple-element.27), channel_id=1, source_target_pairs={{0,0},{1,4},{2,8},{3,12},{4,1},{5,5},{6,9},{7,13},{8,2},{9,6},{10,... | collective-permute-start | bytes 442376 | tf_op jit(solution)/shard_map/ppermute | solution.py:491
  91.6 8.3 %collective-permute-start.2 = (f32[288,128]{1,0:T(8,128)S(1)}, f32[288,128]{1,0:T(8,128)S(1)}, u32[]{:S(2)}, u32[]{:S(2)}) collective-permute-start(f32[288,128]{1,0:T(8,128)S(1)} %get-tuple-element.29), channel_id=1, source_target_pairs={{0,4},{1,8},{2,12},{3,0},{4,5},{5,9},{6,13},{7,1},{8,6},{9,10},{10... | collective-permute-start | bytes 442376 | tf_op jit(solution)/shard_map/ppermute | solution.py:491
  94.0 11.0 %collective-permute-start.3 = (f32[288,128]{1,0:T(8,128)S(1)}, f32[288,128]{1,0:T(8,128)S(1)}, u32[]{:S(2)}, u32[]{:S(2)}) collective-permute-start(f32[288,128]{1,0:T(8,128)S(1)} %get-tuple-element.30), channel_id=1, source_target_pairs={{0,8},{1,12},{2,0},{3,4},{4,9},{5,13},{6,1},{7,5},{8,10},{9,14},{1... | collective-permute-start | bytes 442376 | tf_op jit(solution)/shard_map/ppermute | solution.py:491
  97.1 7.8 %collective-permute-start.4 = (f32[288,128]{1,0:T(8,128)S(1)}, f32[288,128]{1,0:T(8,128)S(1)}, u32[]{:S(2)}, u32[]{:S(2)}) collective-permute-start(f32[288,128]{1,0:T(8,128)S(1)} %get-tuple-element.31), channel_id=1, source_target_pairs={{0,12},{1,0},{2,4},{3,8},{4,13},{5,1},{6,5},{7,9},{8,14},{9,2},{10... | collective-permute-start | bytes 442376 | tf_op jit(solution)/shard_map/ppermute | solution.py:491
  106.1 19.1 %collective-permute-start.7 = (f32[288,512]{1,0:T(8,128)S(1)}, f32[288,512]{1,0:T(8,128)S(1)}, u32[]{:S(2)}, u32[]{:S(2)}) collective-permute-start(f32[288,512]{1,0:T(8,128)S(1)} %share_solve.1.s0), channel_id=1, source_target_pairs={{0,24},{4,28},{8,16},{12,20},{16,8},{20,12},{24,0},{28,4},{1,25},{... | collective-permute-start | bytes 1769480 | tf_op jit(solution)/shard_map/ppermute | solution.py:507
  108.8 16.4 %collective-permute-start.6 = (f32[288,512]{1,0:T(8,128)S(1)}, f32[288,512]{1,0:T(8,128)S(1)}, u32[]{:S(2)}, u32[]{:S(2)}) collective-permute-start(f32[288,512]{1,0:T(8,128)S(1)} %share_solve.1.s0), channel_id=1, source_target_pairs={{0,8},{4,12},{8,0},{12,4},{16,24},{20,28},{24,16},{28,20},{1,9},{5... | collective-permute-start | bytes 1769480 | tf_op jit(solution)/shard_map/ppermute | solution.py:507
  108.8 18.7 %collective-permute-start.13 = (f32[1152,128]{1,0:T(8,128)}, f32[1152,128]{1,0:T(8,128)S(1)}, u32[]{:S(2)}, u32[]{:S(2)}) collective-permute-start(f32[1152,128]{1,0:T(8,128)} %get-tuple-element.37.x0), channel_id=1, source_target_pairs={{0,3},{1,0},{2,1},{3,2},{4,7},{5,4},{6,5},{7,6},{8,11},{9,8},{10,9... | collective-permute-start | bytes 1769480 | tf_op jit(solution)/shard_map/ppermute | solution.py:496
  108.8 18.7 %collective-permute-start.12 = (f32[1152,128]{1,0:T(8,128)}, f32[1152,128]{1,0:T(8,128)S(1)}, u32[]{:S(2)}, u32[]{:S(2)}) collective-permute-start(f32[1152,128]{1,0:T(8,128)} %get-tuple-element.37.x0), channel_id=1, source_target_pairs={{0,1},{1,2},{2,3},{3,0},{4,5},{5,6},{6,7},{7,4},{8,9},{9,10},{10,1... | collective-permute-start | bytes 1769480 | tf_op jit(solution)/shard_map/ppermute | solution.py:495
  112.5 23.6 %copy-start.3 = (s32[4]{0:T(128)S(1)}, s32[4]{0:T(128)}, u32[]{:S(2)}) copy-start(s32[4]{0:T(128)} %constant.46.clone) | copy-start | bytes 52
  125.3 10.2 %collective-permute-start.9 = (f32[288,512]{1,0:T(8,128)S(1)}, f32[288,512]{1,0:T(8,128)}, u32[]{:S(2)}, u32[]{:S(2)}) collective-permute-start(f32[288,512]{1,0:T(8,128)S(1)} %broadcast_select_fusion.1), channel_id=1, source_target_pairs={{0,8},{4,28},{8,0},{12,20},{16,24},{20,12},{24,16},{28,4},{1,9},{5... | collective-permute-start | bytes 1769480 | tf_op jit(solution)/shard_map/ppermute | solution.py:514
  128.4 11.4 %collective-permute-start.14 = (f32[1152,128]{1,0:T(8,128)}, f32[1152,128]{1,0:T(8,128)}, u32[]{:S(2)}, u32[]{:S(2)}) collective-permute-start(f32[1152,128]{1,0:T(8,128)} %broadcast_select_fusion), channel_id=1, source_target_pairs={{0,1},{1,2},{2,3},{3,0},{4,7},{5,4},{6,5},{7,6},{8,9},{9,10},{10,1... | collective-permute-start | bytes 1769480 | tf_op jit(solution)/shard_map/ppermute | solution.py:497
  128.4 17.0 %collective-permute-start.5 = (f32[288,512]{1,0:T(8,128)S(1)}, f32[288,512]{1,0:T(8,128)}, u32[]{:S(2)}, u32[]{:S(2)}) collective-permute-start(f32[288,512]{1,0:T(8,128)S(1)} %share_solve.1.s0), channel_id=1, source_target_pairs={{0,4},{4,0},{8,12},{12,8},{16,20},{20,16},{24,28},{28,24},{1,5},{5... | collective-permute-start | bytes 1769480 | tf_op jit(solution)/shard_map/ppermute | solution.py:507
  129.5 16.0 %collective-permute-start.8 = (f32[288,512]{1,0:T(8,128)S(1)}, f32[288,512]{1,0:T(8,128)}, u32[]{:S(2)}, u32[]{:S(2)}) collective-permute-start(f32[288,512]{1,0:T(8,128)S(1)} %collective-permute-done.6.s2), channel_id=1, source_target_pairs={{0,4},{4,0},{8,12},{12,8},{16,20},{20,16},{24,28},{28,24},{1,5},{5... | collective-permute-start | bytes 1769480 | tf_op jit(solution)/shard_map/ppermute | solution.py:507
  129.5 16.0 %collective-permute-start.11 = (f32[288,512]{1,0:T(8,128)S(1)}, f32[288,512]{1,0:T(8,128)}, u32[]{:S(2)}, u32[]{:S(2)}) collective-permute-start(f32[288,512]{1,0:T(8,128)S(1)} %collective-permute-done.7.t2), channel_id=1, source_target_pairs={{0,4},{4,0},{8,12},{12,8},{16,20},{20,16},{24,28},{28,24},{1,5},{5... | collective-permute-start | bytes 1769480 | tf_op jit(solution)/shard_map/ppermute | solution.py:507
  135.6 9.9 %collective-permute-start.10 = (f32[288,512]{1,0:T(8,128)}, f32[288,512]{1,0:T(8,128)}, u32[]{:S(2)}, u32[]{:S(2)}) collective-permute-start(f32[288,512]{1,0:T(8,128)} %collective-permute-done.9.t0), channel_id=1, source_target_pairs={{0,4},{4,0},{8,12},{12,8},{16,20},{20,16},{24,28},{28,24},{1,5},{5... | collective-permute-start | bytes 1769480 | tf_op jit(solution)/shard_map/ppermute | solution.py:507
  136.3 9.3 %copy-start = (f32[20736,128]{1,0:T(8,128)S(1)}, f32[20736,128]{1,0:T(8,128)}, u32[]{:S(2)}) copy-start(f32[20736,128]{1,0:T(8,128)} %rest.1.base_ref) | copy-start | bytes 31850500
  139.9 1.0 copy-start.2

commit v7 on v6

--- a/solution.py
+++ b/solution.py
@@ -165,15 +165,16 @@
             e[g] = e[g] - tree_sum([below[g][k] * x[k] for k in range(8)])
 
 
-def leading_kernel(core_ref, mine_ref, other_ref, high_ref, low_ref, s_ref, e_ref, w_ref):
+def leading_kernel(quarter_ref, x0, x1, x2, x3, high_ref, low_ref, lead_ref, s_ref, e_ref, w_ref):
     n = 4
     dot = functools.partial(lax.dot_general, precision=HIGHEST, preferred_element_type=F32)
 
 
+    for d, x in enumerate((x0, x1, x2, x3)):
+        lead_ref[:, pl.ds(pl.multiple_of((quarter_ref[0] ^ d) * 32, 32), 32), :] = x[...]
+
     def tile(i, j):
-        mine, other = mine_ref[4 * i + j], other_ref[4 * i + j]
-        first = core_ref[0] == 0
-        return jnp.concatenate([jnp.where(first, mine, other), jnp.where(first, other, mine)], axis=0)
+        return lead_ref[4 * i + j]
 
     for i in range(n):
         for j in range(i + 1):
@@ -208,16 +209,17 @@
     lax.fori_loop(0, n, step, 0)
 
 
-def leading_inverse(core, mine, other):
+def leading_inverse(quarter, parts):
     return pl.pallas_call(
         leading_kernel,
         out_shape=(jax.ShapeDtypeStruct((4, T, 4 * T), BF16),) * 2,
         grid_spec=pltpu.PrefetchScalarGridSpec(
             num_scalar_prefetch=1,
             grid=(),
-            in_specs=[VM(), VM()],
+            in_specs=[VM()] * 4,
             out_specs=(VM(), VM()),
             scratch_shapes=[
+                pltpu.VMEM((16, T, T), F32),
                 pltpu.VMEM((4, 4, T, T), F32),
                 pltpu.VMEM((4, T, 4 * T), F32),
                 pltpu.VMEM((T, T), F32),
@@ -226,7 +228,7 @@
         compiler_params=params(16),
         cost_estimate=pl.CostEstimate(flops=60_000_000_000, bytes_accessed=2_000_000, transcendentals=0),
         name="leading_inverse",
-    )(core, mine, other)
+    )(quarter, *parts)
 
 
 def panel_kernel(col_ref, got_ref, base_ref, after_ref, out_ref, p0, p1, p2, p3, held, places, sem):
@@ -332,50 +334,18 @@
     )(order, *parts, *wt)
 
 
-def rows_kernel(info_ref, x0, x1, x2, x3, high_ref, low_ref, lhs_ref, own_ref, rhs_ref):
-    load_rhs(info_ref, high_ref, low_ref, rhs_ref)
-    my_col, zero_first = info_ref[4], info_ref[5]
-    chunk = 3 * T
-    for c in range(x0.shape[0] // chunk):
-        at = slice(c * chunk, (c + 1) * chunk)
-        total = times_wt([x[at, :] for x in (x0, x1, x2, x3)], rhs_ref)
-        for j in range(4):
-            @pl.when(my_col == j)
-            def _():
-                own_ref[at, :] = total[:, j * T : (j + 1) * T]
-
-        if c == 0:
-            row = lax.broadcasted_iota(jnp.int32, total.shape, 0)
-            total = jnp.where((row < T) & (zero_first == 1), 0.0, total)
-        high, low = split(total)
-        lhs_ref[at, 0:512] = high
-        lhs_ref[at, 512:1024] = low
-
-
-def rows_solve(info, parts, wt):
-    rows = parts[0].shape[0]
-    return pl.pallas_call(
-        rows_kernel,
-        out_shape=(jax.ShapeDtypeStruct((rows, 8 * T), BF16), jax.ShapeDtypeStruct((rows, T), F32)),
-        grid_spec=pltpu.PrefetchScalarGridSpec(
-            num_scalar_prefetch=1,
-            grid=(),
-            in_specs=[VM()] * 6,
-            out_specs=(VM(), VM()),
-            scratch_shapes=[pltpu.VMEM((12 * T, 4 * T), BF16)],
-        ),
-        compiler_params=params(28),
-        cost_estimate=pl.CostEstimate(flops=4_000_000_000, bytes_accessed=8_000_000, transcendentals=0),
-        name="rows_solve",
-    )(info, *parts, *wt)
-
-
-def rest_kernel(tile_cols, group, slot_ref, got_ref, base_ref, out_ref):
+def rest_kernel(tile_cols, group, marks_ref, got_ref, base_ref, out_ref, slots, sem):
+    @pl.when(pl.program_id(0) == 0)
+    def _():
+        look = pltpu.make_async_copy(marks_ref.at[:, 2 * T, :], slots, sem)
+        look.start()
+        look.wait()
+
     out_ref[...] = base_ref[...]
     first = pl.program_id(0) * group * tile_cols
 
     def step(n, _):
-        slot = slot_ref[n] - first
+        slot = slots[n // 2, n % 2].astype(jnp.int32) - first
 
         @pl.when((slot >= 0) & (slot < group * tile_cols))
         def _():
@@ -384,26 +354,24 @@
 
         return 0
 
-    lax.fori_loop(0, slot_ref.shape[0], step, 0, unroll=4)
-
-
-def rest(slots, got, base, tile_rows, tile_cols):
+    lax.fori_loop(0, 2 * slots.shape[0], step, 0, unroll=4)
+
+
+def rest(got, base, tile_rows, tile_cols):
     group = 3
     size = group * T * tile_cols
-    block = pl.BlockSpec((size, T), lambda a, s: (a, 0))
+    block = pl.BlockSpec((size, T), lambda a: (a, 0))
     return pl.pallas_call(
         functools.partial(rest_kernel, tile_cols, group),
         out_shape=jax.ShapeDtypeStruct(base.shape, F32),
-        grid_spec=pltpu.PrefetchScalarGridSpec(
-            num_scalar_prefetch=1,
-            grid=(tile_rows // group,),
-            in_specs=[pl.BlockSpec(got.shape, lambda a, s: (0, 0, 0)), block],
-            out_specs=block,
-        ),
+        grid=(tile_rows // group,),
+        in_specs=[ANY(), pl.BlockSpec(got.shape, lambda a: (0, 0, 0)), block],
+        out_specs=block,
+        scratch_shapes=[pltpu.SMEM((got.shape[0], T), F32), pltpu.SemaphoreType.DMA],
         compiler_params=params(54),
         cost_estimate=pl.CostEstimate(flops=10_000_000_000, bytes_accessed=26_000_000, transcendentals=0),
         name="rest",
-    )(slots, got, base)
+    )(got, got, base)
 
 
 def load_columns(h, k, pieces, rhs_ref):
@@ -416,16 +384,26 @@
             rhs_ref[at, 512:1024] = low
 
 
-def update_kernel(tile_cols, group, row_ref, s0, s1, s2, s3, t0, t1, t2, t3, lhs_ref, own_ref, base_ref, out_ref, rhs_ref):
-    h, k = row_ref[0] // 4, row_ref[0] % 4
+def update_kernel(
+    tile_cols, group, info_ref, s0, s1, s2, s3, t0, t1, t2, t3, x0, x1, x2, x3, high_ref, low_ref, base_ref, out_ref, wt_ref, rhs_ref
+):
+    my_col, my_row = info_ref[4], info_ref[5]
+    h, k = my_row // 4, my_row % 4
 
     @pl.when(pl.program_id(0) == 0)
     def _():
+        load_rhs(info_ref, high_ref, low_ref, wt_ref)
         load_columns(h, k, (s0, s1, s2, s3), rhs_ref)
         load_columns(1 - h, k, (t0, t1, t2, t3), rhs_ref)
 
-    both = lhs_ref[...]
-    lhs = jnp.concatenate([both[:, 0:512], both], axis=1)
+    panel_rows = times_wt([x[...] for x in (x0, x1, x2, x3)], wt_ref)
+    own = panel_rows[:, 0:T]
+    for j in range(1, 4):
+        own = jnp.where(my_col == j, panel_rows[:, j * T : (j + 1) * T], own)
+    row = lax.broadcasted_iota(jnp.int32, panel_rows.shape, 0)
+    leading = (pl.program_id(0) == 0) & (my_row < 4)
+    high, low = split(jnp.where((row < T) & leading, 0.0, panel_rows))
+    lhs = jnp.concatenate([high, high, low], axis=1)
     for q in range(0, tile_cols, 2):
         rhs = rhs_ref[q * T : (q + 2) * T, :]
         rhs = jnp.concatenate([rhs, rhs[:, 0:512]], axis=1)
@@ -434,12 +412,12 @@
             for b in (q, q + 1):
                 at = pl.ds(a * T * tile_cols + b, T, stride=tile_cols)
                 if b == 0:
-                    out_ref[at, :] = own_ref[a * T : (a + 1) * T, :]
+                    out_ref[at, :] = own[a * T : (a + 1) * T, :]
                 else:
                     out_ref[at, :] = base_ref[at, :] - u[a * T : (a + 1) * T, (b - q) * T : (b - q + 1) * T]
 
 
-def update(row, pieces, lhs, own, base, tile_rows, tile_cols):
+def update(info, pieces, parts, wt, base, tile_rows, tile_cols):
     group = 3
     size = group * T * tile_cols
     block = pl.BlockSpec((size, T), lambda a, *_: (a, 0))
@@ -450,17 +428,15 @@
             num_scalar_prefetch=1,
             grid=(tile_rows // group,),
             in_specs=[pl.BlockSpec(x.shape, lambda a, *_: (0, 0)) for x in pieces]
-            + [
-                pl.BlockSpec((group * T, 8 * T), lambda a, *_: (a, 0)),
-                pl.BlockSpec((group * T, T), lambda a, *_: (a, 0)),
-                block,
-            ],
+            + [pl.BlockSpec((group * T, T), lambda a, *_: (a, 0))] * 4
+            + [pl.BlockSpec(x.shape, lambda a, *_: (0, 0, 0)) for x in wt]
+            + [block],
             out_specs=block,
-            scratch_shapes=[pltpu.VMEM((tile_cols * T, 8 * T), BF16)],
+            scratch_shapes=[pltpu.VMEM((12 * T, 4 * T), BF16), pltpu.VMEM((tile_cols * T, 8 * T), BF16)],
         ),
-        compiler_params=params(36),
+        compiler_params=params(42),
         name="update",
-    )(row, *pieces, lhs, own, base)
+    )(info, *pieces, *parts, *wt, base)
 
 
 def local(front, child_updates, child_owner, child_rows, child_cols, child_slot):
@@ -469,17 +445,17 @@
     tile_rows, tile_cols = front.shape[1], front.shape[4]
     slot_total = tile_rows * tile_cols
     flat = front.reshape(tile_rows * T * tile_cols, T)
-    base_panel = front[0, :, 0, :, 0, 0, :].reshape(tile_rows * T, T)
 
     send = route(child_owner[0, :, 0], child_slot[0], child_updates[0], child_rows[0], child_cols[0], 32, slot_total, tile_cols)
 
-    tile = base_panel[:T].reshape(1, 2, 1, T // 2, T)
-    halves = jnp.broadcast_to(tile, (4, 2, 4, T // 2, T)).reshape(32, T // 2, T)
-    mine = lax.all_to_all(halves, ("row", "col"), split_axis=0, concat_axis=0, tiled=True)[:16]
+    tile = front[0, 0, 0, :, 0, 0, :].reshape(1, 4, 1, T // 4, T)
+    quarters = jnp.broadcast_to(tile, (2, 4, 4, T // 4, T)).reshape(32, T // 4, T)
+    mine = lax.all_to_all(quarters, ("row", "col"), split_axis=0, concat_axis=0, tiled=True)[:16]
     mine, send = lax.optimization_barrier((mine, send))
-    other = lax.ppermute(mine, "row", [(r, r ^ 1) for r in range(8)])
+    lead = [mine] + [lax.ppermute(mine, "row", [(r, r ^ d) for r in range(8)]) for d in (1, 2, 3)]
     got = lax.all_to_all(send, ("row", "col"), split_axis=0, concat_axis=0, tiled=True)
-    wt = leading_inverse((my_row % 2).reshape(1), mine, other)
+    wt = leading_inverse((my_row % 4).reshape(1), lead)
+    base_panel = lax.optimization_barrier((front, lead[1]))[0][0, :, 0, :, 0, 0, :].reshape(tile_rows * T, T)
 
     columns, *pieces = panel(my_col.reshape(1), got, base_panel, wt[1])
 
@@ -508,24 +484,16 @@
 
     near, far_side = swap(share, 2), swap(share, 6)
     beside = swap(share, 1)
-    slots = got[:, 2 * T, 0:2].astype(jnp.int32).reshape(64)
-    base = rest(slots, got, flat, tile_rows, tile_cols)
+    base = rest(got, flat, tile_rows, tile_cols)
     near, far_side, base = lax.optimization_barrier((near, far_side, base))
     opposite = lax.ppermute(
         jnp.where(first_core, far_side, near), "row", [(r, r ^ (2 if r % 2 == 0 else 6)) for r in range(8)]
     )
     near_beside, far_beside, opposite_beside = swap(near, 1), swap(far_side, 1), swap(opposite, 1)
 
-    info = jnp.concatenate(
-        [
-            (my_col + jnp.array([0, -1, 1, 2], jnp.int32)) % 4,
-            jnp.stack([my_col, (my_row < 4).astype(jnp.int32)]).astype(jnp.int32),
-        ]
-    )
-    lhs, own = rows_solve(info, (columns, from_left, from_right, far), wt)
-    row = my_row.reshape(1)
-    pieces = (share, beside, near, near_beside, opposite, opposite_beside, far_side, far_beside)
-    result = update(row, pieces, lhs, own, base, tile_rows, tile_cols)
+    info = jnp.concatenate([(my_col + jnp.array([0, -1, 1, 2], jnp.int32)) % 4, jnp.stack([my_col, my_row])])
+    shares = (share, beside, near, near_beside, opposite, opposite_beside, far_side, far_beside)
+    result = update(info, shares, (columns, from_left, from_right, far), wt, base, tile_rows, tile_cols)
     return result.reshape(front.shape)
 
 

time: 160 us -> 158 us (0.988)
  starting transfers between devices: 30 us -> 35.9 us
  waiting for transfers between devices: 49.7 us -> 46 us
  local copies, waits for them, and re-layouts: 4.85 us -> 2.83 us
  other arithmetic: 2.02 us -> 0.26 us
    ppermute x1 -> x3, waiting for transfers between devices: 0.01 us -> 6.72 us  [local(): lax.ppermute(mine, 'row', [(r, r ^ d) for r in range(8)])]
    all_to_all x1, waiting for transfers between devices: 9.07 us -> 3.73 us  [local(): lax.all_to_all(quarters, ('row', 'col'), split_axis=0, concat_axis=0, til...]
    pallas_call x1 -> x0, Pallas kernels: 4.58 us -> none  [rows_solve(): pl.pallas_call(rows_kernel, out_shape=(jax.ShapeDtypeStruct((rows, 8 * T)...]
    pallas_call x1, Pallas kernels: 13.1 us -> 17.3 us  [update(): pl.pallas_call(functools.partial(update_kernel, tile_cols, group), out_sh...]
    all_to_all x1, waiting for transfers between devices: 24.9 us -> 22.1 us  [local(): lax.all_to_all(send, ('row', 'col'), split_axis=0, concat_axis=0, tiled=T...]
    ppermute x4, starting transfers between devices: 7.49 us -> 10.1 us  [local(): parts.append(lax.ppermute(pieces[m], ('row', 'col'), moves))]
    ppermute x1 -> x3, starting transfers between devices: 0.09 us -> 2.23 us  [local(): lax.ppermute(mine, 'row', [(r, r ^ d) for r in range(8)])]
    ppermute x1, starting transfers between devices: 0.01 us -> 1.88 us  [local(): lax.ppermute(columns, 'col', [(c, (c - 1) % 4) for c in range(4)])]
  transfers between devices with their start and end apart: 17 -> 19, of which waited for: 6 -> 7; matrix products, arithmetic and copies ran while one was open for 2% -> 1% of each run, Pallas kernels for 34% -> 32%
where the time goes in v7:
time: 158 us
  Pallas kernels  72.4 us (46%)
  waiting for transfers between devices  46 us (29%)
  starting transfers between devices  35.9 us (23%)
  local copies, waits for them, and re-layouts  2.83 us (2%)
    pallas_call x1, Pallas kernels, leading_inverse(): pl.pallas_call(leading_kernel, out_shape=(jax.ShapeDtypeStruct((4, T, 4 *...  28.3 us
    all_to_all x1, waiting for transfers between devices, local(): lax.all_to_all(send, ('row', 'col'), split_axis=0, concat_axis=0, tiled=T...  22.1 us
    pallas_call x1, Pallas kernels, update(): pl.pallas_call(functools.partial(update_kernel, tile_cols, group), out_sh...  17.3 us
    pallas_call x1, Pallas kernels, rest(): pl.pallas_call(functools.partial(rest_kernel, tile_cols, group), out_shap...  14.2 us
    ppermute x4, starting transfers between devices, local(): parts.append(lax.ppermute(pieces[m], ('row', 'col'), moves))  10.1 us
    all_to_all x1, starting transfers between devices, local(): lax.all_to_all(quarters, ('row', 'col'), split_axis=0, concat_axis=0, til...  8.42 us
    pallas_call x1, Pallas kernels, route(): pl.pallas_call(functools.partial(route_kernel, group, slot_total, tile_co...  8.05 us
    ppermute x3, waiting for transfers between devices, local(): lax.ppermute(mine, 'row', [(r, r ^ d) for r in range(8)])  6.72 us
  transfers between devices with their start and end apart: 19, of which 7 were waited for; matrix products, arithmetic and copies ran while one was open for 1% of the time, Pallas kernels for 32%

profile of v7, /device:TPU:0, one launch (start us, length us, event | category | flops | bytes accessed | tf_op | source)
XLA Modules:
  0.0 157.6 jit_solution(17880551809733974869)
XLA Ops:
  0.8 0.9 broadcast_in_dim.8
  1.7 8.4 %all-to-all-start = ((f32[32,32,128]{2,1,0:T(8,128)}), f32[32,32,128]{2,1,0:T(8,128)S(1)}, u32[]{:S(2)}, u32[]{:S(2)}) async-start(f32[32,32,128]{2,1,0:T(8,128)} %bitcast.3), calls=%async_computation | async-start | bytes 1048576 | tf_op jit(solution)/shard_map/all_to_all | solution.py:453
  10.1 8.0 %route.1 = f32[32,264,128]{2,1,0:T(8,128)} custom-call(s32[32]{0:T(128)} %bitcast.19, s32[32]{0:T(128)} %bitcast.20, f32[32,128,128]{2,1,0:T(8,128)} %bitcast.14, s32[32,128]{1,0:T(8,128)} %bitcast.17, s32[32,128]{1,0:T(8,128)} %bitcast.18), custom_call_target="tpu_custom_call" | custom-call | tf_op jit(solution)/shard_map/route/pallas_call | solution.py:96
  18.2 3.7 %all-to-all-done = f32[32,32,128]{2,1,0:T(8,128)S(1)} async-done(((f32[32,32,128]{2,1,0:T(8,128)}), f32[32,32,128]{2,1,0:T(8,128)S(1)}, u32[]{:S(2)}, u32[]{:S(2)}) %all-to-all-start) | async-done | bytes 524320 | tf_op jit(solution)/shard_map/all_to_all | solution.py:453
  22.5 1.6 %collective-permute-start.1 = (f32[16,32,128]{2,1,0:T(8,128)S(1)}, f32[16,32,128]{2,1,0:T(8,128)S(1)}, u32[]{:S(2)}, u32[]{:S(2)}) collective-permute-start(f32[16,32,128]{2,1,0:T(8,128)S(1)} %slice.12.x0), channel_id=1, source_target_pairs={{0,8},{4,12},{8,0},{12,4},{16,24},{20,28},{24,16},{28,20},{1,9},{5... | collective-permute-start | bytes 786440 | tf_op jit(solution)/shard_map/ppermute | solution.py:455
  24.2 4.9 %all-to-all-start.1 = ((f32[32,264,128]{2,1,0:T(8,128)}), f32[32,264,128]{2,1,0:T(8,128)}, u32[]{:S(2)}, u32[]{:S(2)}) async-start(f32[32,264,128]{2,1,0:T(8,128)} %route.1), calls=%async_computation.1 | async-start | bytes 8650752 | tf_op jit(solution)/shard_map/all_to_all | solution.py:456
  29.1 1.1 slice.11
  30.2 6.7 %collective-permute-done.1.x2 = f32[16,32,128]{2,1,0:T(8,128)S(1)} collective-permute-done((f32[16,32,128]{2,1,0:T(8,128)S(1)}, f32[16,32,128]{2,1,0:T(8,128)S(1)}, u32[]{:S(2)}, u32[]{:S(2)}) %collective-permute-start.1) | collective-permute-done | bytes 262176 | tf_op jit(solution)/shard_map/ppermute | solution.py:455
  36.9 28.3 %leading_inverse.1 = (bf16[4,128,512]{2,1,0:T(8,128)(2,1)S(1)}, bf16[4,128,512]{2,1,0:T(8,128)(2,1)S(1)}) custom-call(s32[1]{0:T(128)} %bitcast.10.quarter_ref, f32[16,32,128]{2,1,0:T(8,128)S(1)} %slice.12.x0, f32[16,32,128]{2,1,0:T(8,128)S(1)} %collective-permute-done.x1, f32[16,32,128]{2,1,0:T(8,128)S(1)} %collective-permute-done.1.x2, ...), custom_call_target="tpu_custom_call" | custom-call | flops 60000002048 | bytes 2000000 | tf_op jit(solution)/shard_map/leading_inverse/pallas_call | solution.py:213
  65.2 22.1 %all-to-all-done.1.got_ref.marks_ref = f32[32,264,128]{2,1,0:T(8,128)} async-done(((f32[32,264,128]{2,1,0:T(8,128)}), f32[32,264,128]{2,1,0:T(8,128)}, u32[]{:S(2)}, u32[]{:S(2)}) %all-to-all-start.1) | async-done | bytes 4325408 | tf_op jit(solution)/shard_map/all_to_all | solution.py:456
  87.3 3.4 %panel.1 = (f32[1152,128]{1,0:T(8,128)S(1)}, f32[288,128]{1,0:T(8,128)S(1)}, f32[288,128]{1,0:T(8,128)S(1)}, f32[288,128]{1,0:T(8,128)S(1)}, f32[288,128]{1,0:T(8,128)S(1)}) custom-call(s32[1]{0:T(128)} %bitcast.col_ref, f32[32,264,128]{2,1,0:T(8,128)} %all-to-all-done.1.got_ref.marks_ref, f32[1152,128]{1,0:T(8,128)S(1)} %bitcast.13, ...), custom_call_target="tpu_custom_call" | custom-call | tf_op jit(solution)/shard_map/panel/pallas_call | solution.py:281
  91.4 1.1 collective-permute-start.4
  92.5 5.1 %collective-permute-start.5 = (f32[288,128]{1,0:T(8,128)S(1)}, f32[288,128]{1,0:T(8,128)S(1)}, u32[]{:S(2)}, u32[]{:S(2)}) collective-permute-start(f32[288,128]{1,0:T(8,128)S(1)} %get-tuple-element.30), channel_id=1, source_target_pairs={{0,8},{1,12},{2,0},{3,4},{4,9},{5,13},{6,1},{7,5},{8,10},{9,14},{1... | collective-permute-start | bytes 442376 | tf_op jit(solution)/shard_map/ppermute | solution.py:467
  97.6 3.2 %collective-permute-start.6 = (f32[288,128]{1,0:T(8,128)S(1)}, f32[288,128]{1,0:T(8,128)S(1)}, u32[]{:S(2)}, u32[]{:S(2)}) collective-permute-start(f32[288,128]{1,0:T(8,128)S(1)} %get-tuple-element.31), channel_id=1, source_target_pairs={{0,12},{1,0},{2,4},{3,8},{4,13},{5,1},{6,5},{7,9},{8,14},{9,2},{10... | collective-permute-start | bytes 442376 | tf_op jit(solution)/shard_map/ppermute | solution.py:467
  101.1 5.0 %collective-permute-done.5.x2 = f32[288,128]{1,0:T(8,128)S(1)} collective-permute-done((f32[288,128]{1,0:T(8,128)S(1)}, f32[288,128]{1,0:T(8,128)S(1)}, u32[]{:S(2)}, u32[]{:S(2)}) %collective-permute-start.5) | collective-permute-done | bytes 147488 | tf_op jit(solution)/shard_map/ppermute | solution.py:467
  106.1 1.2 share_solve.1.s0
  107.3 2.7 %collective-permute-start.9 = (f32[288,512]{1,0:T(8,128)S(1)}, f32[288,512]{1,0:T(8,128)S(1)}, u32[]{:S(2)}, u32[]{:S(2)}) collective-permute-start(f32[288,512]{1,0:T(8,128)S(1)} %share_solve.1.s0), channel_id=1, source_target_pairs={{0,24},{4,28},{8,16},{12,20},{16,8},{20,12},{24,0},{28,4},{1,25},{... | collective-permute-start | bytes 1769480 | tf_op jit(solution)/shard_map/ppermute | solution.py:483
  110.4 1.9 %collective-permute-start.15 = (f32[1152,128]{1,0:T(8,128)S(1)}, f32[1152,128]{1,0:T(8,128)S(1)}, u32[]{:S(2)}, u32[]{:S(2)}) collective-permute-start(f32[1152,128]{1,0:T(8,128)S(1)} %get-tuple-element.37.x0), channel_id=1, source_target_pairs={{0,3},{1,0},{2,1},{3,2},{4,7},{5,4},{6,5},{7,6},{8,11},{9,8},{10,9... | collective-permute-start | bytes 1769480 | tf_op jit(solution)/shard_map/ppermute | solution.py:472
  112.4 14.2 %rest.1.base_ref = f32[20736,128]{1,0:T(8,128)} custom-call(f32[32,264,128]{2,1,0:T(8,128)} %all-to-all-done.1.got_ref.marks_ref, f32[32,264,128]{2,1,0:T(8,128)} %all-to-all-done.1.got_ref.marks_ref, f32[20736,128]{1,0:T(8,128)} %bitcast.16), custom_call_target="tpu_custom_call" | custom-call | flops 10000000000 | bytes 26000000 | tf_op jit(solution)/shard_map/rest/pallas_call | solution.py:364
  126.8 1.8 %collective-permute-start.11 = (f32[288,512]{1,0:T(8,128)S(1)}, f32[288,512]{1,0:T(8,128)S(1)}, u32[]{:S(2)}, u32[]{:S(2)}) collective-permute-start(f32[288,512]{1,0:T(8,128)S(1)} %broadcast_select_fusion.1), channel_id=1, source_target_pairs={{0,8},{4,28},{8,0},{12,20},{16,24},{20,12},{24,16},{28,4},{1,9},{5... | collective-permute-start | bytes 1769480 | tf_op jit(solution)/shard_map/ppermute | solution.py:489
  129.2 2.3 %collective-permute-start.13 = (f32[288,512]{1,0:T(8,128)S(1)}, f32[288,512]{1,0:T(8,128)S(1)}, u32[]{:S(2)}, u32[]{:S(2)}) collective-permute-start(f32[288,512]{1,0:T(8,128)S(1)} %collective-permute-done.9.t2), channel_id=1, source_target_pairs={{0,4},{4,0},{8,12},{12,8},{16,20},{20,16},{24,28},{28,24},{1,5},{5... | collective-permute-start | bytes 1769480 | tf_op jit(solution)/shard_map/ppermute | solution.py:483
  131.5 5.3 %collective-permute-done.11.t0 = f32[288,512]{1,0:T(8,128)S(1)} collective-permute-done((f32[288,512]{1,0:T(8,128)S(1)}, f32[288,512]{1,0:T(8,128)S(1)}, u32[]{:S(2)}, u32[]{:S(2)}) %collective-permute-start.11) | collective-permute-done | bytes 589856 | tf_op jit(solution)/shard_map/ppermute | solution.py:489
  137.4 2.9 %collective-permute-done.16.x3 = f32[1152,128]{1,0:T(8,128)S(1)} collective-permute-done((f32[1152,128]{1,0:T(8,128)S(1)}, f32[1152,128]{1,0:T(8,128)S(1)}, u32[]{:S(2)}, u32[]{:S(2)}) %collective-permute-start.16) | collective-permute-done | bytes 589856 | tf_op jit(solution)/shard_map/ppermute | solution.py:473
  140.3 17.3 %update.1 = f32[20736,128]{1,0:T(8,128)} custom-call(s32[6]{0:T(128)S(1)} %pad_add_fusion.info_ref, f32[288,512]{1,0:T(8,128)S(1)} %share_solve.1.s0, f32[288,512]{1,0:T(8,128)S(1)} %collective-permute-done.7.s1, f32[288,512]{1,0:T(8,128)S(1)} %collective-permute-done.8.s2, f32[288,512]{1,0:T(8,128)S(1)} %collective-permute-done.10.s3, ...), custom_call_target="tpu_custom_call" | custom-call | tf_op jit(solution)/shard_map/update/pallas_call | solution.py:424
  (31 shorter events, 4.4 us)
Async XLA Ops:
  1.7 20.2 %all-to-all-start = ((f32[32,32,128]{2,1,0:T(8,128)}), f32[32,32,128]{2,1,0:T(8,128)S(1)}, u32[]{:S(2)}, u32[]{:S(2)}) async-start(f32[32,32,128]{2,1,0:T(8,128)} %bitcast.3), calls=%async_computation | async-start | bytes 1048576 | tf_op jit(solution)/shard_map/all_to_all | solution.py:453
  21.9 7.1 %collective-permute-start = (f32[16,32,128]{2,1,0:T(8,128)S(1)}, f32[16,32,128]{2,1,0:T(8,128)S(1)}, u32[]{:S(2)}, u32[]{:S(2)}) collective-permute-start(f32[16,32,128]{2,1,0:T(8,128)S(1)} %slice.12.x0), channel_id=1, source_target_pairs={{0,4},{4,0},{8,12},{12,8},{16,20},{20,16},{24,28},{28,24},{1,5},{5... | collective-permute-start | bytes 786440 | tf_op jit(solution)/shard_map/ppermute | solution.py:455
  22.0 8.1 %collective-permute-start.2 = (f32[16,32,128]{2,1,0:T(8,128)S(1)}, f32[16,32,128]{2,1,0:T(8,128)S(1)}, u32[]{:S(2)}, u32[]{:S(2)}) collective-permute-start(f32[16,32,128]{2,1,0:T(8,128)S(1)} %slice.12.x0), channel_id=1, source_target_pairs={{0,12},{4,8},{8,4},{12,0},{16,28},{20,24},{24,20},{28,16},{1,13},{... | collective-permute-start | bytes 786440 | tf_op jit(solution)/shard_map/ppermute | solution.py:455
  22.5 14.3 %collective-permute-start.1 = (f32[16,32,128]{2,1,0:T(8,128)S(1)}, f32[16,32,128]{2,1,0:T(8,128)S(1)}, u32[]{:S(2)}, u32[]{:S(2)}) collective-permute-start(f32[16,32,128]{2,1,0:T(8,128)S(1)} %slice.12.x0), channel_id=1, source_target_pairs={{0,8},{4,12},{8,0},{12,4},{16,24},{20,28},{24,16},{28,20},{1,9},{5... | collective-permute-start | bytes 786440 | tf_op jit(solution)/shard_map/ppermute | solution.py:455
  24.2 63.1 %all-to-all-start.1 = ((f32[32,264,128]{2,1,0:T(8,128)}), f32[32,264,128]{2,1,0:T(8,128)}, u32[]{:S(2)}, u32[]{:S(2)}) async-start(f32[32,264,128]{2,1,0:T(8,128)} %route.1), calls=%async_computation.1 | async-start | bytes 8650752 | tf_op jit(solution)/shard_map/all_to_all | solution.py:456
  90.7 10.1 %collective-permute-start.3 = (f32[288,128]{1,0:T(8,128)S(1)}, f32[288,128]{1,0:T(8,128)S(1)}, u32[]{:S(2)}, u32[]{:S(2)}) collective-permute-start(f32[288,128]{1,0:T(8,128)S(1)} %get-tuple-element.27), channel_id=1, source_target_pairs={{0,0},{1,4},{2,8},{3,12},{4,1},{5,5},{6,9},{7,13},{8,2},{9,6},{10,... | collective-permute-start | bytes 442376 | tf_op jit(solution)/shard_map/ppermute | solution.py:467
  91.4 9.7 %collective-permute-start.4 = (f32[288,128]{1,0:T(8,128)S(1)}, f32[288,128]{1,0:T(8,128)S(1)}, u32[]{:S(2)}, u32[]{:S(2)}) collective-permute-start(f32[288,128]{1,0:T(8,128)S(1)} %get-tuple-element.29), channel_id=1, source_target_pairs={{0,4},{1,8},{2,12},{3,0},{4,5},{5,9},{6,13},{7,1},{8,6},{9,10},{10... | collective-permute-start | bytes 442376 | tf_op jit(solution)/shard_map/ppermute | solution.py:467
  92.5 13.7 %collective-permute-start.5 = (f32[288,128]{1,0:T(8,128)S(1)}, f32[288,128]{1,0:T(8,128)S(1)}, u32[]{:S(2)}, u32[]{:S(2)}) collective-permute-start(f32[288,128]{1,0:T(8,128)S(1)} %get-tuple-element.30), channel_id=1, source_target_pairs={{0,8},{1,12},{2,0},{3,4},{4,9},{5,13},{6,1},{7,5},{8,10},{9,14},{1... | collective-permute-start | bytes 442376 | tf_op jit(solution)/shard_map/ppermute | solution.py:467
  97.6 8.5 %collective-permute-start.6 = (f32[288,128]{1,0:T(8,128)S(1)}, f32[288,128]{1,0:T(8,128)S(1)}, u32[]{:S(2)}, u32[]{:S(2)}) collective-permute-start(f32[288,128]{1,0:T(8,128)S(1)} %get-tuple-element.31), channel_id=1, source_target_pairs={{0,12},{1,0},{2,4},{3,8},{4,13},{5,1},{6,5},{7,9},{8,14},{9,2},{10... | collective-permute-start | bytes 442376 | tf_op jit(solution)/shard_map/ppermute | solution.py:467
  107.3 19.4 %collective-permute-start.9 = (f32[288,512]{1,0:T(8,128)S(1)}, f32[288,512]{1,0:T(8,128)S(1)}, u32[]{:S(2)}, u32[]{:S(2)}) collective-permute-start(f32[288,512]{1,0:T(8,128)S(1)} %share_solve.1.s0), channel_id=1, source_target_pairs={{0,24},{4,28},{8,16},{12,20},{16,8},{20,12},{24,0},{28,4},{1,25},{... | collective-permute-start | bytes 1769480 | tf_op jit(solution)/shard_map/ppermute | solution.py:483
  110.0 16.7 %collective-permute-start.8 = (f32[288,512]{1,0:T(8,128)S(1)}, f32[288,512]{1,0:T(8,128)S(1)}, u32[]{:S(2)}, u32[]{:S(2)}) collective-permute-start(f32[288,512]{1,0:T(8,128)S(1)} %share_solve.1.s0), channel_id=1, source_target_pairs={{0,8},{4,12},{8,0},{12,4},{16,24},{20,28},{24,16},{28,20},{1,9},{5... | collective-permute-start | bytes 1769480 | tf_op jit(solution)/shard_map/ppermute | solution.py:483
  110.4 18.7 %collective-permute-start.15 = (f32[1152,128]{1,0:T(8,128)S(1)}, f32[1152,128]{1,0:T(8,128)S(1)}, u32[]{:S(2)}, u32[]{:S(2)}) collective-permute-start(f32[1152,128]{1,0:T(8,128)S(1)} %get-tuple-element.37.x0), channel_id=1, source_target_pairs={{0,3},{1,0},{2,1},{3,2},{4,7},{5,4},{6,5},{7,6},{8,11},{9,8},{10,9... | collective-permute-start | bytes 1769480 | tf_op jit(solution)/shard_map/ppermute | solution.py:472
  112.3 16.8 %collective-permute-start.14 = (f32[1152,128]{1,0:T(8,128)S(1)}, f32[1152,128]{1,0:T(8,128)S(1)}, u32[]{:S(2)}, u32[]{:S(2)}) collective-permute-start(f32[1152,128]{1,0:T(8,128)S(1)} %get-tuple-element.37.x0), channel_id=1, source_target_pairs={{0,1},{1,2},{2,3},{3,0},{4,5},{5,6},{6,7},{7,4},{8,9},{9,10},{10,1... | collective-permute-start | bytes 1769480 | tf_op jit(solution)/shard_map/ppermute | solution.py:471
  112.4 24.9 %copy-start = (s32[4]{0:T(128)S(1)}, s32[4]{0:T(128)}, u32[]{:S(2)}) copy-start(s32[4]{0:T(128)} %constant.48.clone) | copy-start | bytes 52
  126.8 10.0 %collective-permute-start.11 = (f32[288,512]{1,0:T(8,128)S(1)}, f32[288,512]{1,0:T(8,128)S(1)}, u32[]{:S(2)}, u32[]{:S(2)}) collective-permute-start(f32[288,512]{1,0:T(8,128)S(1)} %broadcast_select_fusion.1), channel_id=1, source_target_pairs={{0,8},{4,28},{8,0},{12,20},{16,24},{20,12},{24,16},{28,4},{1,9},{5... | collective-permute-start | bytes 1769480 | tf_op jit(solution)/shard_map/ppermute | solution.py:489
  128.6 8.8 %collective-permute-start.7 = (f32[288,512]{1,0:T(8,128)S(1)}, f32[288,512]{1,0:T(8,128)S(1)}, u32[]{:S(2)}, u32[]{:S(2)}) collective-permute-start(f32[288,512]{1,0:T(8,128)S(1)} %share_solve.1.s0), channel_id=1, source_target_pairs={{0,4},{4,0},{8,12},{12,8},{16,20},{20,16},{24,28},{28,24},{1,5},{5... | collective-permute-start | bytes 1769480 | tf_op jit(solution)/shard_map/ppermute | solution.py:483
  128.6 11.7 %collective-permute-start.10 = (f32[288,512]{1,0:T(8,128)S(1)}, f32[288,512]{1,0:T(8,128)S(1)}, u32[]{:S(2)}, u32[]{:S(2)}) collective-permute-start(f32[288,512]{1,0:T(8,128)S(1)} %collective-permute-done.8.s2), channel_id=1, source_target_pairs={{0,4},{4,0},{8,12},{12,8},{16,20},{20,16},{24,28},{28,24},{1,5},{5... | collective-permute-start | bytes 1769480 | tf_op jit(solution)/shard_map/ppermute | solution.py:483
  129.2 11.2 %collective-permute-start.16 = (f32[1152,128]{1,0:T(8,128)S(1)}, f32[1152,128]{1,0:T(8,128)S(1)}, u32[]{:S(2)}, u32[]{:S(2)}) collective-permute-start(f32[1152,128]{1,0:T(8,128)S(1)} %broadcast_select_fusion), channel_id=1, source_target_pairs={{0,1},{1,2},{2,3},{3,0},{4,7},{5,4},{6,5},{7,6},{8,9},{9,10},{10,1... | collective-permute-start | bytes 1769480 | tf_op jit(solution)/shard_map/ppermute | solution.py:473
  129.2 11.1 %collective-permute-start.13 = (f32[288,512]{1,0:T(8,128)S(1)}, f32[288,512]{1,0:T(8,128)S(1)}, u32[]{:S(2)}, u32[]{:S(2)}) collective-permute-start(f32[288,512]{1,0:T(8,128)S(1)} %collective-permute-done.9.t2), channel_id=1, source_target_pairs={{0,4},{4,0},{8,12},{12,8},{16,20},{20,16},{24,28},{28,24},{1,5},{5... | collective-permute-start | bytes 1769480 | tf_op jit(solution)/shard_map/ppermute | solution.py:483
  136.8 3.5 %collective-permute-start.12 = (f32[288,512]{1,0:T(8,128)S(1)}, f32[288,512]{1,0:T(8,128)S(1)}, u32[]{:S(2)}, u32[]{:S(2)}) collective-permute-start(f32[288,512]{1,0:T(8,128)S(1)} %collective-permute-done.11.t0), channel_id=1, source_target_pairs={{0,4},{4,0},{8,12},{12,8},{16,20},{20,16},{24,28},{28,24},{1,5},{5... | collective-permute-start | bytes 1769480 | tf_op jit(solution)/shard_map/ppermute | solution.py:483

commit v8 on v7

--- a/solution.py
+++ b/solution.py
@@ -334,18 +334,24 @@
     )(order, *parts, *wt)
 
 
-def rest_kernel(tile_cols, group, marks_ref, got_ref, base_ref, out_ref, slots, sem):
+def rest_kernel(tile_cols, group, marks_ref, got_ref, base_ref, out_ref, marks, slots, sem):
     @pl.when(pl.program_id(0) == 0)
     def _():
-        look = pltpu.make_async_copy(marks_ref.at[:, 2 * T, :], slots, sem)
+        look = pltpu.make_async_copy(marks_ref.at[:, 2 * T, :], marks, sem)
         look.start()
         look.wait()
 
+        def convert(n, _):
+            slots[n] = marks[n // 2, n % 2].astype(jnp.int32)
+            return 0
+
+        lax.fori_loop(0, slots.shape[0], convert, 0, unroll=8)
+
     out_ref[...] = base_ref[...]
     first = pl.program_id(0) * group * tile_cols
 
     def step(n, _):
-        slot = slots[n // 2, n % 2].astype(jnp.int32) - first
+        slot = slots[n] - first
 
         @pl.when((slot >= 0) & (slot < group * tile_cols))
         def _():
@@ -354,7 +360,7 @@
 
         return 0
 
-    lax.fori_loop(0, 2 * slots.shape[0], step, 0, unroll=4)
+    lax.fori_loop(0, slots.shape[0], step, 0, unroll=4)
 
 
 def rest(got, base, tile_rows, tile_cols):
@@ -365,10 +371,14 @@
         functools.partial(rest_kernel, tile_cols, group),
         out_shape=jax.ShapeDtypeStruct(base.shape, F32),
         grid=(tile_rows // group,),
-        in_specs=[ANY(), pl.BlockSpec(got.shape, lambda a: (0, 0, 0)), block],
+        in_specs=[ANY(), pl.BlockSpec(got.shape, lambda a: (0, 0, 0), pipeline_mode=pl.Buffered(1)), block],
         out_specs=block,
-        scratch_shapes=[pltpu.SMEM((got.shape[0], T), F32), pltpu.SemaphoreType.DMA],
-        compiler_params=params(54),
+        scratch_shapes=[
+            pltpu.SMEM((got.shape[0], T), F32),
+            pltpu.SMEM((2 * got.shape[0],), jnp.int32),
+            pltpu.SemaphoreType.DMA,
+        ],
+        compiler_params=params(32),
         cost_estimate=pl.CostEstimate(flops=10_000_000_000, bytes_accessed=26_000_000, transcendentals=0),
         name="rest",
     )(got, got, base)
@@ -427,14 +437,14 @@
         grid_spec=pltpu.PrefetchScalarGridSpec(
             num_scalar_prefetch=1,
             grid=(tile_rows // group,),
-            in_specs=[pl.BlockSpec(x.shape, lambda a, *_: (0, 0)) for x in pieces]
+            in_specs=[pl.BlockSpec(x.shape, lambda a, *_: (0, 0), pipeline_mode=pl.Buffered(1)) for x in pieces]
             + [pl.BlockSpec((group * T, T), lambda a, *_: (a, 0))] * 4
-            + [pl.BlockSpec(x.shape, lambda a, *_: (0, 0, 0)) for x in wt]
+            + [pl.BlockSpec(x.shape, lambda a, *_: (0, 0, 0), pipeline_mode=pl.Buffered(1)) for x in wt]
             + [block],
             out_specs=block,
             scratch_shapes=[pltpu.VMEM((12 * T, 4 * T), BF16), pltpu.VMEM((tile_cols * T, 8 * T), BF16)],
         ),
-        compiler_params=params(42),
+        compiler_params=params(30),
         name="update",
     )(info, *pieces, *parts, *wt, base)
 

time: 158 us -> 156 us (0.987)
  waiting for transfers between devices: 46 us -> 54.2 us
  Pallas kernels: 72.4 us -> 65.4 us
  starting transfers between devices: 35.9 us -> 32.7 us
    pallas_call x1, Pallas kernels: 14.2 us -> 9.28 us  [rest(): pl.pallas_call(functools.partial(rest_kernel, tile_cols, group), out_shap...]
    ppermute x6, waiting for transfers between devices: 0.02 us -> 3.61 us  [swap(): return lax.ppermute(x, 'row', [(r, r ^ bits) for r in range(8)])]
    ppermute x6, starting transfers between devices: 6.42 us -> 3.66 us  [swap(): return lax.ppermute(x, 'row', [(r, r ^ bits) for r in range(8)])]
    pallas_call x1, Pallas kernels: 17.3 us -> 15.3 us  [update(): pl.pallas_call(functools.partial(update_kernel, tile_cols, group), out_sh...]
    ppermute x1, waiting for transfers between devices: 0.01 us -> 1.81 us  [local(): lax.ppermute(columns, 'col', [(c, (c + 1) % 4) for c in range(4)])]
    ppermute x1, waiting for transfers between devices: 2.92 us -> 4.71 us  [local(): lax.ppermute(jnp.where(first_core, from_left, from_right), ('row', 'col')...]
  transfers between devices with their start and end apart: 19 -> 19, of which waited for: 7 -> 10; matrix products, arithmetic and copies ran while one was open for 1% -> 1% of each run, Pallas kernels for 32% -> 29%
where the time goes in v8:
time: 156 us
  Pallas kernels  65.4 us (42%)
  waiting for transfers between devices  54.2 us (35%)
  starting transfers between devices  32.7 us (21%)
  local copies, waits for them, and re-layouts  2.83 us (2%)
    pallas_call x1, Pallas kernels, leading_inverse(): pl.pallas_call(leading_kernel, out_shape=(jax.ShapeDtypeStruct((4, T, 4 *...  28.3 us
    all_to_all x1, waiting for transfers between devices, local(): lax.all_to_all(send, ('row', 'col'), split_axis=0, concat_axis=0, tiled=T...  22.1 us
    pallas_call x1, Pallas kernels, update(): pl.pallas_call(functools.partial(update_kernel, tile_cols, group), out_sh...  15.3 us
    ppermute x4, starting transfers between devices, local(): parts.append(lax.ppermute(pieces[m], ('row', 'col'), moves))  10.2 us
    pallas_call x1, Pallas kernels, rest(): pl.pallas_call(functools.partial(rest_kernel, tile_cols, group), out_shap...  9.28 us
    all_to_all x1, starting transfers between devices, local(): lax.all_to_all(quarters, ('row', 'col'), split_axis=0, concat_axis=0, til...  8.42 us
    pallas_call x1, Pallas kernels, route(): pl.pallas_call(functools.partial(route_kernel, group, slot_total, tile_co...  8.04 us
    ppermute x3, waiting for transfers between devices, local(): lax.ppermute(mine, 'row', [(r, r ^ d) for r in range(8)])  6.73 us
  transfers between devices with their start and end apart: 19, of which 10 were waited for; matrix products, arithmetic and copies ran while one was open for 1% of the time, Pallas kernels for 29%

profile of v8, /device:TPU:0, one launch (start us, length us, event | category | flops | bytes accessed | tf_op | source)
XLA Modules:
  0.0 155.5 jit_solution(3723640458936933764)
XLA Ops:
  1.7 8.4 %all-to-all-start = ((f32[32,32,128]{2,1,0:T(8,128)}), f32[32,32,128]{2,1,0:T(8,128)S(1)}, u32[]{:S(2)}, u32[]{:S(2)}) async-start(f32[32,32,128]{2,1,0:T(8,128)} %bitcast.3), calls=%async_computation | async-start | bytes 1048576 | tf_op jit(solution)/shard_map/all_to_all | solution.py:463
  10.1 8.0 %route.1 = f32[32,264,128]{2,1,0:T(8,128)} custom-call(s32[32]{0:T(128)} %bitcast.19, s32[32]{0:T(128)} %bitcast.20, f32[32,128,128]{2,1,0:T(8,128)} %bitcast.14, s32[32,128]{1,0:T(8,128)} %bitcast.17, s32[32,128]{1,0:T(8,128)} %bitcast.18), custom_call_target="tpu_custom_call" | custom-call | tf_op jit(solution)/shard_map/route/pallas_call | solution.py:96
  18.2 3.7 %all-to-all-done = f32[32,32,128]{2,1,0:T(8,128)S(1)} async-done(((f32[32,32,128]{2,1,0:T(8,128)}), f32[32,32,128]{2,1,0:T(8,128)S(1)}, u32[]{:S(2)}, u32[]{:S(2)}) %all-to-all-start) | async-done | bytes 524320 | tf_op jit(solution)/shard_map/all_to_all | solution.py:463
  22.5 1.6 %collective-permute-start.1 = (f32[16,32,128]{2,1,0:T(8,128)S(1)}, f32[16,32,128]{2,1,0:T(8,128)S(1)}, u32[]{:S(2)}, u32[]{:S(2)}) collective-permute-start(f32[16,32,128]{2,1,0:T(8,128)S(1)} %slice.12.x0), channel_id=1, source_target_pairs={{0,8},{4,12},{8,0},{12,4},{16,24},{20,28},{24,16},{28,20},{1,9},{5... | collective-permute-start | bytes 786440 | tf_op jit(solution)/shard_map/ppermute | solution.py:465
  24.2 4.9 %all-to-all-start.1 = ((f32[32,264,128]{2,1,0:T(8,128)}), f32[32,264,128]{2,1,0:T(8,128)}, u32[]{:S(2)}, u32[]{:S(2)}) async-start(f32[32,264,128]{2,1,0:T(8,128)} %route.1), calls=%async_computation.1 | async-start | bytes 8650752 | tf_op jit(solution)/shard_map/all_to_all | solution.py:466
  29.0 1.1 slice.11
  30.2 6.7 %collective-permute-done.1.x2 = f32[16,32,128]{2,1,0:T(8,128)S(1)} collective-permute-done((f32[16,32,128]{2,1,0:T(8,128)S(1)}, f32[16,32,128]{2,1,0:T(8,128)S(1)}, u32[]{:S(2)}, u32[]{:S(2)}) %collective-permute-start.1) | collective-permute-done | bytes 262176 | tf_op jit(solution)/shard_map/ppermute | solution.py:465
  36.9 28.3 %leading_inverse.1 = (bf16[4,128,512]{2,1,0:T(8,128)(2,1)S(1)}, bf16[4,128,512]{2,1,0:T(8,128)(2,1)S(1)}) custom-call(s32[1]{0:T(128)} %bitcast.10.quarter_ref, f32[16,32,128]{2,1,0:T(8,128)S(1)} %slice.12.x0, f32[16,32,128]{2,1,0:T(8,128)S(1)} %collective-permute-done.x1, f32[16,32,128]{2,1,0:T(8,128)S(1)} %collective-permute-done.1.x2, ...), custom_call_target="tpu_custom_call" | custom-call | flops 60000002048 | bytes 2000000 | tf_op jit(solution)/shard_map/leading_inverse/pallas_call | solution.py:213
  65.2 22.1 %all-to-all-done.1.got_ref.marks_ref = f32[32,264,128]{2,1,0:T(8,128)} async-done(((f32[32,264,128]{2,1,0:T(8,128)}), f32[32,264,128]{2,1,0:T(8,128)}, u32[]{:S(2)}, u32[]{:S(2)}) %all-to-all-start.1) | async-done | bytes 4325408 | tf_op jit(solution)/shard_map/all_to_all | solution.py:466
  87.3 3.4 %panel.1 = (f32[1152,128]{1,0:T(8,128)S(1)}, f32[288,128]{1,0:T(8,128)S(1)}, f32[288,128]{1,0:T(8,128)S(1)}, f32[288,128]{1,0:T(8,128)S(1)}, f32[288,128]{1,0:T(8,128)S(1)}) custom-call(s32[1]{0:T(128)} %bitcast.col_ref, f32[32,264,128]{2,1,0:T(8,128)} %all-to-all-done.1.got_ref.marks_ref, f32[1152,128]{1,0:T(8,128)S(1)} %bitcast.13, ...), custom_call_target="tpu_custom_call" | custom-call | tf_op jit(solution)/shard_map/panel/pallas_call | solution.py:281
  91.3 1.3 collective-permute-start.4
  92.6 5.0 %collective-permute-start.5 = (f32[288,128]{1,0:T(8,128)S(1)}, f32[288,128]{1,0:T(8,128)S(1)}, u32[]{:S(2)}, u32[]{:S(2)}) collective-permute-start(f32[288,128]{1,0:T(8,128)S(1)} %get-tuple-element.30), channel_id=1, source_target_pairs={{0,8},{1,12},{2,0},{3,4},{4,9},{5,13},{6,1},{7,5},{8,10},{9,14},{1... | collective-permute-start | bytes 442376 | tf_op jit(solution)/shard_map/ppermute | solution.py:477
  97.6 3.3 %collective-permute-start.6 = (f32[288,128]{1,0:T(8,128)S(1)}, f32[288,128]{1,0:T(8,128)S(1)}, u32[]{:S(2)}, u32[]{:S(2)}) collective-permute-start(f32[288,128]{1,0:T(8,128)S(1)} %get-tuple-element.31), channel_id=1, source_target_pairs={{0,12},{1,0},{2,4},{3,8},{4,13},{5,1},{6,5},{7,9},{8,14},{9,2},{10... | collective-permute-start | bytes 442376 | tf_op jit(solution)/shard_map/ppermute | solution.py:477
  101.2 5.0 %collective-permute-done.5.x2 = f32[288,128]{1,0:T(8,128)S(1)} collective-permute-done((f32[288,128]{1,0:T(8,128)S(1)}, f32[288,128]{1,0:T(8,128)S(1)}, u32[]{:S(2)}, u32[]{:S(2)}) %collective-permute-start.5) | collective-permute-done | bytes 147488 | tf_op jit(solution)/shard_map/ppermute | solution.py:477
  106.2 1.2 share_solve.1.s0
  107.4 2.6 %collective-permute-start.9 = (f32[288,512]{1,0:T(8,128)S(1)}, f32[288,512]{1,0:T(8,128)S(1)}, u32[]{:S(2)}, u32[]{:S(2)}) collective-permute-start(f32[288,512]{1,0:T(8,128)S(1)} %share_solve.1.s0), channel_id=1, source_target_pairs={{0,24},{4,28},{8,16},{12,20},{16,8},{20,12},{24,0},{28,4},{1,25},{... | collective-permute-start | bytes 1769480 | tf_op jit(solution)/shard_map/ppermute | solution.py:493
  110.4 1.8 %collective-permute-start.15 = (f32[1152,128]{1,0:T(8,128)S(1)}, f32[1152,128]{1,0:T(8,128)S(1)}, u32[]{:S(2)}, u32[]{:S(2)}) collective-permute-start(f32[1152,128]{1,0:T(8,128)S(1)} %get-tuple-element.37.x0), channel_id=1, source_target_pairs={{0,3},{1,0},{2,1},{3,2},{4,7},{5,4},{6,5},{7,6},{8,11},{9,8},{10,9... | collective-permute-start | bytes 1769480 | tf_op jit(solution)/shard_map/ppermute | solution.py:482
  112.4 9.3 %rest.1.base_ref = f32[20736,128]{1,0:T(8,128)S(1)} custom-call(f32[32,264,128]{2,1,0:T(8,128)} %all-to-all-done.1.got_ref.marks_ref, f32[32,264,128]{2,1,0:T(8,128)} %all-to-all-done.1.got_ref.marks_ref, f32[20736,128]{1,0:T(8,128)} %bitcast.16), custom_call_target="tpu_custom_call" | custom-call | flops 10000000000 | bytes 26000000 | tf_op jit(solution)/shard_map/rest/pallas_call | solution.py:370
  121.7 2.8 %collective-permute-done.9.t2 = f32[288,512]{1,0:T(8,128)S(1)} collective-permute-done((f32[288,512]{1,0:T(8,128)S(1)}, f32[288,512]{1,0:T(8,128)S(1)}, u32[]{:S(2)}, u32[]{:S(2)}) %collective-permute-start.9) | collective-permute-done | bytes 589856 | tf_op jit(solution)/shard_map/ppermute | solution.py:493
  125.4 1.2 collective-permute-start.11
  127.2 1.8 %collective-permute-done.14.x1 = f32[1152,128]{1,0:T(8,128)S(1)} collective-permute-done((f32[1152,128]{1,0:T(8,128)S(1)}, f32[1152,128]{1,0:T(8,128)S(1)}, u32[]{:S(2)}, u32[]{:S(2)}) %collective-permute-start.14) | collective-permute-done | bytes 589856 | tf_op jit(solution)/shard_map/ppermute | solution.py:481
  129.2 6.2 %collective-permute-done.11.t0 = f32[288,512]{1,0:T(8,128)S(1)} collective-permute-done((f32[288,512]{1,0:T(8,128)S(1)}, f32[288,512]{1,0:T(8,128)S(1)}, u32[]{:S(2)}, u32[]{:S(2)}) %collective-permute-start.11) | collective-permute-done | bytes 589856 | tf_op jit(solution)/shard_map/ppermute | solution.py:499
  135.5 4.7 %collective-permute-done.16.x3 = f32[1152,128]{1,0:T(8,128)S(1)} collective-permute-done((f32[1152,128]{1,0:T(8,128)S(1)}, f32[1152,128]{1,0:T(8,128)S(1)}, u32[]{:S(2)}, u32[]{:S(2)}) %collective-permute-start.16) | collective-permute-done | bytes 589856 | tf_op jit(solution)/shard_map/ppermute | solution.py:483
  140.2 15.3 %update.1 = f32[20736,128]{1,0:T(8,128)} custom-call(s32[6]{0:T(128)S(1)} %pad_add_fusion.info_ref, f32[288,512]{1,0:T(8,128)S(1)} %share_solve.1.s0, f32[288,512]{1,0:T(8,128)S(1)} %collective-permute-done.7.s1, f32[288,512]{1,0:T(8,128)S(1)} %collective-permute-done.8.s2, f32[288,512]{1,0:T(8,128)S(1)} %collective-permute-done.10.s3, ...), custom_call_target="tpu_custom_call" | custom-call | tf_op jit(solution)/shard_map/update/pallas_call | solution.py:434
  (31 shorter events, 5.8 us)
Async XLA Ops:
  1.7 20.2 %all-to-all-start = ((f32[32,32,128]{2,1,0:T(8,128)}), f32[32,32,128]{2,1,0:T(8,128)S(1)}, u32[]{:S(2)}, u32[]{:S(2)}) async-start(f32[32,32,128]{2,1,0:T(8,128)} %bitcast.3), calls=%async_computation | async-start | bytes 1048576 | tf_op jit(solution)/shard_map/all_to_all | solution.py:463
  21.9 7.1 %collective-permute-start = (f32[16,32,128]{2,1,0:T(8,128)S(1)}, f32[16,32,128]{2,1,0:T(8,128)S(1)}, u32[]{:S(2)}, u32[]{:S(2)}) collective-permute-start(f32[16,32,128]{2,1,0:T(8,128)S(1)} %slice.12.x0), channel_id=1, source_target_pairs={{0,4},{4,0},{8,12},{12,8},{16,20},{20,16},{24,28},{28,24},{1,5},{5... | collective-permute-start | bytes 786440 | tf_op jit(solution)/shard_map/ppermute | solution.py:465
  22.0 8.1 %collective-permute-start.2 = (f32[16,32,128]{2,1,0:T(8,128)S(1)}, f32[16,32,128]{2,1,0:T(8,128)S(1)}, u32[]{:S(2)}, u32[]{:S(2)}) collective-permute-start(f32[16,32,128]{2,1,0:T(8,128)S(1)} %slice.12.x0), channel_id=1, source_target_pairs={{0,12},{4,8},{8,4},{12,0},{16,28},{20,24},{24,20},{28,16},{1,13},{... | collective-permute-start | bytes 786440 | tf_op jit(solution)/shard_map/ppermute | solution.py:465
  22.5 14.3 %collective-permute-start.1 = (f32[16,32,128]{2,1,0:T(8,128)S(1)}, f32[16,32,128]{2,1,0:T(8,128)S(1)}, u32[]{:S(2)}, u32[]{:S(2)}) collective-permute-start(f32[16,32,128]{2,1,0:T(8,128)S(1)} %slice.12.x0), channel_id=1, source_target_pairs={{0,8},{4,12},{8,0},{12,4},{16,24},{20,28},{24,16},{28,20},{1,9},{5... | collective-permute-start | bytes 786440 | tf_op jit(solution)/shard_map/ppermute | solution.py:465
  24.2 63.1 %all-to-all-start.1 = ((f32[32,264,128]{2,1,0:T(8,128)}), f32[32,264,128]{2,1,0:T(8,128)}, u32[]{:S(2)}, u32[]{:S(2)}) async-start(f32[32,264,128]{2,1,0:T(8,128)} %route.1), calls=%async_computation.1 | async-start | bytes 8650752 | tf_op jit(solution)/shard_map/all_to_all | solution.py:466
  90.7 10.3 %collective-permute-start.3 = (f32[288,128]{1,0:T(8,128)S(1)}, f32[288,128]{1,0:T(8,128)S(1)}, u32[]{:S(2)}, u32[]{:S(2)}) collective-permute-start(f32[288,128]{1,0:T(8,128)S(1)} %get-tuple-element.27), channel_id=1, source_target_pairs={{0,0},{1,4},{2,8},{3,12},{4,1},{5,5},{6,9},{7,13},{8,2},{9,6},{10,... | collective-permute-start | bytes 442376 | tf_op jit(solution)/shard_map/ppermute | solution.py:477
  91.3 9.8 %collective-permute-start.4 = (f32[288,128]{1,0:T(8,128)S(1)}, f32[288,128]{1,0:T(8,128)S(1)}, u32[]{:S(2)}, u32[]{:S(2)}) collective-permute-start(f32[288,128]{1,0:T(8,128)S(1)} %get-tuple-element.29), channel_id=1, source_target_pairs={{0,4},{1,8},{2,12},{3,0},{4,5},{5,9},{6,13},{7,1},{8,6},{9,10},{10... | collective-permute-start | bytes 442376 | tf_op jit(solution)/shard_map/ppermute | solution.py:477
  92.6 13.6 %collective-permute-start.5 = (f32[288,128]{1,0:T(8,128)S(1)}, f32[288,128]{1,0:T(8,128)S(1)}, u32[]{:S(2)}, u32[]{:S(2)}) collective-permute-start(f32[288,128]{1,0:T(8,128)S(1)} %get-tuple-element.30), channel_id=1, source_target_pairs={{0,8},{1,12},{2,0},{3,4},{4,9},{5,13},{6,1},{7,5},{8,10},{9,14},{1... | collective-permute-start | bytes 442376 | tf_op jit(solution)/shard_map/ppermute | solution.py:477
  97.6 8.6 %collective-permute-start.6 = (f32[288,128]{1,0:T(8,128)S(1)}, f32[288,128]{1,0:T(8,128)S(1)}, u32[]{:S(2)}, u32[]{:S(2)}) collective-permute-start(f32[288,128]{1,0:T(8,128)S(1)} %get-tuple-element.31), channel_id=1, source_target_pairs={{0,12},{1,0},{2,4},{3,8},{4,13},{5,1},{6,5},{7,9},{8,14},{9,2},{10... | collective-permute-start | bytes 442376 | tf_op jit(solution)/shard_map/ppermute | solution.py:477
  107.4 17.1 %collective-permute-start.9 = (f32[288,512]{1,0:T(8,128)S(1)}, f32[288,512]{1,0:T(8,128)S(1)}, u32[]{:S(2)}, u32[]{:S(2)}) collective-permute-start(f32[288,512]{1,0:T(8,128)S(1)} %share_solve.1.s0), channel_id=1, source_target_pairs={{0,24},{4,28},{8,16},{12,20},{16,8},{20,12},{24,0},{28,4},{1,25},{... | collective-permute-start | bytes 1769480 | tf_op jit(solution)/shard_map/ppermute | solution.py:493
  109.9 15.4 %collective-permute-start.8 = (f32[288,512]{1,0:T(8,128)S(1)}, f32[288,512]{1,0:T(8,128)S(1)}, u32[]{:S(2)}, u32[]{:S(2)}) collective-permute-start(f32[288,512]{1,0:T(8,128)S(1)} %share_solve.1.s0), channel_id=1, source_target_pairs={{0,8},{4,12},{8,0},{12,4},{16,24},{20,28},{24,16},{28,20},{1,9},{5... | collective-permute-start | bytes 1769480 | tf_op jit(solution)/shard_map/ppermute | solution.py:493
  110.4 16.7 %collective-permute-start.15 = (f32[1152,128]{1,0:T(8,128)S(1)}, f32[1152,128]{1,0:T(8,128)S(1)}, u32[]{:S(2)}, u32[]{:S(2)}) collective-permute-start(f32[1152,128]{1,0:T(8,128)S(1)} %get-tuple-element.37.x0), channel_id=1, source_target_pairs={{0,3},{1,0},{2,1},{3,2},{4,7},{5,4},{6,5},{7,6},{8,11},{9,8},{10,9... | collective-permute-start | bytes 1769480 | tf_op jit(solution)/shard_map/ppermute | solution.py:482
  112.2 16.8 %collective-permute-start.14 = (f32[1152,128]{1,0:T(8,128)S(1)}, f32[1152,128]{1,0:T(8,128)S(1)}, u32[]{:S(2)}, u32[]{:S(2)}) collective-permute-start(f32[1152,128]{1,0:T(8,128)S(1)} %get-tuple-element.37.x0), channel_id=1, source_target_pairs={{0,1},{1,2},{2,3},{3,0},{4,5},{5,6},{6,7},{7,4},{8,9},{9,10},{10,1... | collective-permute-start | bytes 1769480 | tf_op jit(solution)/shard_map/ppermute | solution.py:481
  112.4 23.0 %copy-start = (s32[4]{0:T(128)S(1)}, s32[4]{0:T(128)}, u32[]{:S(2)}) copy-start(s32[4]{0:T(128)} %constant.48.clone) | copy-start | bytes 52
  125.4 10.0 %collective-permute-start.11 = (f32[288,512]{1,0:T(8,128)S(1)}, f32[288,512]{1,0:T(8,128)S(1)}, u32[]{:S(2)}, u32[]{:S(2)}) collective-permute-start(f32[288,512]{1,0:T(8,128)S(1)} %broadcast_select_fusion.1), channel_id=1, source_target_pairs={{0,8},{4,28},{8,0},{12,20},{16,24},{20,12},{24,16},{28,4},{1,9},{5... | collective-permute-start | bytes 1769480 | tf_op jit(solution)/shard_map/ppermute | solution.py:499
  126.6 8.8 %collective-permute-start.7 = (f32[288,512]{1,0:T(8,128)S(1)}, f32[288,512]{1,0:T(8,128)S(1)}, u32[]{:S(2)}, u32[]{:S(2)}) collective-permute-start(f32[288,512]{1,0:T(8,128)S(1)} %share_solve.1.s0), channel_id=1, source_target_pairs={{0,4},{4,0},{8,12},{12,8},{16,20},{20,16},{24,28},{28,24},{1,5},{5... | collective-permute-start | bytes 1769480 | tf_op jit(solution)/shard_map/ppermute | solution.py:493
  126.9 13.3 %collective-permute-start.10 = (f32[288,512]{1,0:T(8,128)S(1)}, f32[288,512]{1,0:T(8,128)S(1)}, u32[]{:S(2)}, u32[]{:S(2)}) collective-permute-start(f32[288,512]{1,0:T(8,128)S(1)} %collective-permute-done.8.s2), channel_id=1, source_target_pairs={{0,4},{4,0},{8,12},{12,8},{16,20},{20,16},{24,28},{28,24},{1,5},{5... | collective-permute-start | bytes 1769480 | tf_op jit(solution)/shard_map/ppermute | solution.py:493
  129.0 11.2 %collective-permute-start.16 = (f32[1152,128]{1,0:T(8,128)S(1)}, f32[1152,128]{1,0:T(8,128)S(1)}, u32[]{:S(2)}, u32[]{:S(2)}) collective-permute-start(f32[1152,128]{1,0:T(8,128)S(1)} %broadcast_select_fusion), channel_id=1, source_target_pairs={{0,1},{1,2},{2,3},{3,0},{4,7},{5,4},{6,5},{7,6},{8,9},{9,10},{10,1... | collective-permute-start | bytes 1769480 | tf_op jit(solution)/shard_map/ppermute | solution.py:483
  129.1 11.1 %collective-permute-start.13 = (f32[288,512]{1,0:T(8,128)S(1)}, f32[288,512]{1,0:T(8,128)S(1)}, u32[]{:S(2)}, u32[]{:S(2)}) collective-permute-start(f32[288,512]{1,0:T(8,128)S(1)} %collective-permute-done.9.t2), channel_id=1, source_target_pairs={{0,4},{4,0},{8,12},{12,8},{16,20},{20,16},{24,28},{28,24},{1,5},{5... | collective-permute-start | bytes 1769480 | tf_op jit(solution)/shard_map/ppermute | solution.py:493
  135.4 4.8 %collective-permute-start.12 = (f32[288,512]{1,0:T(8,128)S(1)}, f32[288,512]{1,0:T(8,128)S(1)}, u32[]{:S(2)}, u32[]{:S(2)}) collective-permute-start(f32[288,512]{1,0:T(8,128)S(1)} %collective-permute-done.11.t0), channel_id=1, source_target_pairs={{0,4},{4,0},{8,12},{12,8},{16,20},{20,16},{24,28},{28,24},{1,5},{5... | collective-permute-start | bytes 1769480 | tf_op jit(solution)/shard_map/ppermute | solution.py:493

commit v9 on v8

--- a/solution.py
+++ b/solution.py
@@ -165,13 +165,15 @@
             e[g] = e[g] - tree_sum([below[g][k] * x[k] for k in range(8)])
 
 
-def leading_kernel(quarter_ref, x0, x1, x2, x3, high_ref, low_ref, lead_ref, s_ref, e_ref, w_ref):
+def leading_kernel(offsets, me_ref, halves_ref, high_ref, low_ref, lead_ref, s_ref, e_ref, w_ref):
     n = 4
     dot = functools.partial(lax.dot_general, precision=HIGHEST, preferred_element_type=F32)
 
 
-    for d, x in enumerate((x0, x1, x2, x3)):
-        lead_ref[:, pl.ds(pl.multiple_of((quarter_ref[0] ^ d) * 32, 32), 32), :] = x[...]
+    for i, offset in enumerate(offsets):
+        source = me_ref[0] ^ offset
+        at = pl.ds(pl.multiple_of(source // 16 * (T // 2), T // 2), T // 2)
+        lead_ref[source % 16, at, :] = halves_ref[i]
 
     def tile(i, j):
         return lead_ref[4 * i + j]
@@ -209,14 +211,14 @@
     lax.fori_loop(0, n, step, 0)
 
 
-def leading_inverse(quarter, parts):
+def leading_inverse(me, halves, offsets):
     return pl.pallas_call(
-        leading_kernel,
+        functools.partial(leading_kernel, offsets),
         out_shape=(jax.ShapeDtypeStruct((4, T, 4 * T), BF16),) * 2,
         grid_spec=pltpu.PrefetchScalarGridSpec(
             num_scalar_prefetch=1,
             grid=(),
-            in_specs=[VM()] * 4,
+            in_specs=[VM()],
             out_specs=(VM(), VM()),
             scratch_shapes=[
                 pltpu.VMEM((16, T, T), F32),
@@ -226,9 +228,9 @@
             ],
         ),
         compiler_params=params(16),
-        cost_estimate=pl.CostEstimate(flops=60_000_000_000, bytes_accessed=2_000_000, transcendentals=0),
+        cost_estimate=pl.CostEstimate(flops=1_000_000, bytes_accessed=2_000_000, transcendentals=0),
         name="leading_inverse",
-    )(quarter, *parts)
+    )(me, halves)
 
 
 def panel_kernel(col_ref, got_ref, base_ref, after_ref, out_ref, p0, p1, p2, p3, held, places, sem):
@@ -458,14 +460,18 @@
 
     send = route(child_owner[0, :, 0], child_slot[0], child_updates[0], child_rows[0], child_cols[0], 32, slot_total, tile_cols)
 
-    tile = front[0, 0, 0, :, 0, 0, :].reshape(1, 4, 1, T // 4, T)
-    quarters = jnp.broadcast_to(tile, (2, 4, 4, T // 4, T)).reshape(32, T // 4, T)
-    mine = lax.all_to_all(quarters, ("row", "col"), split_axis=0, concat_axis=0, tiled=True)[:16]
-    mine, send = lax.optimization_barrier((mine, send))
-    lead = [mine] + [lax.ppermute(mine, "row", [(r, r ^ d) for r in range(8)]) for d in (1, 2, 3)]
+    tile = front[0, 0, 0, :, 0, 0, :]
+    lower = lax.ppermute(tile[T // 2 :], "row", [(r, r + 4) for r in range(4)])
+    lead = jnp.where(my_row < 4, tile[: T // 2], lower)[None]
+    offsets = [0]
+    for axis, size, bit, offset in (("row", 8, 4, 16), ("col", 4, 2, 2), ("col", 4, 1, 1), ("row", 8, 2, 8), ("row", 8, 1, 4)):
+        lead = jnp.concatenate([lead, lax.ppermute(lead, axis, [(i, i ^ bit) for i in range(size)])], axis=0)
+        offsets = offsets + [o ^ offset for o in offsets]
+        if offset == 16:
+            lead, send = lax.optimization_barrier((lead, send))
     got = lax.all_to_all(send, ("row", "col"), split_axis=0, concat_axis=0, tiled=True)
-    wt = leading_inverse((my_row % 4).reshape(1), lead)
-    base_panel = lax.optimization_barrier((front, lead[1]))[0][0, :, 0, :, 0, 0, :].reshape(tile_rows * T, T)
+    wt = leading_inverse((my_row * 4 + my_col).reshape(1), lead, offsets)
+    base_panel = lax.optimization_barrier((front, lead))[0][0, :, 0, :, 0, 0, :].reshape(tile_rows * T, T)
 
     columns, *pieces = panel(my_col.reshape(1), got, base_panel, wt[1])
 

time: 156 us -> 188 us (1.21)
  waiting for transfers between devices: 54.2 us -> 81 us
  starting transfers between devices: 32.7 us -> 38 us
    ppermute x3 -> x6, waiting for transfers between devices: 6.73 us -> 61.6 us  [the longest x5 60 us: local(): lax.ppermute(lead, axis, [(i, i ^ bit) for i in range(size)])]
    all_to_all x1, waiting for transfers between devices: 22.1 us -> 0.01 us  [local(): lax.all_to_all(send, ('row', 'col'), split_axis=0, concat_axis=0, tiled=T...]
    ppermute x3 -> x6, starting transfers between devices: 2.23 us -> 15.7 us  [the longest x5 10.5 us: local(): lax.ppermute(lead, axis, [(i, i ^ bit) for i in range(size)])]
    all_to_all x1 -> x0, starting transfers between devices: 8.42 us -> none  [local(): lax.all_to_all(quarters, ('row', 'col'), split_axis=0, concat_axis=0, til...]
    all_to_all x1 -> x0, waiting for transfers between devices: 3.73 us -> none  [local(): lax.all_to_all(quarters, ('row', 'col'), split_axis=0, concat_axis=0, til...]
    ppermute x4, starting transfers between devices: 10.2 us -> 7.94 us  [local(): parts.append(lax.ppermute(pieces[m], ('row', 'col'), moves))]
  transfers between devices with their start and end apart: 19 -> 21, of which waited for: 10 -> 12; matrix products, arithmetic and copies ran while one was open for 1% -> 1% of each run, Pallas kernels for 29% -> 24%
where the time goes in v9:
time: 188 us; the launch traced here: 187 us
  waiting for transfers between devices  81 us (43%)
  Pallas kernels  65.5 us (35%)
  starting transfers between devices  38 us (20%)
  local copies, waits for them, and re-layouts  1.97 us (1%)
    ppermute x5, waiting for transfers between devices, local(): lax.ppermute(lead, axis, [(i, i ^ bit) for i in range(size)])  60 us
    pallas_call x1, Pallas kernels, leading_inverse(): pl.pallas_call(functools.partial(leading_kernel, offsets), out_shape=(jax...  28.4 us
    pallas_call x1, Pallas kernels, update(): pl.pallas_call(functools.partial(update_kernel, tile_cols, group), out_sh...  15.3 us
    ppermute x5, starting transfers between devices, local(): lax.ppermute(lead, axis, [(i, i ^ bit) for i in range(size)])  10.5 us
    pallas_call x1, Pallas kernels, rest(): pl.pallas_call(functools.partial(rest_kernel, tile_cols, group), out_shap...  9.24 us
    pallas_call x1, Pallas kernels, route(): pl.pallas_call(functools.partial(route_kernel, group, slot_total, tile_co...  8.04 us
    ppermute x4, starting transfers between devices, local(): parts.append(lax.ppermute(pieces[m], ('row', 'col'), moves))  7.94 us
    ppermute x1, waiting for transfers between devices, local(): lax.ppermute(jnp.where(first_core, far_side, near), 'row', [(r, r ^ (2 if...  6.71 us
  transfers between devices with their start and end apart: 21, of which 12 were waited for; matrix products, arithmetic and copies ran while one was open for 1% of the time, Pallas kernels for 24%

profile of v9, /device:TPU:0, one launch (start us, length us, event | category | flops | bytes accessed | tf_op | source)
XLA Modules:
  0.0 187.1 jit_solution(10989537399388101810)
XLA Ops:
  0.8 5.2 %collective-permute-start = (f32[64,128]{1,0:T(8,128)S(1)}, f32[64,128]{1,0:T(8,128)S(1)}, u32[]{:S(2)}, u32[]{:S(2)}) collective-permute-start(f32[64,128]{1,0:T(8,128)S(1)} %bitcast.23), channel_id=1, source_target_pairs={{0,16},{4,20},{8,24},{12,28},{1,17},{5,21},{9,25},{13,29},{2,18},{... | collective-permute-start | bytes 98312 | tf_op jit(solution)/shard_map/ppermute | solution.py:464
  6.0 1.6 collective-permute-done
  7.5 3.8 %collective-permute-start.1 = (f32[1,64,128]{2,1,0:T(8,128)S(1)}, f32[1,64,128]{2,1,0:T(8,128)S(1)}, u32[]{:S(2)}, u32[]{:S(2)}) collective-permute-start(f32[1,64,128]{2,1,0:T(8,128)S(1)} %select_bitcast_fusion), channel_id=1, source_target_pairs={{0,16},{4,20},{8,24},{12,28},{16,0},{20,4},{24,8},{28,12},{1,17},{... | collective-permute-start | bytes 98312 | tf_op jit(solution)/shard_map/ppermute | solution.py:468
  11.4 8.0 %route.1 = f32[32,264,128]{2,1,0:T(8,128)} custom-call(s32[32]{0:T(128)} %bitcast.26, s32[32]{0:T(128)} %bitcast.27, f32[32,128,128]{2,1,0:T(8,128)} %bitcast.20, s32[32,128]{1,0:T(8,128)} %bitcast.24, s32[32,128]{1,0:T(8,128)} %bitcast.25), custom_call_target="tpu_custom_call" | custom-call | tf_op jit(solution)/shard_map/route/pallas_call | solution.py:96
  19.4 5.9 %all-to-all-start = ((f32[32,264,128]{2,1,0:T(8,128)}), f32[32,264,128]{2,1,0:T(8,128)}, u32[]{:S(2)}, u32[]{:S(2)}) async-start(f32[32,264,128]{2,1,0:T(8,128)} %route.1), calls=%async_computation | async-start | bytes 8650752 | tf_op jit(solution)/shard_map/all_to_all | solution.py:472
  25.4 3.3 %collective-permute-start.2 = (f32[2,64,128]{2,1,0:T(8,128)S(1)}, f32[2,64,128]{2,1,0:T(8,128)S(1)}, u32[]{:S(2)}, u32[]{:S(2)}) collective-permute-start(f32[2,64,128]{2,1,0:T(8,128)S(1)} %pad_maximum_fusion.3), channel_id=1, source_target_pairs={{0,2},{1,3},{2,0},{3,1},{4,6},{5,7},{6,4},{7,5},{8,10},{9,11},{10,... | collective-permute-start | bytes 196616 | tf_op jit(solution)/shard_map/ppermute | solution.py:468
  28.7 49.7 %collective-permute-done.2 = f32[2,64,128]{2,1,0:T(8,128)S(1)} collective-permute-done((f32[2,64,128]{2,1,0:T(8,128)S(1)}, f32[2,64,128]{2,1,0:T(8,128)S(1)}, u32[]{:S(2)}, u32[]{:S(2)}) %collective-permute-start.2) | collective-permute-done | bytes 65568 | tf_op jit(solution)/shard_map/ppermute | solution.py:468
  78.4 1.8 collective-permute-start.3
  80.2 3.3 %collective-permute-done.3 = f32[4,64,128]{2,1,0:T(8,128)S(1)} collective-permute-done((f32[4,64,128]{2,1,0:T(8,128)S(1)}, f32[4,64,128]{2,1,0:T(8,128)S(1)}, u32[]{:S(2)}, u32[]{:S(2)}) %collective-permute-start.3) | collective-permute-done | bytes 131104 | tf_op jit(solution)/shard_map/ppermute | solution.py:468
  83.5 1.5 collective-permute-start.4
  85.1 5.2 %collective-permute-done.4 = f32[8,64,128]{2,1,0:T(8,128)S(1)} collective-permute-done((f32[8,64,128]{2,1,0:T(8,128)S(1)}, f32[8,64,128]{2,1,0:T(8,128)S(1)}, u32[]{:S(2)}, u32[]{:S(2)}) %collective-permute-start.4) | collective-permute-done | bytes 262176 | tf_op jit(solution)/shard_map/ppermute | solution.py:468
  90.5 1.8 collective-permute-done.5
  93.4 28.4 %leading_inverse.1 = (bf16[4,128,512]{2,1,0:T(8,128)(2,1)S(1)}, bf16[4,128,512]{2,1,0:T(8,128)(2,1)S(1)}) custom-call(s32[1]{0:T(128)} %bitcast.11.me_ref, f32[32,64,128]{2,1,0:T(8,128)S(1)} %constant_dynamic-update-slice_fusion.halves_ref), custom_call_target="tpu_custom_call" | custom-call | flops 1000000 | bytes 2000000 | tf_op jit(solution)/shard_map/leading_inverse/pallas_call | solution.py:215
  121.8 3.4 %panel.1 = (f32[1152,128]{1,0:T(8,128)S(1)}, f32[288,128]{1,0:T(8,128)S(1)}, f32[288,128]{1,0:T(8,128)S(1)}, f32[288,128]{1,0:T(8,128)S(1)}, f32[288,128]{1,0:T(8,128)S(1)}) custom-call(s32[1]{0:T(128)} %bitcast.col_ref, f32[32,264,128]{2,1,0:T(8,128)} %all-to-all-done.got_ref.marks_ref, f32[1152,128]{1,0:T(8,128)S(1)} %bitcast.19, ...), custom_call_target="tpu_custom_call" | custom-call | tf_op jit(solution)/shard_map/panel/pallas_call | solution.py:283
  125.9 3.5 %collective-permute-start.7 = (f32[288,128]{1,0:T(8,128)S(1)}, f32[288,128]{1,0:T(8,128)S(1)}, u32[]{:S(2)}, u32[]{:S(2)}) collective-permute-start(f32[288,128]{1,0:T(8,128)S(1)} %get-tuple-element.29), channel_id=1, source_target_pairs={{0,4},{1,8},{2,12},{3,0},{4,5},{5,9},{6,13},{7,1},{8,6},{9,10},{10... | collective-permute-start | bytes 442376 | tf_op jit(solution)/shard_map/ppermute | solution.py:483
  129.4 3.1 %collective-permute-start.8 = (f32[288,128]{1,0:T(8,128)S(1)}, f32[288,128]{1,0:T(8,128)S(1)}, u32[]{:S(2)}, u32[]{:S(2)}) collective-permute-start(f32[288,128]{1,0:T(8,128)S(1)} %get-tuple-element.30), channel_id=1, source_target_pairs={{0,8},{1,12},{2,0},{3,4},{4,9},{5,13},{6,1},{7,5},{8,10},{9,14},{1... | collective-permute-start | bytes 442376 | tf_op jit(solution)/shard_map/ppermute | solution.py:483
  133.9 4.9 %collective-permute-done.8.x2 = f32[288,128]{1,0:T(8,128)S(1)} collective-permute-done((f32[288,128]{1,0:T(8,128)S(1)}, f32[288,128]{1,0:T(8,128)S(1)}, u32[]{:S(2)}, u32[]{:S(2)}) %collective-permute-start.8) | collective-permute-done | bytes 147488 | tf_op jit(solution)/shard_map/ppermute | solution.py:483
  140.0 3.4 %collective-permute-start.12 = (f32[288,512]{1,0:T(8,128)S(1)}, f32[288,512]{1,0:T(8,128)S(1)}, u32[]{:S(2)}, u32[]{:S(2)}) collective-permute-start(f32[288,512]{1,0:T(8,128)S(1)} %share_solve.1.s0), channel_id=1, source_target_pairs={{0,24},{4,28},{8,16},{12,20},{16,8},{20,12},{24,0},{28,4},{1,25},{... | collective-permute-start | bytes 1769480 | tf_op jit(solution)/shard_map/ppermute | solution.py:499
  145.4 9.2 %rest.1.base_ref = f32[20736,128]{1,0:T(8,128)S(1)} custom-call(f32[32,264,128]{2,1,0:T(8,128)} %all-to-all-done.got_ref.marks_ref, f32[32,264,128]{2,1,0:T(8,128)} %all-to-all-done.got_ref.marks_ref, f32[20736,128]{1,0:T(8,128)} %bitcast.22), custom_call_target="tpu_custom_call" | custom-call | flops 10000000000 | bytes 26000000 | tf_op jit(solution)/shard_map/rest/pallas_call | solution.py:372
  154.6 2.5 %collective-permute-done.12.t2 = f32[288,512]{1,0:T(8,128)S(1)} collective-permute-done((f32[288,512]{1,0:T(8,128)S(1)}, f32[288,512]{1,0:T(8,128)S(1)}, u32[]{:S(2)}, u32[]{:S(2)}) %collective-permute-start.12) | collective-permute-done | bytes 589856 | tf_op jit(solution)/shard_map/ppermute | solution.py:499
  157.9 1.8 collective-permute-start.14
  161.2 6.7 %collective-permute-done.14.t0 = f32[288,512]{1,0:T(8,128)S(1)} collective-permute-done((f32[288,512]{1,0:T(8,128)S(1)}, f32[288,512]{1,0:T(8,128)S(1)}, u32[]{:S(2)}, u32[]{:S(2)}) %collective-permute-start.14) | collective-permute-done | bytes 589856 | tf_op jit(solution)/shard_map/ppermute | solution.py:505
  168.2 3.6 %collective-permute-done.19.x3 = f32[1152,128]{1,0:T(8,128)S(1)} collective-permute-done((f32[1152,128]{1,0:T(8,128)S(1)}, f32[1152,128]{1,0:T(8,128)S(1)}, u32[]{:S(2)}, u32[]{:S(2)}) %collective-permute-start.19) | collective-permute-done | bytes 589856 | tf_op jit(solution)/shard_map/ppermute | solution.py:489
  171.8 15.3 %update.1 = f32[20736,128]{1,0:T(8,128)} custom-call(s32[6]{0:T(128)S(1)} %pad_add_fusion.info_ref, f32[288,512]{1,0:T(8,128)S(1)} %share_solve.1.s0, f32[288,512]{1,0:T(8,128)S(1)} %collective-permute-done.10.s1, f32[288,512]{1,0:T(8,128)S(1)} %collective-permute-done.11.s2, f32[288,512]{1,0:T(8,128)S(1)} %collective-permute-done.13.s3, ...), custom_call_target="tpu_custom_call" | custom-call | tf_op jit(solution)/shard_map/update/pallas_call | solution.py:436
  (43 shorter events, 10.0 us)
Async XLA Ops:
  0.8 6.8 %collective-permute-start = (f32[64,128]{1,0:T(8,128)S(1)}, f32[64,128]{1,0:T(8,128)S(1)}, u32[]{:S(2)}, u32[]{:S(2)}) collective-permute-start(f32[64,128]{1,0:T(8,128)S(1)} %bitcast.23), channel_id=1, source_target_pairs={{0,16},{4,20},{8,24},{12,28},{1,17},{5,21},{9,25},{13,29},{2,18},{... | collective-permute-start | bytes 98312 | tf_op jit(solution)/shard_map/ppermute | solution.py:464
  7.5 11.9 %collective-permute-start.1 = (f32[1,64,128]{2,1,0:T(8,128)S(1)}, f32[1,64,128]{2,1,0:T(8,128)S(1)}, u32[]{:S(2)}, u32[]{:S(2)}) collective-permute-start(f32[1,64,128]{2,1,0:T(8,128)S(1)} %select_bitcast_fusion), channel_id=1, source_target_pairs={{0,16},{4,20},{8,24},{12,28},{16,0},{20,4},{24,8},{28,12},{1,17},{... | collective-permute-start | bytes 98312 | tf_op jit(solution)/shard_map/ppermute | solution.py:468
  19.4 102.4 %all-to-all-start = ((f32[32,264,128]{2,1,0:T(8,128)}), f32[32,264,128]{2,1,0:T(8,128)}, u32[]{:S(2)}, u32[]{:S(2)}) async-start(f32[32,264,128]{2,1,0:T(8,128)} %route.1), calls=%async_computation | async-start | bytes 8650752 | tf_op jit(solution)/shard_map/all_to_all | solution.py:472
  25.4 53.0 %collective-permute-start.2 = (f32[2,64,128]{2,1,0:T(8,128)S(1)}, f32[2,64,128]{2,1,0:T(8,128)S(1)}, u32[]{:S(2)}, u32[]{:S(2)}) collective-permute-start(f32[2,64,128]{2,1,0:T(8,128)S(1)} %pad_maximum_fusion.3), channel_id=1, source_target_pairs={{0,2},{1,3},{2,0},{3,1},{4,6},{5,7},{6,4},{7,5},{8,10},{9,11},{10,... | collective-permute-start | bytes 196616 | tf_op jit(solution)/shard_map/ppermute | solution.py:468
  78.4 5.1 %collective-permute-start.3 = (f32[4,64,128]{2,1,0:T(8,128)S(1)}, f32[4,64,128]{2,1,0:T(8,128)S(1)}, u32[]{:S(2)}, u32[]{:S(2)}) collective-permute-start(f32[4,64,128]{2,1,0:T(8,128)S(1)} %pad_maximum_fusion.2), channel_id=1, source_target_pairs={{0,1},{1,0},{2,3},{3,2},{4,5},{5,4},{6,7},{7,6},{8,9},{9,8},{10,11... | collective-permute-start | bytes 393224 | tf_op jit(solution)/shard_map/ppermute | solution.py:468
  83.5 6.7 %collective-permute-start.4 = (f32[8,64,128]{2,1,0:T(8,128)S(1)}, f32[8,64,128]{2,1,0:T(8,128)S(1)}, u32[]{:S(2)}, u32[]{:S(2)}) collective-permute-start(f32[8,64,128]{2,1,0:T(8,128)S(1)} %pad_maximum_fusion.1), channel_id=1, source_target_pairs={{0,8},{4,12},{8,0},{12,4},{16,24},{20,28},{24,16},{28,20},{1,9},{5... | collective-permute-start | bytes 786440 | tf_op jit(solution)/shard_map/ppermute | solution.py:468
  90.3 2.0 %collective-permute-start.5 = (f32[16,64,128]{2,1,0:T(8,128)S(1)}, f32[16,64,128]{2,1,0:T(8,128)S(1)}, u32[]{:S(2)}, u32[]{:S(2)}) collective-permute-start(f32[16,64,128]{2,1,0:T(8,128)S(1)} %pad_maximum_fusion), channel_id=1, source_target_pairs={{0,4},{4,0},{8,12},{12,8},{16,20},{20,16},{24,28},{28,24},{1,5},{5... | collective-permute-start | bytes 1572872 | tf_op jit(solution)/shard_map/ppermute | solution.py:468
  125.2 8.0 %collective-permute-start.6 = (f32[288,128]{1,0:T(8,128)S(1)}, f32[288,128]{1,0:T(8,128)S(1)}, u32[]{:S(2)}, u32[]{:S(2)}) collective-permute-start(f32[288,128]{1,0:T(8,128)S(1)} %get-tuple-element.27), channel_id=1, source_target_pairs={{0,0},{1,4},{2,8},{3,12},{4,1},{5,5},{6,9},{7,13},{8,2},{9,6},{10,... | collective-permute-start | bytes 442376 | tf_op jit(solution)/shard_map/ppermute | solution.py:483
  125.9 8.0 %collective-permute-start.7 = (f32[288,128]{1,0:T(8,128)S(1)}, f32[288,128]{1,0:T(8,128)S(1)}, u32[]{:S(2)}, u32[]{:S(2)}) collective-permute-start(f32[288,128]{1,0:T(8,128)S(1)} %get-tuple-element.29), channel_id=1, source_target_pairs={{0,4},{1,8},{2,12},{3,0},{4,5},{5,9},{6,13},{7,1},{8,6},{9,10},{10... | collective-permute-start | bytes 442376 | tf_op jit(solution)/shard_map/ppermute | solution.py:483
  129.4 9.4 %collective-permute-start.8 = (f32[288,128]{1,0:T(8,128)S(1)}, f32[288,128]{1,0:T(8,128)S(1)}, u32[]{:S(2)}, u32[]{:S(2)}) collective-permute-start(f32[288,128]{1,0:T(8,128)S(1)} %get-tuple-element.30), channel_id=1, source_target_pairs={{0,8},{1,12},{2,0},{3,4},{4,9},{5,13},{6,1},{7,5},{8,10},{9,14},{1... | collective-permute-start | bytes 442376 | tf_op jit(solution)/shard_map/ppermute | solution.py:483
  132.5 6.3 %collective-permute-start.9 = (f32[288,128]{1,0:T(8,128)S(1)}, f32[288,128]{1,0:T(8,128)S(1)}, u32[]{:S(2)}, u32[]{:S(2)}) collective-permute-start(f32[288,128]{1,0:T(8,128)S(1)} %get-tuple-element.31), channel_id=1, source_target_pairs={{0,12},{1,0},{2,4},{3,8},{4,13},{5,1},{6,5},{7,9},{8,14},{9,2},{10... | collective-permute-start | bytes 442376 | tf_op jit(solution)/shard_map/ppermute | solution.py:483
  140.0 17.1 %collective-permute-start.12 = (f32[288,512]{1,0:T(8,128)S(1)}, f32[288,512]{1,0:T(8,128)S(1)}, u32[]{:S(2)}, u32[]{:S(2)}) collective-permute-start(f32[288,512]{1,0:T(8,128)S(1)} %share_solve.1.s0), channel_id=1, source_target_pairs={{0,24},{4,28},{8,16},{12,20},{16,8},{20,12},{24,0},{28,4},{1,25},{... | collective-permute-start | bytes 1769480 | tf_op jit(solution)/shard_map/ppermute | solution.py:499
  143.4 14.5 %collective-permute-start.11 = (f32[288,512]{1,0:T(8,128)S(1)}, f32[288,512]{1,0:T(8,128)S(1)}, u32[]{:S(2)}, u32[]{:S(2)}) collective-permute-start(f32[288,512]{1,0:T(8,128)S(1)} %share_solve.1.s0), channel_id=1, source_target_pairs={{0,8},{4,12},{8,0},{12,4},{16,24},{20,28},{24,16},{28,20},{1,9},{5... | collective-permute-start | bytes 1769480 | tf_op jit(solution)/shard_map/ppermute | solution.py:499
  143.4 16.9 %collective-permute-start.18 = (f32[1152,128]{1,0:T(8,128)S(1)}, f32[1152,128]{1,0:T(8,128)S(1)}, u32[]{:S(2)}, u32[]{:S(2)}) collective-permute-start(f32[1152,128]{1,0:T(8,128)S(1)} %get-tuple-element.37.x0), channel_id=1, source_target_pairs={{0,3},{1,0},{2,1},{3,2},{4,7},{5,4},{6,5},{7,6},{8,11},{9,8},{10,9... | collective-permute-start | bytes 1769480 | tf_op jit(solution)/shard_map/ppermute | solution.py:488
  144.6 16.0 %collective-permute-start.17 = (f32[1152,128]{1,0:T(8,128)S(1)}, f32[1152,128]{1,0:T(8,128)S(1)}, u32[]{:S(2)}, u32[]{:S(2)}) collective-permute-start(f32[1152,128]{1,0:T(8,128)S(1)} %get-tuple-element.37.x0), channel_id=1, source_target_pairs={{0,1},{1,2},{2,3},{3,0},{4,5},{5,6},{6,7},{7,4},{8,9},{9,10},{10,1... | collective-permute-start | bytes 1769480 | tf_op jit(solution)/shard_map/ppermute | solution.py:487
  145.4 22.7 %copy-start = (s32[4]{0:T(128)S(1)}, s32[4]{0:T(128)}, u32[]{:S(2)}) copy-start(s32[4]{0:T(128)} %constant.44.clone) | copy-start | bytes 52
  157.9 10.0 %collective-permute-start.14 = (f32[288,512]{1,0:T(8,128)S(1)}, f32[288,512]{1,0:T(8,128)S(1)}, u32[]{:S(2)}, u32[]{:S(2)}) collective-permute-start(f32[288,512]{1,0:T(8,128)S(1)} %broadcast_select_fusion.1), channel_id=1, source_target_pairs={{0,8},{4,28},{8,0},{12,20},{16,24},{20,12},{24,16},{28,4},{1,9},{5... | collective-permute-start | bytes 1769480 | tf_op jit(solution)/shard_map/ppermute | solution.py:505
  159.7 8.5 %collective-permute-start.10 = (f32[288,512]{1,0:T(8,128)S(1)}, f32[288,512]{1,0:T(8,128)S(1)}, u32[]{:S(2)}, u32[]{:S(2)}) collective-permute-start(f32[288,512]{1,0:T(8,128)S(1)} %share_solve.1.s0), channel_id=1, source_target_pairs={{0,4},{4,0},{8,12},{12,8},{16,20},{20,16},{24,28},{28,24},{1,5},{5... | collective-permute-start | bytes 1769480 | tf_op jit(solution)/shard_map/ppermute | solution.py:499
  159.7 12.0 %collective-permute-start.13 = (f32[288,512]{1,0:T(8,128)S(1)}, f32[288,512]{1,0:T(8,128)S(1)}, u32[]{:S(2)}, u32[]{:S(2)}) collective-permute-start(f32[288,512]{1,0:T(8,128)S(1)} %collective-permute-done.11.s2), channel_id=1, source_target_pairs={{0,4},{4,0},{8,12},{12,8},{16,20},{20,16},{24,28},{28,24},{1,5},{5... | collective-permute-start | bytes 1769480 | tf_op jit(solution)/shard_map/ppermute | solution.py:499
  160.6 11.2 %collective-permute-start.19 = (f32[1152,128]{1,0:T(8,128)S(1)}, f32[1152,128]{1,0:T(8,128)S(1)}, u32[]{:S(2)}, u32[]{:S(2)}) collective-permute-start(f32[1152,128]{1,0:T(8,128)S(1)} %broadcast_select_fusion), channel_id=1, source_target_pairs={{0,1},{1,2},{2,3},{3,0},{4,7},{5,4},{6,5},{7,6},{8,9},{9,10},{10,1... | collective-permute-start | bytes 1769480 | tf_op jit(solution)/shard_map/ppermute | solution.py:489
  161.2 10.6 %collective-permute-start.16 = (f32[288,512]{1,0:T(8,128)S(1)}, f32[288,512]{1,0:T(8,128)S(1)}, u32[]{:S(2)}, u32[]{:S(2)}) collective-permute-start(f32[288,512]{1,0:T(8,128)S(1)} %collective-permute-done.12.t2), channel_id=1, source_target_pairs={{0,4},{4,0},{8,12},{12,8},{16,20},{20,16},{24,28},{28,24},{1,5},{5... | collective-permute-start | bytes 1769480 | tf_op jit(solution)/shard_map/ppermute | solution.py:499
  167.9 3.9 %collective-permute-start.15 = (f32[288,512]{1,0:T(8,128)S(1)}, f32[288,512]{1,0:T(8,128)S(1)}, u32[]{:S(2)}, u32[]{:S(2)}) collective-permute-start(f32[288,512]{1,0:T(8,128)S(1)} %collective-permute-done.14.t0), channel_id=1, source_target_pairs={{0,4},{4,0},{8,12},{12,8},{16,20},{20,16},{24,28},{28,24},{1,5},{5... | collective-permute-start | bytes 1769480 | tf_op jit(solution)/shard_map/ppermute | solution.py:499

commit v10 on v8

--- a/solution.py
+++ b/solution.py
@@ -165,13 +165,13 @@
             e[g] = e[g] - tree_sum([below[g][k] * x[k] for k in range(8)])
 
 
-def leading_kernel(quarter_ref, x0, x1, x2, x3, high_ref, low_ref, lead_ref, s_ref, e_ref, w_ref):
+def leading_kernel(core_ref, x0, x1, high_ref, low_ref, lead_ref, s_ref, e_ref, w_ref):
     n = 4
     dot = functools.partial(lax.dot_general, precision=HIGHEST, preferred_element_type=F32)
 
 
-    for d, x in enumerate((x0, x1, x2, x3)):
-        lead_ref[:, pl.ds(pl.multiple_of((quarter_ref[0] ^ d) * 32, 32), 32), :] = x[...]
+    for d, x in enumerate((x0, x1)):
+        lead_ref[:, pl.ds(pl.multiple_of((core_ref[0] ^ d) * 64, 64), 64), :] = x[...]
 
     def tile(i, j):
         return lead_ref[4 * i + j]
@@ -209,14 +209,14 @@
     lax.fori_loop(0, n, step, 0)
 
 
-def leading_inverse(quarter, parts):
+def leading_inverse(core, parts):
     return pl.pallas_call(
         leading_kernel,
         out_shape=(jax.ShapeDtypeStruct((4, T, 4 * T), BF16),) * 2,
         grid_spec=pltpu.PrefetchScalarGridSpec(
             num_scalar_prefetch=1,
             grid=(),
-            in_specs=[VM()] * 4,
+            in_specs=[VM()] * 2,
             out_specs=(VM(), VM()),
             scratch_shapes=[
                 pltpu.VMEM((16, T, T), F32),
@@ -228,7 +228,7 @@
         compiler_params=params(16),
         cost_estimate=pl.CostEstimate(flops=60_000_000_000, bytes_accessed=2_000_000, transcendentals=0),
         name="leading_inverse",
-    )(quarter, *parts)
+    )(core, *parts)
 
 
 def panel_kernel(col_ref, got_ref, base_ref, after_ref, out_ref, p0, p1, p2, p3, held, places, sem):
@@ -458,13 +458,13 @@
 
     send = route(child_owner[0, :, 0], child_slot[0], child_updates[0], child_rows[0], child_cols[0], 32, slot_total, tile_cols)
 
-    tile = front[0, 0, 0, :, 0, 0, :].reshape(1, 4, 1, T // 4, T)
-    quarters = jnp.broadcast_to(tile, (2, 4, 4, T // 4, T)).reshape(32, T // 4, T)
-    mine = lax.all_to_all(quarters, ("row", "col"), split_axis=0, concat_axis=0, tiled=True)[:16]
+    tile = front[0, 0, 0, :, 0, 0, :].reshape(1, 2, 1, T // 2, T)
+    halves = jnp.broadcast_to(tile, (4, 2, 4, T // 2, T)).reshape(32, T // 2, T)
+    mine = lax.all_to_all(halves, ("row", "col"), split_axis=0, concat_axis=0, tiled=True)[:16]
     mine, send = lax.optimization_barrier((mine, send))
-    lead = [mine] + [lax.ppermute(mine, "row", [(r, r ^ d) for r in range(8)]) for d in (1, 2, 3)]
+    lead = [mine] + [lax.ppermute(mine, "row", [(r, r ^ d) for r in range(8)]) for d in (1,)]
     got = lax.all_to_all(send, ("row", "col"), split_axis=0, concat_axis=0, tiled=True)
-    wt = leading_inverse((my_row % 4).reshape(1), lead)
+    wt = leading_inverse((my_row % 2).reshape(1), lead)
     base_panel = lax.optimization_barrier((front, lead[1]))[0][0, :, 0, :, 0, 0, :].reshape(tile_rows * T, T)
 
     columns, *pieces = panel(my_col.reshape(1), got, base_panel, wt[1])

time: 156 us -> 152 us (0.974)
  waiting for transfers between devices: 54.2 us -> 51 us
  starting transfers between devices: 32.7 us -> 30.4 us
    ppermute x3 -> x1, waiting for transfers between devices: 6.73 us -> 0.01 us  [local(): lax.ppermute(mine, 'row', [(r, r ^ d) for r in range(8)])]
    all_to_all x1, waiting for transfers between devices: 3.73 us -> 9.07 us  [local(): lax.all_to_all(halves, ('row', 'col'), split_axis=0, concat_axis=0, tiled...]
    ppermute x4, starting transfers between devices: 10.2 us -> 7.34 us  [local(): parts.append(lax.ppermute(pieces[m], ('row', 'col'), moves))]
    ppermute x6, starting transfers between devices: 3.66 us -> 5.95 us  [swap(): return lax.ppermute(x, 'row', [(r, r ^ bits) for r in range(8)])]
    ppermute x3 -> x1, starting transfers between devices: 2.23 us -> 0.09 us  [local(): lax.ppermute(mine, 'row', [(r, r ^ d) for r in range(8)])]
    ppermute x1, waiting for transfers between devices: 4.71 us -> 2.66 us  [local(): lax.ppermute(jnp.where(first_core, from_left, from_right), ('row', 'col')...]
    ppermute x1, waiting for transfers between devices: 1.81 us -> 0.01 us  [local(): lax.ppermute(columns, 'col', [(c, (c + 1) % 4) for c in range(4)])]
    ppermute x1, starting transfers between devices: 1.75 us -> 0.01 us  [local(): lax.ppermute(columns, 'col', [(c, (c - 1) % 4) for c in range(4)])]
  transfers between devices with their start and end apart: 19 -> 17, of which waited for: 10 -> 7; matrix products, arithmetic and copies ran while one was open for 1% -> 1% of each run, Pallas kernels for 29% -> 30%
where the time goes in v10:
time: 152 us; the launch traced here: 150 us
  Pallas kernels  65.5 us (43%)
  waiting for transfers between devices  51 us (34%)
  starting transfers between devices  30.4 us (20%)
  local copies, waits for them, and re-layouts  3.1 us (2%)
    pallas_call x1, Pallas kernels, leading_inverse(): pl.pallas_call(leading_kernel, out_shape=(jax.ShapeDtypeStruct((4, T, 4 *...  28.3 us
    all_to_all x1, waiting for transfers between devices, local(): lax.all_to_all(send, ('row', 'col'), split_axis=0, concat_axis=0, tiled=T...  23.7 us
    pallas_call x1, Pallas kernels, update(): pl.pallas_call(functools.partial(update_kernel, tile_cols, group), out_sh...  15.3 us
    pallas_call x1, Pallas kernels, rest(): pl.pallas_call(functools.partial(rest_kernel, tile_cols, group), out_shap...  9.3 us
    all_to_all x1, waiting for transfers between devices, local(): lax.all_to_all(halves, ('row', 'col'), split_axis=0, concat_axis=0, tiled...  9.07 us
    all_to_all x1, starting transfers between devices, local(): lax.all_to_all(halves, ('row', 'col'), split_axis=0, concat_axis=0, tiled...  8.42 us
    pallas_call x1, Pallas kernels, route(): pl.pallas_call(functools.partial(route_kernel, group, slot_total, tile_co...  8.04 us
    ppermute x4, starting transfers between devices, local(): parts.append(lax.ppermute(pieces[m], ('row', 'col'), moves))  7.34 us
  transfers between devices with their start and end apart: 17, of which 7 were waited for; matrix products, arithmetic and copies ran while one was open for 1% of the time, Pallas kernels for 30%

profile of v10, /device:TPU:0, one launch (start us, length us, event | category | flops | bytes accessed | tf_op | source)
XLA Modules:
  0.0 150.5 jit_solution(13963304160998061362)
XLA Ops:
  0.8 1.1 broadcast_in_dim.8
  2.0 8.4 %all-to-all-start = ((f32[32,64,128]{2,1,0:T(8,128)}), f32[32,64,128]{2,1,0:T(8,128)S(1)}, u32[]{:S(2)}, u32[]{:S(2)}) async-start(f32[32,64,128]{2,1,0:T(8,128)} %bitcast.3), calls=%async_computation | async-start | bytes 2097152 | tf_op jit(solution)/shard_map/all_to_all | solution.py:463
  10.4 8.0 %route.1 = f32[32,264,128]{2,1,0:T(8,128)} custom-call(s32[32]{0:T(128)} %bitcast.19, s32[32]{0:T(128)} %bitcast.20, f32[32,128,128]{2,1,0:T(8,128)} %bitcast.14, s32[32,128]{1,0:T(8,128)} %bitcast.17, s32[32,128]{1,0:T(8,128)} %bitcast.18), custom_call_target="tpu_custom_call" | custom-call | tf_op jit(solution)/shard_map/route/pallas_call | solution.py:96
  18.4 9.1 %all-to-all-done = f32[32,64,128]{2,1,0:T(8,128)S(1)} async-done(((f32[32,64,128]{2,1,0:T(8,128)}), f32[32,64,128]{2,1,0:T(8,128)S(1)}, u32[]{:S(2)}, u32[]{:S(2)}) %all-to-all-start) | async-done | bytes 1048608 | tf_op jit(solution)/shard_map/all_to_all | solution.py:463
  27.7 4.9 %all-to-all-start.1 = ((f32[32,264,128]{2,1,0:T(8,128)}), f32[32,264,128]{2,1,0:T(8,128)}, u32[]{:S(2)}, u32[]{:S(2)}) async-start(f32[32,264,128]{2,1,0:T(8,128)} %route.1), calls=%async_computation.1 | async-start | bytes 8650752 | tf_op jit(solution)/shard_map/all_to_all | solution.py:466
  33.7 28.3 %leading_inverse.1 = (bf16[4,128,512]{2,1,0:T(8,128)(2,1)S(1)}, bf16[4,128,512]{2,1,0:T(8,128)(2,1)S(1)}) custom-call(s32[1]{0:T(128)} %bitcast.10.core_ref, f32[16,64,128]{2,1,0:T(8,128)S(1)} %slice.12.x0, f32[16,64,128]{2,1,0:T(8,128)S(1)} %collective-permute-done.x1), custom_call_target="tpu_custom_call" | custom-call | flops 60000002048 | bytes 2000000 | tf_op jit(solution)/shard_map/leading_inverse/pallas_call | solution.py:213
  61.9 23.7 %all-to-all-done.1.got_ref.marks_ref = f32[32,264,128]{2,1,0:T(8,128)} async-done(((f32[32,264,128]{2,1,0:T(8,128)}), f32[32,264,128]{2,1,0:T(8,128)}, u32[]{:S(2)}, u32[]{:S(2)}) %all-to-all-start.1) | async-done | bytes 4325408 | tf_op jit(solution)/shard_map/all_to_all | solution.py:466
  85.7 3.5 %panel.1 = (f32[1152,128]{1,0:T(8,128)S(1)}, f32[288,128]{1,0:T(8,128)S(1)}, f32[288,128]{1,0:T(8,128)S(1)}, f32[288,128]{1,0:T(8,128)S(1)}, f32[288,128]{1,0:T(8,128)S(1)}) custom-call(s32[1]{0:T(128)} %bitcast.col_ref, f32[32,264,128]{2,1,0:T(8,128)} %all-to-all-done.1.got_ref.marks_ref, f32[1152,128]{1,0:T(8,128)S(1)} %bitcast.13, ...), custom_call_target="tpu_custom_call" | custom-call | tf_op jit(solution)/shard_map/panel/pallas_call | solution.py:281
  89.8 2.2 %collective-permute-start.2 = (f32[288,128]{1,0:T(8,128)S(1)}, f32[288,128]{1,0:T(8,128)S(1)}, u32[]{:S(2)}, u32[]{:S(2)}) collective-permute-start(f32[288,128]{1,0:T(8,128)S(1)} %get-tuple-element.29), channel_id=1, source_target_pairs={{0,4},{1,8},{2,12},{3,0},{4,5},{5,9},{6,13},{7,1},{8,6},{9,10},{10... | collective-permute-start | bytes 442376 | tf_op jit(solution)/shard_map/ppermute | solution.py:477
  92.1 3.2 %collective-permute-start.3 = (f32[288,128]{1,0:T(8,128)S(1)}, f32[288,128]{1,0:T(8,128)S(1)}, u32[]{:S(2)}, u32[]{:S(2)}) collective-permute-start(f32[288,128]{1,0:T(8,128)S(1)} %get-tuple-element.30), channel_id=1, source_target_pairs={{0,8},{1,12},{2,0},{3,4},{4,9},{5,13},{6,1},{7,5},{8,10},{9,14},{1... | collective-permute-start | bytes 442376 | tf_op jit(solution)/shard_map/ppermute | solution.py:477
  95.2 1.2 collective-permute-start.4
  96.5 1.5 %collective-permute-done.2.x1 = f32[288,128]{1,0:T(8,128)S(1)} collective-permute-done((f32[288,128]{1,0:T(8,128)S(1)}, f32[288,128]{1,0:T(8,128)S(1)}, u32[]{:S(2)}, u32[]{:S(2)}) %collective-permute-start.2) | collective-permute-done | bytes 147488 | tf_op jit(solution)/shard_map/ppermute | solution.py:477
  98.0 5.0 %collective-permute-done.3.x2 = f32[288,128]{1,0:T(8,128)S(1)} collective-permute-done((f32[288,128]{1,0:T(8,128)S(1)}, f32[288,128]{1,0:T(8,128)S(1)}, u32[]{:S(2)}, u32[]{:S(2)}) %collective-permute-start.3) | collective-permute-done | bytes 147488 | tf_op jit(solution)/shard_map/ppermute | solution.py:477
  103.0 1.2 share_solve.1.s0
  104.2 2.8 %collective-permute-start.7 = (f32[288,512]{1,0:T(8,128)S(1)}, f32[288,512]{1,0:T(8,128)S(1)}, u32[]{:S(2)}, u32[]{:S(2)}) collective-permute-start(f32[288,512]{1,0:T(8,128)S(1)} %share_solve.1.s0), channel_id=1, source_target_pairs={{0,24},{4,28},{8,16},{12,20},{16,8},{20,12},{24,0},{28,4},{1,25},{... | collective-permute-start | bytes 1769480 | tf_op jit(solution)/shard_map/ppermute | solution.py:493
  107.0 2.0 %collective-permute-start.12 = (f32[1152,128]{1,0:T(8,128)S(1)}, f32[1152,128]{1,0:T(8,128)S(1)}, u32[]{:S(2)}, u32[]{:S(2)}) collective-permute-start(f32[1152,128]{1,0:T(8,128)S(1)} %get-tuple-element.37.x0), channel_id=1, source_target_pairs={{0,1},{1,2},{2,3},{3,0},{4,5},{5,6},{6,7},{7,4},{8,9},{9,10},{10,1... | collective-permute-start | bytes 1769480 | tf_op jit(solution)/shard_map/ppermute | solution.py:481
  109.0 9.3 %rest.1.base_ref = f32[20736,128]{1,0:T(8,128)S(1)} custom-call(f32[32,264,128]{2,1,0:T(8,128)} %all-to-all-done.1.got_ref.marks_ref, f32[32,264,128]{2,1,0:T(8,128)} %all-to-all-done.1.got_ref.marks_ref, f32[20736,128]{1,0:T(8,128)} %bitcast.16), custom_call_target="tpu_custom_call" | custom-call | flops 10000000000 | bytes 26000000 | tf_op jit(solution)/shard_map/rest/pallas_call | solution.py:370
  118.3 3.0 %collective-permute-done.7.t2 = f32[288,512]{1,0:T(8,128)S(1)} collective-permute-done((f32[288,512]{1,0:T(8,128)S(1)}, f32[288,512]{1,0:T(8,128)S(1)}, u32[]{:S(2)}, u32[]{:S(2)}) %collective-permute-start.7) | collective-permute-done | bytes 589856 | tf_op jit(solution)/shard_map/ppermute | solution.py:493
  121.4 1.3 collective-permute-start.9
  122.8 1.1 collective-permute-start.5
  124.4 1.2 collective-permute-start.11
  125.6 6.0 %collective-permute-done.9.t0 = f32[288,512]{1,0:T(8,128)S(1)} collective-permute-done((f32[288,512]{1,0:T(8,128)S(1)}, f32[288,512]{1,0:T(8,128)S(1)}, u32[]{:S(2)}, u32[]{:S(2)}) %collective-permute-start.9) | collective-permute-done | bytes 589856 | tf_op jit(solution)/shard_map/ppermute | solution.py:499
  132.5 2.7 %collective-permute-done.14.x3 = f32[1152,128]{1,0:T(8,128)S(1)} collective-permute-done((f32[1152,128]{1,0:T(8,128)S(1)}, f32[1152,128]{1,0:T(8,128)S(1)}, u32[]{:S(2)}, u32[]{:S(2)}) %collective-permute-start.14) | collective-permute-done | bytes 589856 | tf_op jit(solution)/shard_map/ppermute | solution.py:483
  135.2 15.3 %update.1 = f32[20736,128]{1,0:T(8,128)} custom-call(s32[6]{0:T(128)S(1)} %pad_add_fusion.info_ref, f32[288,512]{1,0:T(8,128)S(1)} %share_solve.1.s0, f32[288,512]{1,0:T(8,128)S(1)} %collective-permute-done.5.s1, f32[288,512]{1,0:T(8,128)S(1)} %collective-permute-done.6.s2, f32[288,512]{1,0:T(8,128)S(1)} %collective-permute-done.8.s3, ...), custom_call_target="tpu_custom_call" | custom-call | tf_op jit(solution)/shard_map/update/pallas_call | solution.py:434
  (27 shorter events, 4.3 us)
Async XLA Ops:
  2.0 25.5 %all-to-all-start = ((f32[32,64,128]{2,1,0:T(8,128)}), f32[32,64,128]{2,1,0:T(8,128)S(1)}, u32[]{:S(2)}, u32[]{:S(2)}) async-start(f32[32,64,128]{2,1,0:T(8,128)} %bitcast.3), calls=%async_computation | async-start | bytes 2097152 | tf_op jit(solution)/shard_map/all_to_all | solution.py:463
  27.5 5.0 %collective-permute-start = (f32[16,64,128]{2,1,0:T(8,128)S(1)}, f32[16,64,128]{2,1,0:T(8,128)S(1)}, u32[]{:S(2)}, u32[]{:S(2)}) collective-permute-start(f32[16,64,128]{2,1,0:T(8,128)S(1)} %slice.12.x0), channel_id=1, source_target_pairs={{0,4},{4,0},{8,12},{12,8},{16,20},{20,16},{24,28},{28,24},{1,5},{5... | collective-permute-start | bytes 1572872 | tf_op jit(solution)/shard_map/ppermute | solution.py:465
  27.7 58.0 %all-to-all-start.1 = ((f32[32,264,128]{2,1,0:T(8,128)}), f32[32,264,128]{2,1,0:T(8,128)}, u32[]{:S(2)}, u32[]{:S(2)}) async-start(f32[32,264,128]{2,1,0:T(8,128)} %route.1), calls=%async_computation.1 | async-start | bytes 8650752 | tf_op jit(solution)/shard_map/all_to_all | solution.py:466
  89.1 7.4 %collective-permute-start.1 = (f32[288,128]{1,0:T(8,128)S(1)}, f32[288,128]{1,0:T(8,128)S(1)}, u32[]{:S(2)}, u32[]{:S(2)}) collective-permute-start(f32[288,128]{1,0:T(8,128)S(1)} %get-tuple-element.27), channel_id=1, source_target_pairs={{0,0},{1,4},{2,8},{3,12},{4,1},{5,5},{6,9},{7,13},{8,2},{9,6},{10,... | collective-permute-start | bytes 442376 | tf_op jit(solution)/shard_map/ppermute | solution.py:477
  89.8 8.2 %collective-permute-start.2 = (f32[288,128]{1,0:T(8,128)S(1)}, f32[288,128]{1,0:T(8,128)S(1)}, u32[]{:S(2)}, u32[]{:S(2)}) collective-permute-start(f32[288,128]{1,0:T(8,128)S(1)} %get-tuple-element.29), channel_id=1, source_target_pairs={{0,4},{1,8},{2,12},{3,0},{4,5},{5,9},{6,13},{7,1},{8,6},{9,10},{10... | collective-permute-start | bytes 442376 | tf_op jit(solution)/shard_map/ppermute | solution.py:477
  92.1 11.0 %collective-permute-start.3 = (f32[288,128]{1,0:T(8,128)S(1)}, f32[288,128]{1,0:T(8,128)S(1)}, u32[]{:S(2)}, u32[]{:S(2)}) collective-permute-start(f32[288,128]{1,0:T(8,128)S(1)} %get-tuple-element.30), channel_id=1, source_target_pairs={{0,8},{1,12},{2,0},{3,4},{4,9},{5,13},{6,1},{7,5},{8,10},{9,14},{1... | collective-permute-start | bytes 442376 | tf_op jit(solution)/shard_map/ppermute | solution.py:477
  95.2 7.8 %collective-permute-start.4 = (f32[288,128]{1,0:T(8,128)S(1)}, f32[288,128]{1,0:T(8,128)S(1)}, u32[]{:S(2)}, u32[]{:S(2)}) collective-permute-start(f32[288,128]{1,0:T(8,128)S(1)} %get-tuple-element.31), channel_id=1, source_target_pairs={{0,12},{1,0},{2,4},{3,8},{4,13},{5,1},{6,5},{7,9},{8,14},{9,2},{10... | collective-permute-start | bytes 442376 | tf_op jit(solution)/shard_map/ppermute | solution.py:477
  104.2 17.1 %collective-permute-start.7 = (f32[288,512]{1,0:T(8,128)S(1)}, f32[288,512]{1,0:T(8,128)S(1)}, u32[]{:S(2)}, u32[]{:S(2)}) collective-permute-start(f32[288,512]{1,0:T(8,128)S(1)} %share_solve.1.s0), channel_id=1, source_target_pairs={{0,24},{4,28},{8,16},{12,20},{16,8},{20,12},{24,0},{28,4},{1,25},{... | collective-permute-start | bytes 1769480 | tf_op jit(solution)/shard_map/ppermute | solution.py:493
  107.0 14.4 %collective-permute-start.6 = (f32[288,512]{1,0:T(8,128)S(1)}, f32[288,512]{1,0:T(8,128)S(1)}, u32[]{:S(2)}, u32[]{:S(2)}) collective-permute-start(f32[288,512]{1,0:T(8,128)S(1)} %share_solve.1.s0), channel_id=1, source_target_pairs={{0,8},{4,12},{8,0},{12,4},{16,24},{20,28},{24,16},{28,20},{1,9},{5... | collective-permute-start | bytes 1769480 | tf_op jit(solution)/shard_map/ppermute | solution.py:493
  107.0 16.9 %collective-permute-start.13 = (f32[1152,128]{1,0:T(8,128)S(1)}, f32[1152,128]{1,0:T(8,128)S(1)}, u32[]{:S(2)}, u32[]{:S(2)}) collective-permute-start(f32[1152,128]{1,0:T(8,128)S(1)} %get-tuple-element.37.x0), channel_id=1, source_target_pairs={{0,3},{1,0},{2,1},{3,2},{4,7},{5,4},{6,5},{7,6},{8,11},{9,8},{10,9... | collective-permute-start | bytes 1769480 | tf_op jit(solution)/shard_map/ppermute | solution.py:482
  107.0 16.9 %collective-permute-start.12 = (f32[1152,128]{1,0:T(8,128)S(1)}, f32[1152,128]{1,0:T(8,128)S(1)}, u32[]{:S(2)}, u32[]{:S(2)}) collective-permute-start(f32[1152,128]{1,0:T(8,128)S(1)} %get-tuple-element.37.x0), channel_id=1, source_target_pairs={{0,1},{1,2},{2,3},{3,0},{4,5},{5,6},{6,7},{7,4},{8,9},{9,10},{10,1... | collective-permute-start | bytes 1769480 | tf_op jit(solution)/shard_map/ppermute | solution.py:481
  109.0 23.4 %copy-start = (s32[4]{0:T(128)S(1)}, s32[4]{0:T(128)}, u32[]{:S(2)}) copy-start(s32[4]{0:T(128)} %constant.46.clone) | copy-start | bytes 52
  121.4 10.1 %collective-permute-start.9 = (f32[288,512]{1,0:T(8,128)S(1)}, f32[288,512]{1,0:T(8,128)S(1)}, u32[]{:S(2)}, u32[]{:S(2)}) collective-permute-start(f32[288,512]{1,0:T(8,128)S(1)} %broadcast_select_fusion.1), channel_id=1, source_target_pairs={{0,8},{4,28},{8,0},{12,20},{16,24},{20,12},{24,16},{28,4},{1,9},{5... | collective-permute-start | bytes 1769480 | tf_op jit(solution)/shard_map/ppermute | solution.py:499
  122.8 9.7 %collective-permute-start.5 = (f32[288,512]{1,0:T(8,128)S(1)}, f32[288,512]{1,0:T(8,128)S(1)}, u32[]{:S(2)}, u32[]{:S(2)}) collective-permute-start(f32[288,512]{1,0:T(8,128)S(1)} %share_solve.1.s0), channel_id=1, source_target_pairs={{0,4},{4,0},{8,12},{12,8},{16,20},{20,16},{24,28},{28,24},{1,5},{5... | collective-permute-start | bytes 1769480 | tf_op jit(solution)/shard_map/ppermute | solution.py:493
  123.9 11.3 %collective-permute-start.8 = (f32[288,512]{1,0:T(8,128)S(1)}, f32[288,512]{1,0:T(8,128)S(1)}, u32[]{:S(2)}, u32[]{:S(2)}) collective-permute-start(f32[288,512]{1,0:T(8,128)S(1)} %collective-permute-done.6.s2), channel_id=1, source_target_pairs={{0,4},{4,0},{8,12},{12,8},{16,20},{20,16},{24,28},{28,24},{1,5},{5... | collective-permute-start | bytes 1769480 | tf_op jit(solution)/shard_map/ppermute | solution.py:493
  124.0 11.2 %collective-permute-start.14 = (f32[1152,128]{1,0:T(8,128)S(1)}, f32[1152,128]{1,0:T(8,128)S(1)}, u32[]{:S(2)}, u32[]{:S(2)}) collective-permute-start(f32[1152,128]{1,0:T(8,128)S(1)} %broadcast_select_fusion), channel_id=1, source_target_pairs={{0,1},{1,2},{2,3},{3,0},{4,7},{5,4},{6,5},{7,6},{8,9},{9,10},{10,1... | collective-permute-start | bytes 1769480 | tf_op jit(solution)/shard_map/ppermute | solution.py:483
  124.4 10.7 %collective-permute-start.11 = (f32[288,512]{1,0:T(8,128)S(1)}, f32[288,512]{1,0:T(8,128)S(1)}, u32[]{:S(2)}, u32[]{:S(2)}) collective-permute-start(f32[288,512]{1,0:T(8,128)S(1)} %collective-permute-done.7.t2), channel_id=1, source_target_pairs={{0,4},{4,0},{8,12},{12,8},{16,20},{20,16},{24,28},{28,24},{1,5},{5... | collective-permute-start | bytes 1769480 | tf_op jit(solution)/shard_map/ppermute | solution.py:493
  131.6 3.6 %collective-permute-start.10 = (f32[288,512]{1,0:T(8,128)S(1)}, f32[288,512]{1,0:T(8,128)S(1)}, u32[]{:S(2)}, u32[]{:S(2)}) collective-permute-start(f32[288,512]{1,0:T(8,128)S(1)} %collective-permute-done.9.t0), channel_id=1, source_target_pairs={{0,4},{4,0},{8,12},{12,8},{16,20},{20,16},{24,28},{28,24},{1,5},{5... | collective-permute-start | bytes 1769480 | tf_op jit(solution)/shard_map/ppermute | solution.py:493
